TPU v7x, 32 devices: a whole 2x2x4 slice. The times are simulated.
32 devices in a mesh: dp: 4 (over y, core), dom: 8 (over z, x).
Axes of the slice: x: 2, y: 2, z: 4, core: 2. Of those that a mesh axis runs over, the one named last changes fastest.
Arguments:
- features: bfloat16 [32768, 1024], P(('dp', 'dom')), may hold values from -6 to 6
- w_first: bfloat16 [1024, 1024], replicated, may hold values from -0.1875 to 0.1875
- b_first: bfloat16 [1024], replicated, may hold values from -3 to 3
- w_second: bfloat16 [1024, 256], replicated, may hold values from -0.1875 to 0.1875
- b_second: bfloat16 [256], replicated, may hold values from -3 to 3
- dest_part: int32 [32768], P(('dp', 'dom')), may hold values from 0 to 31, as said below
- dest_slot: int32 [32768], P(('dp', 'dom')), may hold values from 0 to 3071, as said below
- tile_coords: int32 [1536, 2], P(('dp', 'dom')), may hold values from 0 to 39, as said below
- tile_values: bfloat16 [1536, 128, 128], P(('dp', 'dom')), may hold values from -0.25 to 0.25
- halo_send: int32 [32, 2, 8], P(('dp', 'dom')), may hold values from 0 to 23, as said below
Outputs:
- smoothed: bfloat16 [98304, 256], P(('dp', 'dom'))
Inputs may be any that keep to these rules, and one draw needn't show every extreme that they name: `dest_part`: every part holds at most 3072 rows and one part exactly 3072; the rows of one part are dealt over the devices so that the counts that two devices send it differ by at most one, so at most 96 rows go from one device to one part and every device sends exactly 96 to the fullest part. `dest_slot`: within a part, its rows take the slots 0 to its size minus one, each once. `tile_coords`: 48 tiles a part, parts in order. Column 0 is a block of the part; column 1 indexes its extended blocks. The part's first 24 tiles are (b, b) for each block b, the next 16 have sources 24 to 39 in order. `halo_send`: listed blocks hold rows of the part and may repeat.
All inputs are finite; a program needn't handle non-finite values.
Results may differ from a plain program's by a relative error of at most 0.0062.
Values may be sent and summed in bfloat16 or wider, within the bound.
No kernel may reach another device: no remote copies, remote signals or barrier semaphores. Data moves between devices by JAX's collectives and lax.ppermute only.
A program may use at most 64 MiB of HBM per device.

v0:
```python
import functools

import jax
import jax.numpy as jnp
from jax import lax
from jax.experimental import pallas as pl
from jax.experimental.pallas import tpu as pltpu
from jax.sharding import PartitionSpec as P

HOPS = 2
ALPHA = 0.1
LANES = 128
PACK = 16
GROUP = LANES // PACK
VMEM_LIMIT = 48 * 1024 * 1024

BF16 = jnp.bfloat16
F32 = jnp.float32


def iota(shape, dim):
    return lax.broadcasted_iota(jnp.int32, shape, dim)


def gelu(value):
    return 0.5 * value * (1.0 + lax.erf(value * (0.5**0.5)))


def project_kernel(
    parts,
    slots,
    features,
    w_first,
    b_first,
    w_second,
    b_second,
    dest_part,
    dest_slot,
    lane_base,
    out,
    embedded,
):
    step = pl.program_id(0)
    block = features.shape[0]
    width = w_second.shape[1]
    total = None
    chunk = 256
    for first in range(0, w_first.shape[1], chunk):
        columns = slice(first, first + chunk)
        hidden = jnp.dot(features[...], w_first[:, columns], preferred_element_type=F32)
        hidden = gelu(hidden + b_first[:, columns].astype(F32)).astype(BF16)
        term = jnp.dot(hidden, w_second[columns, :], preferred_element_type=F32)
        total = term if total is None else total + term
    rows = pl.ds(pl.multiple_of(step * block, block), block)
    embedded[rows, :] = (total + b_second[...].astype(F32)).astype(BF16)

    @pl.when(step == pl.num_programs(0) - 1)
    def _():
        count = dest_part.shape[1]
        part = dest_part[...]
        onehot = (iota((parts, count), 0) == part).astype(F32)
        blocks = [onehot[:, at : at + LANES] for at in range(0, count, LANES)]
        earlier = (iota((LANES, LANES), 0) < iota((LANES, LANES), 1)).astype(BF16)
        within = jnp.dot(
            jnp.concatenate(blocks, axis=0).astype(BF16), earlier, preferred_element_type=F32
        )
        offset = jnp.zeros((parts, 1), F32)
        pieces = []
        for index, piece in enumerate(blocks):
            before = within[index * parts : (index + 1) * parts, :] + offset
            pieces.append(jnp.sum(before * piece, axis=0, keepdims=True))
            offset = offset + jnp.sum(piece, axis=1, keepdims=True)
        position = jnp.concatenate(pieces, axis=1).astype(jnp.int32)
        target = part * slots + position

        coded = dest_slot[...] + 1
        high = jnp.right_shift(coded, 6)
        low = coded - high * 64
        place = (iota((LANES, count), 0) == position).astype(BF16)
        digits = []
        for digit in (high, low):
            marked = (onehot * digit.astype(F32)).astype(BF16)
            digits.append(
                lax.dot_general(
                    marked, place, (((1,), (1,)), ((), ())), preferred_element_type=F32
                )
            )
        base = lane_base[0]
        lane = iota((parts, LANES), 1)
        mine = (lane >= base) & (lane < base + PACK)
        row = iota((parts, PACK, LANES), 1)
        listed = jnp.zeros((parts, PACK, LANES), F32)
        for at, digit in zip((0, 8), digits):
            for j in range(slots // PACK):
                turned = pltpu.roll(digit, lax.rem(base - j * PACK + LANES, LANES), 1)
                turned = jnp.where(mine, turned, 0.0)
                listed = jnp.where(row == at + j, turned[:, None, :], listed)
        halves = width // LANES
        out[:, halves * slots :, :] = listed.astype(BF16)

        size = GROUP * slots
        slot = iota((size, count), 0)
        for group in range(parts // GROUP):
            select = (slot == target - group * size).astype(BF16)
            moved = jnp.dot(select, embedded[...], preferred_element_type=F32).astype(BF16)
            for half in range(halves):
                piece = moved[:, half * LANES : (half + 1) * LANES]
                out[group * GROUP : (group + 1) * GROUP, half * slots : (half + 1) * slots, :] = (
                    piece.reshape(GROUP, slots, LANES)
                )


def project(parts, slots, features, w_first, b_first, w_second, b_second, part, slot, lane_base):
    rows, depth = features.shape
    hidden, width = w_second.shape
    block = rows // 4
    length = (width // LANES) * slots + PACK
    whole = lambda shape: pl.BlockSpec(shape, lambda i: (0,) * len(shape))
    return pl.pallas_call(
        functools.partial(project_kernel, parts, slots),
        out_shape=jax.ShapeDtypeStruct((parts, length, LANES), BF16),
        grid=(rows // block,),
        in_specs=[
            pl.BlockSpec((block, depth), lambda i: (i, 0)),
            whole((depth, hidden)),
            whole((1, hidden)),
            whole((hidden, width)),
            whole((1, width)),
            whole((1, rows)),
            whole((1, rows)),
            pl.BlockSpec(memory_space=pltpu.SMEM),
        ],
        out_specs=whole((parts, length, LANES)),
        scratch_shapes=[pltpu.VMEM((rows, width), BF16)],
        compiler_params=pltpu.CompilerParams(vmem_limit_bytes=VMEM_LIMIT),
        cost_estimate=pl.CostEstimate(
            flops=2 * rows * hidden * (depth + width), bytes_accessed=8 << 20, transcendentals=0
        ),
        name="project",
    )(
        features,
        w_first,
        b_first.reshape(1, hidden),
        w_second,
        b_second.reshape(1, width),
        part.reshape(1, rows),
        slot.reshape(1, rows),
        lane_base,
    )


def send_blocks(field, halo_send, send):
    for side in range(send.shape[0]):
        for k in range(send.shape[1]):
            send[side, k] = field[halo_send[side, k]]


def place_kernel(slots, half, halves, arrived, halo_send, start, send, size):
    groups = arrived.shape[0] // GROUP
    chunks = slots // PACK
    ids, rows = [], []
    filled = jnp.zeros((1, LANES), F32)
    for group in range(groups):
        sources = slice(group * GROUP, (group + 1) * GROUP)
        listed = jnp.sum(arrived[sources, halves * slots :, :].astype(F32), axis=0)
        coded = listed[:8] * 64.0 + listed[8:]
        for j in range(chunks):
            code = coded[j : j + 1, :]
            ids.append(code.astype(jnp.int32) - 1)
            filled = filled + (code > 0.0).astype(F32)
            first = half * slots + j * PACK
            rows.append(arrived[sources, first : first + PACK, :].reshape(LANES, LANES))
    ids = jnp.concatenate(ids, axis=1)
    rows = jnp.concatenate(rows, axis=0)
    size[0] = jnp.sum(filled).astype(jnp.int32)
    block_count, block_rows, _ = start.shape
    several = 4
    slot = iota((several * block_rows, ids.shape[1]), 0)
    for first in range(0, block_count, several):
        select = (slot == ids - first * block_rows).astype(BF16)
        placed = jnp.dot(select, rows, preferred_element_type=F32).astype(BF16)
        start[first : first + several] = placed.reshape(several, block_rows, LANES)
    send_blocks(start, halo_send, send)


def place(slots, half, halves, blocks, arrived, halo_send):
    block_count, block_rows = blocks
    vmem = pl.BlockSpec(memory_space=pltpu.VMEM)
    smem = pl.BlockSpec(memory_space=pltpu.SMEM)
    listed = halo_send.shape[1]
    return pl.pallas_call(
        functools.partial(place_kernel, slots, half, halves),
        out_shape=[
            jax.ShapeDtypeStruct((block_count, block_rows, LANES), BF16),
            jax.ShapeDtypeStruct((2, listed, block_rows, LANES), BF16),
            jax.ShapeDtypeStruct((1,), jnp.int32),
        ],
        in_specs=[vmem, smem],
        out_specs=[vmem, vmem, smem],
        compiler_params=pltpu.CompilerParams(vmem_limit_bytes=VMEM_LIMIT),
        cost_estimate=pl.CostEstimate(
            flops=2 * (block_count * block_rows) ** 2 * LANES, bytes_accessed=3 << 20, transcendentals=0
        ),
        name="place",
    )(arrived, halo_send)


def hop_kernel(last, *refs):
    tiles, coords, halo_send, size, start, current, low, high = refs[:8]
    if last:
        out, summed = refs[-2:]
        send = None
    else:
        out, send, summed = refs[-3:]
    block_count, block_rows, width = start.shape
    listed = low.shape[0]
    for b in range(block_count):
        summed[b] = jnp.dot(tiles[b], current[b], preferred_element_type=F32)
    first = block_count + 2 * listed
    for t in range(block_count, tiles.shape[0]):
        if t < block_count + listed:
            source = low[t - block_count]
        elif t < first:
            source = high[t - block_count - listed]
        else:
            index = coords[2 * t + 1]
            source = current[jnp.minimum(index, block_count - 1)]
            below = low[jnp.clip(index - block_count, 0, listed - 1)]
            above = high[jnp.clip(index - block_count - listed, 0, listed - 1)]
            source = jnp.where(index < block_count, source, below)
            source = jnp.where(index < block_count + listed, source, above)
        target = coords[2 * t]
        summed[target] += jnp.dot(tiles[t], source, preferred_element_type=F32)
    row = iota((block_rows, width), 0)
    for b in range(block_count):
        mixed = (1.0 - ALPHA) * summed[b] + ALPHA * start[b].astype(F32)
        mixed = jnp.where(row < size[0] - b * block_rows, mixed, 0.0).astype(BF16)
        if last:
            out[b * block_rows : (b + 1) * block_rows, :] = mixed
        else:
            out[b] = mixed
    if send is not None:
        send_blocks(out, halo_send, send)


def hop(tiles, coords, halo_send, size, start, current, low, high, half=None, halves=1, held=None):
    block_count, block_rows, width = start.shape
    listed = low.shape[0]
    last = half is not None
    vmem = pl.BlockSpec(memory_space=pltpu.VMEM)
    smem = pl.BlockSpec(memory_space=pltpu.SMEM)
    operands = [tiles, coords, halo_send, size, start, current, low, high]
    in_specs = [vmem, smem, smem, smem, vmem, vmem, vmem, vmem]
    aliases = {}
    if last:
        capacity = block_count * block_rows
        out_shape = jax.ShapeDtypeStruct((capacity, width * halves), BF16)
        out_specs = pl.BlockSpec((capacity, width), lambda i: (0, half))
        if held is not None:
            aliases = {len(operands): 0}
            operands.append(held)
            in_specs.append(pl.BlockSpec(memory_space=pl.ANY))
        in_specs = [
            spec if spec is not vmem else pl.BlockSpec(x.shape, lambda i, n=x.ndim: (0,) * n)
            for spec, x in zip(in_specs, operands)
        ]
        grid = (1,)
    else:
        out_shape = [
            jax.ShapeDtypeStruct((block_count, block_rows, width), BF16),
            jax.ShapeDtypeStruct((2, listed, block_rows, width), BF16),
        ]
        out_specs = [vmem, vmem]
        grid = ()
    return pl.pallas_call(
        functools.partial(hop_kernel, last),
        out_shape=out_shape,
        grid=grid,
        in_specs=in_specs,
        out_specs=out_specs,
        scratch_shapes=[pltpu.VMEM((block_count, block_rows, width), F32)],
        input_output_aliases=aliases,
        compiler_params=pltpu.CompilerParams(vmem_limit_bytes=VMEM_LIMIT),
        cost_estimate=pl.CostEstimate(
            flops=2 * tiles.size * width, bytes_accessed=5 << 20, transcendentals=0
        ),
        name="hop",
    )(*operands)


def local(
    features,
    w_first,
    b_first,
    w_second,
    b_second,
    dest_part,
    dest_slot,
    tile_coords,
    tile_values,
    halo_send,
):
    count_dp = lax.axis_size("dp")
    count_dom = lax.axis_size("dom")
    parts = count_dp * count_dom
    row_count = features.shape[0]
    capacity = 3 * row_count
    slots = -(-capacity // parts // PACK) * PACK
    width = w_second.shape[1]
    halves = width // LANES
    block_rows = tile_values.shape[1]
    block_count = capacity // block_rows
    me = lax.axis_index("dp") * count_dom + lax.axis_index("dom")
    lane_base = (lax.rem(me, GROUP) * PACK).astype(jnp.int32).reshape(1)
    outgoing = project(
        parts, slots, features, w_first, b_first, w_second, b_second, dest_part, dest_slot, lane_base
    )
    arrived = lax.all_to_all(outgoing, ("dp", "dom"), split_axis=0, concat_axis=0, tiled=True)
    coords = tile_coords.reshape(-1)
    lists = halo_send[0]
    forward = [(i, (i + 1) % count_dom) for i in range(count_dom)]
    backward = [((i + 1) % count_dom, i) for i in range(count_dom)]

    def exchange(send):
        return lax.ppermute(send[0], "dom", forward), lax.ppermute(send[1], "dom", backward)

    starts, fields, halos = [], [], []
    size = None
    for half in range(halves):
        start, send, size = place(slots, half, halves, (block_count, block_rows), arrived, lists)
        starts.append(start)
        fields.append(start)
        halos.append(exchange(send))
    for repeat in range(HOPS - 1):
        for half in range(halves):
            fields[half], send = hop(
                tile_values, coords, lists, size, starts[half], fields[half], *halos[half]
            )
            halos[half] = exchange(send)
    held = None
    for half in range(halves):
        held = hop(
            tile_values, coords, lists, size, starts[half], fields[half], *halos[half],
            half=half, halves=halves, held=held,
        )
    return held


def solution(mesh):
    placed = (
        P(("dp", "dom"), None),
        P(),
        P(),
        P(),
        P(),
        P(("dp", "dom")),
        P(("dp", "dom")),
        P(("dp", "dom"), None),
        P(("dp", "dom"), None, None),
        P(("dp", "dom"), None, None),
    )
    return jax.shard_map(
        local, mesh=mesh, in_specs=placed, out_specs=P(("dp", "dom"), None), check_vma=False
    )
```

profile of v0, /device:TPU:0, one launch (start us, length us, event | category | flops | bytes accessed | tf_op | source)
XLA Modules:
  0.0 122.3 jit_solution(10801743087680725393)
XLA Ops:
  0.0 0.7 reshape.19.b_first
  0.7 0.7 reshape.20.b_second
  1.3 0.0 copy-start.2
  1.3 1.6 %copy-done.2 = bf16[1024,1024]{1,0:T(8,128)(2,1)S(1)} copy-done((bf16[1024,1024]{1,0:T(8,128)(2,1)S(1)}, bf16[1024,1024]{1,0:T(8,128)(2,1)}, u32[]{:S(2)}) %copy-start.2) | copy-done | bytes 2097176
  2.9 0.0 copy-start.3
  2.9 1.0 copy-done.3
  4.0 0.0 copy-start.4
  4.0 0.7 copy-done.4
  4.7 0.0 copy-start.5
  4.7 0.7 copy-done.5
  5.4 10.7 %project.1 = bf16[32,208,128]{2,1,0:T(8,128)(2,1)} custom-call(bf16[1024,1024]{1,0:T(8,128)(2,1)S(1)} %copy-done.2, bf16[1024,1024]{1,0:T(8,128)(2,1)} %w_first.1, bf16[1,1024]{1,0:T(2,128)(2,1)S(1)} %reshape.19.b_first, bf16[1024,256]{1,0:T(8,128)(2,1)S(1)} %copy-done.3, bf16[1,256]{1,0:T(2,128)(2,1)S(1)} %reshape.20.b_second, s32[1,1024]{1,0:T(1,128)S(1)} %bitcast.26, ...), custom_call_target="tpu_custom_call" | custom-call | flops 2684354560 | bytes 8388608 | tf_op jit(solution)/shard_map/project/pallas_call | solution.py:119
  16.0 0.0 copy-start.6
  16.0 0.0 copy-start.1
  16.0 7.3 %all-to-all-start = ((bf16[32,208,128]{2,1,0:T(8,128)(2,1)}), bf16[32,208,128]{2,1,0:T(8,128)(2,1)S(1)}, u32[]{:S(2)}, u32[]{:S(2)}) async-start(bf16[32,208,128]{2,1,0:T(8,128)(2,1)} %project.1), calls=%async_computation | async-start | bytes 3407872 | tf_op jit(solution)/shard_map/all_to_all | solution.py:318
  23.3 0.0 copy-done.6
  23.4 0.1 copy.13
  23.4 0.1 reshape.18.refs_1_
  23.6 41.4 %all-to-all-done.arrived = bf16[32,208,128]{2,1,0:T(8,128)(2,1)S(1)} async-done(((bf16[32,208,128]{2,1,0:T(8,128)(2,1)}), bf16[32,208,128]{2,1,0:T(8,128)(2,1)S(1)}, u32[]{:S(2)}, u32[]{:S(2)}) %all-to-all-start) | async-done | bytes 1703968 | tf_op jit(solution)/shard_map/all_to_all | solution.py:318
  65.0 0.0 copy-done.1
  65.0 6.0 %place.3 = (bf16[24,128,128]{2,1,0:T(8,128)(2,1)S(1)}, bf16[2,8,128,128]{3,2,1,0:T(8,128)(2,1)S(1)}, s32[1]{0:T(128)}) custom-call(bf16[32,208,128]{2,1,0:T(8,128)(2,1)S(1)} %all-to-all-done.arrived, s32[2,8]{1,0:T(2,128)S(1)} %bitcast.20), custom_call_target="tpu_custom_call" | custom-call | flops 2415919104 | bytes 3145728 | tf_op jit(solution)/shard_map/place/pallas_call | solution.py:191
  71.1 0.4 collective-permute-start.4
  71.5 4.4 %collective-permute-start.5 = (bf16[8,128,128]{2,1,0:T(8,128)(2,1)S(1)}, bf16[8,128,128]{2,1,0:T(8,128)(2,1)S(1)}, u32[]{:S(2)}, u32[]{:S(2)}) collective-permute-start(bf16[8,128,128]{2,1,0:T(8,128)(2,1)S(1)} %get-tuple-element.25), channel_id=1, source_target_pairs={{1,0},{2,1},{3,2},{4,3},{5,4},{6,5},{7,6},{0,7},{9,8},{10,9},{11,1... | collective-permute-start | bytes 786440 | tf_op jit(solution)/shard_map/ppermute | solution.py:325
  75.8 0.0 copy-start
  75.8 6.0 %place.2 = (bf16[24,128,128]{2,1,0:T(8,128)(2,1)S(1)}, bf16[2,8,128,128]{3,2,1,0:T(8,128)(2,1)S(1)}, s32[1]{0:T(128)}) custom-call(bf16[32,208,128]{2,1,0:T(8,128)(2,1)S(1)} %all-to-all-done.arrived, s32[2,8]{1,0:T(2,128)S(1)} %bitcast.21), custom_call_target="tpu_custom_call" | custom-call | flops 2415919104 | bytes 3145728 | tf_op jit(solution)/shard_map/place/pallas_call | solution.py:191
  81.9 0.1 collective-permute-start
  82.0 4.7 %collective-permute-start.1 = (bf16[8,128,128]{2,1,0:T(8,128)(2,1)S(1)}, bf16[8,128,128]{2,1,0:T(8,128)(2,1)S(1)}, u32[]{:S(2)}, u32[]{:S(2)}) collective-permute-start(bf16[8,128,128]{2,1,0:T(8,128)(2,1)S(1)} %get-tuple-element.29), channel_id=1, source_target_pairs={{1,0},{2,1},{3,2},{4,3},{5,4},{6,5},{7,6},{0,7},{9,8},{10,9},{11,1... | collective-permute-start | bytes 786440 | tf_op jit(solution)/shard_map/ppermute | solution.py:325
  86.7 2.6 %collective-permute-done.4.refs_6_ = bf16[8,128,128]{2,1,0:T(8,128)(2,1)S(1)} collective-permute-done((bf16[8,128,128]{2,1,0:T(8,128)(2,1)S(1)}, bf16[8,128,128]{2,1,0:T(8,128)(2,1)S(1)}, u32[]{:S(2)}, u32[]{:S(2)}) %collective-permute-start.4) | collective-permute-done | bytes 262176 | tf_op jit(solution)/shard_map/ppermute | solution.py:325
  89.3 0.0 collective-permute-done.5.refs_7_
  89.3 0.0 copy-done
  89.3 2.2 %hop.5 = (bf16[24,128,128]{2,1,0:T(8,128)(2,1)S(1)}, bf16[2,8,128,128]{3,2,1,0:T(8,128)(2,1)S(1)}) custom-call(bf16[48,128,128]{2,1,0:T(8,128)(2,1)S(1)} %copy-done, s32[96]{0:T(128)S(1)} %reshape.18.refs_1_, s32[2,8]{1,0:T(2,128)S(1)} %bitcast.22, s32[1]{0:T(128)} %get-tuple-element.14.refs_3_, bf16[24,128,128]{2,1,0:T(8,128)(2,1)S(1)} %get-tuple-element.19.refs_4_.refs_5_, ...), custom_call_target="tpu_custom_call" | custom-call | flops 201326592 | bytes 5242880 | tf_op jit(solution)/shard_map/hop/pallas_call | solution.py:275
  91.6 2.5 %collective-permute-start.6 = (bf16[8,128,128]{2,1,0:T(8,128)(2,1)S(1)}, bf16[8,128,128]{2,1,0:T(8,128)(2,1)S(1)}, u32[]{:S(2)}, u32[]{:S(2)}) collective-permute-start(bf16[8,128,128]{2,1,0:T(8,128)(2,1)S(1)} %get-tuple-element.24), channel_id=1, source_target_pairs={{0,1},{1,2},{2,3},{3,4},{4,5},{5,6},{6,7},{7,0},{8,9},{9,10},{10,1... | collective-permute-start | bytes 786440 | tf_op jit(solution)/shard_map/ppermute | solution.py:325
  94.2 2.2 %collective-permute-start.7 = (bf16[8,128,128]{2,1,0:T(8,128)(2,1)S(1)}, bf16[8,128,128]{2,1,0:T(8,128)(2,1)S(1)}, u32[]{:S(2)}, u32[]{:S(2)}) collective-permute-start(bf16[8,128,128]{2,1,0:T(8,128)(2,1)S(1)} %get-tuple-element.23), channel_id=1, source_target_pairs={{1,0},{2,1},{3,2},{4,3},{5,4},{6,5},{7,6},{0,7},{9,8},{10,9},{11,1... | collective-permute-start | bytes 786440 | tf_op jit(solution)/shard_map/ppermute | solution.py:325
  96.4 0.0 collective-permute-done.refs_6_
  96.4 6.7 %collective-permute-done.1.refs_7_ = bf16[8,128,128]{2,1,0:T(8,128)(2,1)S(1)} collective-permute-done((bf16[8,128,128]{2,1,0:T(8,128)(2,1)S(1)}, bf16[8,128,128]{2,1,0:T(8,128)(2,1)S(1)}, u32[]{:S(2)}, u32[]{:S(2)}) %collective-permute-start.1) | collective-permute-done | bytes 262176 | tf_op jit(solution)/shard_map/ppermute | solution.py:325
  103.1 2.2 %hop.4 = (bf16[24,128,128]{2,1,0:T(8,128)(2,1)S(1)}, bf16[2,8,128,128]{3,2,1,0:T(8,128)(2,1)S(1)}) custom-call(bf16[48,128,128]{2,1,0:T(8,128)(2,1)S(1)} %copy-done, s32[96]{0:T(128)S(1)} %reshape.18.refs_1_, s32[2,8]{1,0:T(2,128)S(1)} %bitcast.23, s32[1]{0:T(128)} %get-tuple-element.14.refs_3_, bf16[24,128,128]{2,1,0:T(8,128)(2,1)S(1)} %get-tuple-element.15.refs_4_.refs_5_, ...), custom_call_target="tpu_custom_call" | custom-call | flops 201326592 | bytes 5242880 | tf_op jit(solution)/shard_map/hop/pallas_call | solution.py:275
  105.4 0.1 collective-permute-start.2
  105.4 4.7 %collective-permute-start.3 = (bf16[8,128,128]{2,1,0:T(8,128)(2,1)S(1)}, bf16[8,128,128]{2,1,0:T(8,128)(2,1)S(1)}, u32[]{:S(2)}, u32[]{:S(2)}) collective-permute-start(bf16[8,128,128]{2,1,0:T(8,128)(2,1)S(1)} %get-tuple-element.27), channel_id=1, source_target_pairs={{1,0},{2,1},{3,2},{4,3},{5,4},{6,5},{7,6},{0,7},{9,8},{10,9},{11,1... | collective-permute-start | bytes 786440 | tf_op jit(solution)/shard_map/ppermute | solution.py:325
  110.1 2.0 %collective-permute-done.6.refs_6_ = bf16[8,128,128]{2,1,0:T(8,128)(2,1)S(1)} collective-permute-done((bf16[8,128,128]{2,1,0:T(8,128)(2,1)S(1)}, bf16[8,128,128]{2,1,0:T(8,128)(2,1)S(1)}, u32[]{:S(2)}, u32[]{:S(2)}) %collective-permute-start.6) | collective-permute-done | bytes 262176 | tf_op jit(solution)/shard_map/ppermute | solution.py:325
  112.2 0.0 collective-permute-done.7.refs_7_
  112.2 3.1 %hop.6.refs_8_ = bf16[3072,256]{1,0:T(8,128)(2,1)} custom-call(bf16[48,128,128]{2,1,0:T(8,128)(2,1)S(1)} %copy-done, s32[96]{0:T(128)S(1)} %reshape.18.refs_1_, s32[2,8]{1,0:T(2,128)S(1)} %bitcast.24, s32[1]{0:T(128)} %get-tuple-element.14.refs_3_, bf16[24,128,128]{2,1,0:T(8,128)(2,1)S(1)} %get-tuple-element.19.refs_4_.refs_5_, ...), custom_call_target="tpu_custom_call" | custom-call | flops 201326592 | bytes 5242880 | tf_op jit(solution)/shard_map/hop/pallas_call | solution.py:275
  115.3 1.8 %collective-permute-done.2.refs_6_ = bf16[8,128,128]{2,1,0:T(8,128)(2,1)S(1)} collective-permute-done((bf16[8,128,128]{2,1,0:T(8,128)(2,1)S(1)}, bf16[8,128,128]{2,1,0:T(8,128)(2,1)S(1)}, u32[]{:S(2)}, u32[]{:S(2)}) %collective-permute-start.2) | collective-permute-done | bytes 262176 | tf_op jit(solution)/shard_map/ppermute | solution.py:325
  117.0 2.2 %collective-permute-done.3.refs_7_ = bf16[8,128,128]{2,1,0:T(8,128)(2,1)S(1)} collective-permute-done((bf16[8,128,128]{2,1,0:T(8,128)(2,1)S(1)}, bf16[8,128,128]{2,1,0:T(8,128)(2,1)S(1)}, u32[]{:S(2)}, u32[]{:S(2)}) %collective-permute-start.3) | collective-permute-done | bytes 262176 | tf_op jit(solution)/shard_map/ppermute | solution.py:325
  119.2 3.1 %hop.7 = bf16[3072,256]{1,0:T(8,128)(2,1)} custom-call(bf16[48,128,128]{2,1,0:T(8,128)(2,1)S(1)} %copy-done, s32[96]{0:T(128)S(1)} %reshape.18.refs_1_, s32[2,8]{1,0:T(2,128)S(1)} %bitcast.25, s32[1]{0:T(128)} %get-tuple-element.14.refs_3_, bf16[24,128,128]{2,1,0:T(8,128)(2,1)S(1)} %get-tuple-element.15.refs_4_.refs_5_, ...), custom_call_target="tpu_custom_call", output_to_operand_aliasing={{}: (8, {})} | custom-call | flops 201326592 | bytes 5242880 | tf_op jit(solution)/shard_map/hop/pallas_call | solution.py:275
  (4 shorter events, 0.2 us)
Async XLA Ops:
  1.3 1.6 %copy-start.2 = (bf16[1024,1024]{1,0:T(8,128)(2,1)S(1)}, bf16[1024,1024]{1,0:T(8,128)(2,1)}, u32[]{:S(2)}) copy-start(bf16[1024,1024]{1,0:T(8,128)(2,1)} %features.1) | copy-start | bytes 6291460
  2.9 1.0 copy-start.3
  4.0 0.7 copy-start.4
  4.7 0.7 copy-start.5
  16.0 7.3 %copy-start.6 = (s32[48,2]{0,1:T(2,128)S(1)}, s32[48,2]{0,1:T(2,128)}, u32[]{:S(2)}) copy-start(s32[48,2]{0,1:T(2,128)} %param.17) | copy-start | bytes 1156
  16.0 48.9 %copy-start.1 = (s32[1,2,8]{2,1,0:T(2,128)S(1)}, s32[1,2,8]{2,1,0:T(2,128)}, u32[]{:S(2)}) copy-start(s32[1,2,8]{2,1,0:T(2,128)} %param.19) | copy-start | bytes 196
  16.0 48.9 %all-to-all-start = ((bf16[32,208,128]{2,1,0:T(8,128)(2,1)}), bf16[32,208,128]{2,1,0:T(8,128)(2,1)S(1)}, u32[]{:S(2)}, u32[]{:S(2)}) async-start(bf16[32,208,128]{2,1,0:T(8,128)(2,1)} %project.1), calls=%async_computation | async-start | bytes 3407872 | tf_op jit(solution)/shard_map/all_to_all | solution.py:318
  71.1 18.3 %collective-permute-start.4 = (bf16[8,128,128]{2,1,0:T(8,128)(2,1)S(1)}, bf16[8,128,128]{2,1,0:T(8,128)(2,1)S(1)}, u32[]{:S(2)}, u32[]{:S(2)}) collective-permute-start(bf16[8,128,128]{2,1,0:T(8,128)(2,1)S(1)} %get-tuple-element.26), channel_id=1, source_target_pairs={{0,1},{1,2},{2,3},{3,4},{4,5},{5,6},{6,7},{7,0},{8,9},{9,10},{10,1... | collective-permute-start | bytes 786440 | tf_op jit(solution)/shard_map/ppermute | solution.py:325
  71.5 17.9 %collective-permute-start.5 = (bf16[8,128,128]{2,1,0:T(8,128)(2,1)S(1)}, bf16[8,128,128]{2,1,0:T(8,128)(2,1)S(1)}, u32[]{:S(2)}, u32[]{:S(2)}) collective-permute-start(bf16[8,128,128]{2,1,0:T(8,128)(2,1)S(1)} %get-tuple-element.25), channel_id=1, source_target_pairs={{1,0},{2,1},{3,2},{4,3},{5,4},{6,5},{7,6},{0,7},{9,8},{10,9},{11,1... | collective-permute-start | bytes 786440 | tf_op jit(solution)/shard_map/ppermute | solution.py:325
  75.8 13.5 %copy-start = (bf16[48,128,128]{2,1,0:T(8,128)(2,1)S(1)}, bf16[48,128,128]{2,1,0:T(8,128)(2,1)}, u32[]{:S(2)}) copy-start(bf16[48,128,128]{2,1,0:T(8,128)(2,1)} %refs_0_.7) | copy-start | bytes 4718596
  81.9 14.5 %collective-permute-start = (bf16[8,128,128]{2,1,0:T(8,128)(2,1)S(1)}, bf16[8,128,128]{2,1,0:T(8,128)(2,1)S(1)}, u32[]{:S(2)}, u32[]{:S(2)}) collective-permute-start(bf16[8,128,128]{2,1,0:T(8,128)(2,1)S(1)} %get-tuple-element.30), channel_id=1, source_target_pairs={{0,1},{1,2},{2,3},{3,4},{4,5},{5,6},{6,7},{7,0},{8,9},{9,10},{10,1... | collective-permute-start | bytes 786440 | tf_op jit(solution)/shard_map/ppermute | solution.py:325
  82.0 21.1 %collective-permute-start.1 = (bf16[8,128,128]{2,1,0:T(8,128)(2,1)S(1)}, bf16[8,128,128]{2,1,0:T(8,128)(2,1)S(1)}, u32[]{:S(2)}, u32[]{:S(2)}) collective-permute-start(bf16[8,128,128]{2,1,0:T(8,128)(2,1)S(1)} %get-tuple-element.29), channel_id=1, source_target_pairs={{1,0},{2,1},{3,2},{4,3},{5,4},{6,5},{7,6},{0,7},{9,8},{10,9},{11,1... | collective-permute-start | bytes 786440 | tf_op jit(solution)/shard_map/ppermute | solution.py:325
  91.6 20.5 %collective-permute-start.6 = (bf16[8,128,128]{2,1,0:T(8,128)(2,1)S(1)}, bf16[8,128,128]{2,1,0:T(8,128)(2,1)S(1)}, u32[]{:S(2)}, u32[]{:S(2)}) collective-permute-start(bf16[8,128,128]{2,1,0:T(8,128)(2,1)S(1)} %get-tuple-element.24), channel_id=1, source_target_pairs={{0,1},{1,2},{2,3},{3,4},{4,5},{5,6},{6,7},{7,0},{8,9},{9,10},{10,1... | collective-permute-start | bytes 786440 | tf_op jit(solution)/shard_map/ppermute | solution.py:325
  94.2 18.0 %collective-permute-start.7 = (bf16[8,128,128]{2,1,0:T(8,128)(2,1)S(1)}, bf16[8,128,128]{2,1,0:T(8,128)(2,1)S(1)}, u32[]{:S(2)}, u32[]{:S(2)}) collective-permute-start(bf16[8,128,128]{2,1,0:T(8,128)(2,1)S(1)} %get-tuple-element.23), channel_id=1, source_target_pairs={{1,0},{2,1},{3,2},{4,3},{5,4},{6,5},{7,6},{0,7},{9,8},{10,9},{11,1... | collective-permute-start | bytes 786440 | tf_op jit(solution)/shard_map/ppermute | solution.py:325
  105.4 11.6 %collective-permute-start.2 = (bf16[8,128,128]{2,1,0:T(8,128)(2,1)S(1)}, bf16[8,128,128]{2,1,0:T(8,128)(2,1)S(1)}, u32[]{:S(2)}, u32[]{:S(2)}) collective-permute-start(bf16[8,128,128]{2,1,0:T(8,128)(2,1)S(1)} %get-tuple-element.28), channel_id=1, source_target_pairs={{0,1},{1,2},{2,3},{3,4},{4,5},{5,6},{6,7},{7,0},{8,9},{9,10},{10,1... | collective-permute-start | bytes 786440 | tf_op jit(solution)/shard_map/ppermute | solution.py:325
  105.4 13.8 %collective-permute-start.3 = (bf16[8,128,128]{2,1,0:T(8,128)(2,1)S(1)}, bf16[8,128,128]{2,1,0:T(8,128)(2,1)S(1)}, u32[]{:S(2)}, u32[]{:S(2)}) collective-permute-start(bf16[8,128,128]{2,1,0:T(8,128)(2,1)S(1)} %get-tuple-element.27), channel_id=1, source_target_pairs={{1,0},{2,1},{3,2},{4,3},{5,4},{6,5},{7,6},{0,7},{9,8},{10,9},{11,1... | collective-permute-start | bytes 786440 | tf_op jit(solution)/shard_map/ppermute | solution.py:325
where the time goes:
time: 123 us; the launch traced here: 122 us
  waiting for transfers between devices  56.7 us (46%)
  Pallas kernels  33.4 us (27%)
  starting transfers between devices  26.4 us (21%)
  local copies, waits for them, and re-layouts  5.73 us (5%)
    all_to_all x1, waiting for transfers between devices, local(): lax.all_to_all(outgoing, ('dp', 'dom'), split_axis=0, concat_axis=0, tile...  41.4 us
    ppermute x4, starting transfers between devices, exchange(): lax.ppermute(send[1], 'dom', backward)  16 us
    pallas_call x2, Pallas kernels, place(): pl.pallas_call(functools.partial(place_kernel, slots, half, halves), out_...  12.1 us
    pallas_call x1, Pallas kernels, project(): pl.pallas_call(functools.partial(project_kernel, parts, slots), out_shape...  10.7 us
    pallas_call x4, Pallas kernels, hop(): pl.pallas_call(functools.partial(hop_kernel, last), out_shape=out_shape,...  10.7 us
    ppermute x4, waiting for transfers between devices, exchange(): lax.ppermute(send[1], 'dom', backward)  8.88 us
    all_to_all x1, starting transfers between devices, local(): lax.all_to_all(outgoing, ('dp', 'dom'), split_axis=0, concat_axis=0, tile...  7.3 us
    ppermute x4, waiting for transfers between devices, exchange(): lax.ppermute(send[0], 'dom', forward)  6.39 us
  transfers between devices with their start and end apart: 9, of which 6 were waited for; matrix products, arithmetic and copies ran while one was open for 0% of the time, Pallas kernels for 11%

commit v1 on v0

v1 whole, which is shorter than its diff:
```python
import functools

import jax
import jax.numpy as jnp
from jax import lax
from jax.experimental import pallas as pl
from jax.experimental.pallas import tpu as pltpu
from jax.sharding import PartitionSpec as P

HOPS = 2
ALPHA = 0.1
LANES = 128
PACK = 16
GROUP = LANES // PACK
VMEM_LIMIT = 48 * 1024 * 1024
PROJECT_VMEM = 62 * 1024 * 1024

BF16 = jnp.bfloat16
F32 = jnp.float32


def iota(shape, dim):
    return lax.broadcasted_iota(jnp.int32, shape, dim)


def gelu(value):
    return 0.5 * value * (1.0 + lax.erf(value * (0.5**0.5)))


def project_kernel(
    parts,
    slots,
    features_hbm,
    w_first_hbm,
    b_first,
    w_second_hbm,
    b_second,
    dest_part,
    dest_slot,
    lane_base,
    out,
    features,
    w_first,
    w_second,
    embedded,
    packed,
    arrival,
    leaving,
):
    copies = [
        pltpu.make_async_copy(source, held, arrival.at[index])
        for index, (source, held) in enumerate(
            ((features_hbm, features), (w_first_hbm, w_first), (w_second_hbm, w_second))
        )
    ]
    for copy in copies:
        copy.start()
    width = w_second.shape[1]
    count = dest_part.shape[0]
    part = dest_part[...][None, :]
    onehot = (iota((parts, count), 0) == part).astype(F32)
    blocks = [onehot[:, at : at + LANES] for at in range(0, count, LANES)]
    earlier = (iota((LANES, LANES), 0) < iota((LANES, LANES), 1)).astype(BF16)
    within = jnp.dot(
        jnp.concatenate(blocks, axis=0).astype(BF16), earlier, preferred_element_type=F32
    )
    offset = jnp.zeros((parts, 1), F32)
    pieces = []
    for index, piece in enumerate(blocks):
        before = within[index * parts : (index + 1) * parts, :] + offset
        pieces.append(jnp.sum(before * piece, axis=0, keepdims=True))
        offset = offset + jnp.sum(piece, axis=1, keepdims=True)
    position = jnp.concatenate(pieces, axis=1).astype(jnp.int32)
    target = part * slots + position

    coded = dest_slot[...][None, :] + 1
    high = jnp.right_shift(coded, 6)
    low = coded - high * 64
    spot = (iota((LANES, count), 0) == position).astype(BF16)
    digits = []
    for digit in (high, low):
        marked = (onehot * digit.astype(F32)).astype(BF16)
        digits.append(
            lax.dot_general(marked, spot, (((1,), (1,)), ((), ())), preferred_element_type=F32)
        )
    base = lane_base[0]
    lane = iota((parts, LANES), 1)
    mine = (lane >= base) & (lane < base + PACK)
    row = iota((parts, PACK, LANES), 1)
    listed = jnp.zeros((parts, PACK, LANES), F32)
    for at, digit in zip((0, 8), digits):
        for j in range(slots // PACK):
            turned = pltpu.roll(digit, lax.rem(base - j * PACK + LANES, LANES), 1)
            turned = jnp.where(mine, turned, 0.0)
            listed = jnp.where(row == at + j, turned[:, None, :], listed)
    halves = width // LANES
    packed[:, halves * slots :, :] = listed.astype(BF16)

    copies[0].wait()
    copies[1].wait()
    hidden = jnp.dot(features[...], w_first[...], preferred_element_type=F32)
    hidden = gelu(hidden + b_first[...].astype(F32)[None, :]).astype(BF16)
    copies[2].wait()
    total = jnp.dot(hidden, w_second[...], preferred_element_type=F32)
    embedded[...] = (total + b_second[...].astype(F32)[None, :]).astype(BF16)

    size = GROUP * slots
    slot = iota((size, count), 0)
    sends = []
    for group in range(parts // GROUP):
        select = (slot == target - group * size).astype(BF16)
        moved = jnp.dot(select, embedded[...], preferred_element_type=F32).astype(BF16)
        dests = slice(group * GROUP, (group + 1) * GROUP)
        for half in range(halves):
            piece = moved[:, half * LANES : (half + 1) * LANES]
            packed[dests, half * slots : (half + 1) * slots, :] = piece.reshape(
                GROUP, slots, LANES
            )
        sends.append(pltpu.make_async_copy(packed.at[dests], out.at[dests], leaving.at[group]))
        sends[-1].start()
    for send in sends:
        send.wait()


def project(parts, slots, features, w_first, b_first, w_second, b_second, part, slot, lane_base):
    rows, depth = features.shape
    hidden, width = w_second.shape
    length = (width // LANES) * slots + PACK
    vmem = pl.BlockSpec(memory_space=pltpu.VMEM)
    hbm = pl.BlockSpec(memory_space=pl.ANY)
    return pl.pallas_call(
        functools.partial(project_kernel, parts, slots),
        out_shape=jax.ShapeDtypeStruct((parts, length, LANES), BF16),
        in_specs=[hbm, hbm, vmem, hbm, vmem, vmem, vmem, pl.BlockSpec(memory_space=pltpu.SMEM)],
        out_specs=hbm,
        scratch_shapes=[
            pltpu.VMEM((rows, depth), BF16),
            pltpu.VMEM((depth, hidden), BF16),
            pltpu.VMEM((hidden, width), BF16),
            pltpu.VMEM((rows, width), BF16),
            pltpu.VMEM((parts, length, LANES), BF16),
            pltpu.SemaphoreType.DMA((3,)),
            pltpu.SemaphoreType.DMA((parts // GROUP,)),
        ],
        compiler_params=pltpu.CompilerParams(vmem_limit_bytes=PROJECT_VMEM),
        cost_estimate=pl.CostEstimate(
            flops=2 * rows * hidden * (depth + width), bytes_accessed=8 << 20, transcendentals=0
        ),
        name="project",
    )(features, w_first, b_first, w_second, b_second, part, slot, lane_base)


def arrived_rows(slots, halves, arrived):
    ids, rows = [], []
    for first in range(0, arrived.shape[0], GROUP):
        sources = slice(first, first + GROUP)
        listed = jnp.sum(arrived[sources, halves * slots :, :].astype(F32), axis=0)
        coded = (listed[:8] * 64.0 + listed[8:]).astype(jnp.int32)
        for j in range(slots // PACK):
            ids.append(coded[j : j + 1, :] - 1)
            pieces = []
            for half in range(halves):
                at = half * slots + j * PACK
                pieces.append(arrived[sources, at : at + PACK, :].reshape(LANES, LANES))
            rows.append(jnp.concatenate(pieces, axis=1))
    return jnp.concatenate(ids, axis=1), jnp.concatenate(rows, axis=0)


def listed_kernel(slots, halves, arrived, halo_send, *sends):
    ids, rows = arrived_rows(slots, halves, arrived)
    _, listed, block_rows, _ = sends[0].shape
    slot = iota((block_rows, ids.shape[1]), 0)
    several = 4
    for side in range(2):
        for first in range(0, listed, several):
            select = [
                (slot == ids - halo_send[side, k] * block_rows).astype(BF16)
                for k in range(first, first + several)
            ]
            placed = jnp.dot(jnp.concatenate(select, axis=0), rows, preferred_element_type=F32)
            for half, send in enumerate(sends):
                piece = placed[:, half * LANES : (half + 1) * LANES].astype(BF16)
                send[side, first : first + several] = piece.reshape(several, block_rows, LANES)


def place_kernel(slots, halves, arrived, size, *starts):
    ids, rows = arrived_rows(slots, halves, arrived)
    size[0] = jnp.sum((ids >= 0).astype(jnp.int32))
    block_count, block_rows, _ = starts[0].shape
    several = 4
    slot = iota((several * block_rows, ids.shape[1]), 0)
    for first in range(0, block_count, several):
        select = (slot == ids - first * block_rows).astype(BF16)
        placed = jnp.dot(select, rows, preferred_element_type=F32)
        for half, start in enumerate(starts):
            piece = placed[:, half * LANES : (half + 1) * LANES].astype(BF16)
            start[first : first + several] = piece.reshape(several, block_rows, LANES)


def vmem_spec():
    return pl.BlockSpec(memory_space=pltpu.VMEM)


def smem_spec():
    return pl.BlockSpec(memory_space=pltpu.SMEM)


def listed_blocks(slots, halves, block_rows, arrived, halo_send):
    listed = halo_send.shape[1]
    depth = arrived.shape[0] * slots
    return pl.pallas_call(
        functools.partial(listed_kernel, slots, halves),
        out_shape=[jax.ShapeDtypeStruct((2, listed, block_rows, LANES), BF16)] * halves,
        in_specs=[vmem_spec(), smem_spec()],
        out_specs=[vmem_spec()] * halves,
        compiler_params=pltpu.CompilerParams(vmem_limit_bytes=VMEM_LIMIT),
        cost_estimate=pl.CostEstimate(
            flops=4 * listed * block_rows * depth * halves * LANES,
            bytes_accessed=4 << 20,
            transcendentals=0,
        ),
        name="listed",
    )(arrived, halo_send)


def place(slots, halves, block_count, block_rows, arrived):
    depth = arrived.shape[0] * slots
    return pl.pallas_call(
        functools.partial(place_kernel, slots, halves),
        out_shape=[jax.ShapeDtypeStruct((1,), jnp.int32)]
        + [jax.ShapeDtypeStruct((block_count, block_rows, LANES), BF16)] * halves,
        in_specs=[vmem_spec()],
        out_specs=[smem_spec()] + [vmem_spec()] * halves,
        compiler_params=pltpu.CompilerParams(vmem_limit_bytes=VMEM_LIMIT),
        cost_estimate=pl.CostEstimate(
            flops=2 * block_count * block_rows * depth * halves * LANES,
            bytes_accessed=4 << 20,
            transcendentals=0,
        ),
        name="place",
    )(arrived)


def inner_kernel(halo, tiles, coords, start, current, partial):
    block_count = start.shape[0]
    for b in range(block_count):
        term = jnp.dot(tiles[b], current[b], preferred_element_type=F32)
        partial[b] = (1.0 - ALPHA) * term + ALPHA * start[b].astype(F32)
    for t in range(block_count + 2 * halo, tiles.shape[0]):
        index = coords[2 * t + 1]
        source = current[jnp.minimum(index, block_count - 1)]
        source = jnp.where(index < block_count, source, jnp.zeros_like(source))
        term = jnp.dot(tiles[t], source, preferred_element_type=F32)
        partial[coords[2 * t]] += (1.0 - ALPHA) * term


def outer_kernel(last, *refs):
    tiles, coords, halo_send, size, partial, low, high = refs[:7]
    if last:
        out, summed = refs[-2:]
    else:
        out, send, summed = refs[-3:]
    block_count, block_rows, width = partial.shape
    listed = low.shape[0]
    own = block_count
    summed[...] = jnp.zeros_like(summed)
    for t in range(own, tiles.shape[0]):
        if t < own + listed:
            source = low[t - own]
        elif t < own + 2 * listed:
            source = high[t - own - listed]
        else:
            index = coords[2 * t + 1]
            below = low[jnp.clip(index - own, 0, listed - 1)]
            above = high[jnp.clip(index - own - listed, 0, listed - 1)]
            source = jnp.where(index < own + listed, below, above)
            source = jnp.where(index < own, jnp.zeros_like(source), source)
        summed[coords[2 * t]] += jnp.dot(tiles[t], source, preferred_element_type=F32)
    row = iota((block_rows, width), 0)
    for b in range(block_count):
        mixed = (1.0 - ALPHA) * summed[b] + partial[b]
        mixed = jnp.where(row < size[0] - b * block_rows, mixed, 0.0).astype(BF16)
        if last:
            out[b * block_rows : (b + 1) * block_rows, :] = mixed
        else:
            out[b] = mixed
    if not last:
        for side in range(2):
            for k in range(listed):
                send[side, k] = out[halo_send[side, k]]


def inner(halo, tiles, coords, start, current):
    return pl.pallas_call(
        functools.partial(inner_kernel, halo),
        out_shape=jax.ShapeDtypeStruct(start.shape, F32),
        in_specs=[vmem_spec(), smem_spec(), vmem_spec(), vmem_spec()],
        out_specs=vmem_spec(),
        compiler_params=pltpu.CompilerParams(vmem_limit_bytes=VMEM_LIMIT),
        cost_estimate=pl.CostEstimate(
            flops=tiles.size * LANES, bytes_accessed=4 << 20, transcendentals=0
        ),
        name="inner",
    )(tiles, coords, start, current)


def outer(tiles, coords, halo_send, size, partial, low, high, half=None, halves=1, held=None):
    block_count, block_rows, width = partial.shape
    listed = low.shape[0]
    last = half is not None
    operands = [tiles, coords, halo_send, size, partial, low, high]
    vmem = vmem_spec()
    in_specs = [vmem, smem_spec(), smem_spec(), smem_spec(), vmem, vmem, vmem]
    aliases = {}
    if last:
        capacity = block_count * block_rows
        out_shape = jax.ShapeDtypeStruct((capacity, width * halves), BF16)
        out_specs = pl.BlockSpec((capacity, width), lambda i: (0, half))
        if held is not None:
            aliases = {len(operands): 0}
            operands.append(held)
            in_specs.append(pl.BlockSpec(memory_space=pl.ANY))
        in_specs = [
            spec if spec is not vmem else pl.BlockSpec(x.shape, lambda i, n=x.ndim: (0,) * n)
            for spec, x in zip(in_specs, operands)
        ]
        grid = (1,)
    else:
        out_shape = [
            jax.ShapeDtypeStruct((block_count, block_rows, width), BF16),
            jax.ShapeDtypeStruct((2, listed, block_rows, width), BF16),
        ]
        out_specs = [vmem, vmem]
        grid = ()
    return pl.pallas_call(
        functools.partial(outer_kernel, last),
        out_shape=out_shape,
        grid=grid,
        in_specs=in_specs,
        out_specs=out_specs,
        scratch_shapes=[pltpu.VMEM((block_count, block_rows, width), F32)],
        input_output_aliases=aliases,
        compiler_params=pltpu.CompilerParams(vmem_limit_bytes=VMEM_LIMIT),
        cost_estimate=pl.CostEstimate(
            flops=tiles.size * width, bytes_accessed=4 << 20, transcendentals=0
        ),
        name="outer",
    )(*operands)


def local(
    features,
    w_first,
    b_first,
    w_second,
    b_second,
    dest_part,
    dest_slot,
    tile_coords,
    tile_values,
    halo_send,
):
    count_dp = lax.axis_size("dp")
    count_dom = lax.axis_size("dom")
    parts = count_dp * count_dom
    row_count = features.shape[0]
    capacity = 3 * row_count
    slots = -(-capacity // parts // PACK) * PACK
    width = w_second.shape[1]
    halves = width // LANES
    block_rows = tile_values.shape[1]
    block_count = capacity // block_rows
    me = lax.axis_index("dp") * count_dom + lax.axis_index("dom")
    lane_base = (lax.rem(me, GROUP) * PACK).astype(jnp.int32).reshape(1)
    outgoing = project(
        parts, slots, features, w_first, b_first, w_second, b_second, dest_part, dest_slot, lane_base
    )
    arrived = lax.all_to_all(outgoing, ("dp", "dom"), split_axis=0, concat_axis=0, tiled=True)
    coords = tile_coords.reshape(-1)
    lists = halo_send[0]
    forward = [(i, (i + 1) % count_dom) for i in range(count_dom)]
    backward = [((i + 1) % count_dom, i) for i in range(count_dom)]

    def exchange(send):
        return lax.ppermute(send[0], "dom", forward), lax.ppermute(send[1], "dom", backward)

    halos = [
        exchange(send) for send in listed_blocks(slots, halves, block_rows, arrived, lists)
    ]
    size, *starts = place(slots, halves, block_count, block_rows, arrived)
    fields = list(starts)
    held = None
    for repeat in range(HOPS):
        for half in range(halves):
            partial = inner(lists.shape[1], tile_values, coords, starts[half], fields[half])
            operands = tile_values, coords, lists, size, partial, *halos[half]
            if repeat < HOPS - 1:
                fields[half], send = outer(*operands)
                halos[half] = exchange(send)
            else:
                held = outer(*operands, half=half, halves=halves, held=held)
    return held


def solution(mesh):
    placed = (
        P(("dp", "dom"), None),
        P(),
        P(),
        P(),
        P(),
        P(("dp", "dom")),
        P(("dp", "dom")),
        P(("dp", "dom"), None),
        P(("dp", "dom"), None, None),
        P(("dp", "dom"), None, None),
    )
    return jax.shard_map(
        local, mesh=mesh, in_specs=placed, out_specs=P(("dp", "dom"), None), check_vma=False
    )
```

time: 123 us -> 115 us (0.935)
  local copies, waits for them, and re-layouts: 5.73 us -> 0.4 us
  waiting for transfers between devices: 56.7 us -> 54.2 us
    unnamed x15 -> x7, local copies, waits for them, and re-layouts: 4.11 us -> 0.11 us
    ppermute x4, waiting for transfers between devices: 6.39 us -> 2.73 us  [exchange(): lax.ppermute(send[0], 'dom', forward)]
    ppermute x4, starting transfers between devices: 3.06 us -> 0.58 us  [exchange(): lax.ppermute(send[0], 'dom', forward)]
    ppermute x4, starting transfers between devices: 16 us -> 18.5 us  [exchange(): lax.ppermute(send[1], 'dom', backward)]
    reshape x2 -> x0, local copies, waits for them, and re-layouts: 1.34 us -> none  [the longest x1 0.69 us: project(): b_first.reshape(1, hidden)]
    pallas_call x6 -> x10, Pallas kernels: 22.7 us -> 22.7 us  [the longest x4 9.16 us: outer(): pl.pallas_call(functools.partial(outer_kernel, last), out_shape=out_shape...]
  transfers between devices with their start and end apart: 9 -> 9, of which waited for: 6 -> 6; matrix products, arithmetic and copies ran while one was open for 0% -> 0% of each run, Pallas kernels for 11% -> 14%
where the time goes in v1:
time: 115 us; the launch traced here: 114 us
  waiting for transfers between devices  54.2 us (47%)
  Pallas kernels  33.2 us (29%)
  starting transfers between devices  26.3 us (23%)
    all_to_all x1, waiting for transfers between devices, local(): lax.all_to_all(outgoing, ('dp', 'dom'), split_axis=0, concat_axis=0, tile...  41.4 us
    ppermute x4, starting transfers between devices, exchange(): lax.ppermute(send[1], 'dom', backward)  18.5 us
    pallas_call x1, Pallas kernels, project(): pl.pallas_call(functools.partial(project_kernel, parts, slots), out_shape...  10.5 us
    ppermute x4, waiting for transfers between devices, exchange(): lax.ppermute(send[1], 'dom', backward)  10 us
    pallas_call x4, Pallas kernels, outer(): pl.pallas_call(functools.partial(outer_kernel, last), out_shape=out_shape...  9.16 us
    all_to_all x1, starting transfers between devices, local(): lax.all_to_all(outgoing, ('dp', 'dom'), split_axis=0, concat_axis=0, tile...  7.28 us
    pallas_call x1, Pallas kernels, place(): pl.pallas_call(functools.partial(place_kernel, slots, halves), out_shape=...  5.5 us
    pallas_call x4, Pallas kernels, inner(): pl.pallas_call(functools.partial(inner_kernel, halo), out_shape=jax.Shape...  4.12 us
  transfers between devices with their start and end apart: 9, of which 6 were waited for; matrix products, arithmetic and copies ran while one was open for 0% of the time, Pallas kernels for 14%

profile of v1, /device:TPU:0, one launch (start us, length us, event | category | flops | bytes accessed | tf_op | source)
XLA Modules:
  0.0 114.3 jit_solution(4165964257377169295)
XLA Ops:
  0.0 10.5 %project.1 = bf16[32,208,128]{2,1,0:T(8,128)(2,1)} custom-call(bf16[1024,1024]{1,0:T(8,128)(2,1)} %features_hbm.1, bf16[1024,1024]{1,0:T(8,128)(2,1)} %w_first_hbm.1, bf16[1024]{0:T(1024)(128)(2,1)} %b_first.1, bf16[1024,256]{1,0:T(8,128)(2,1)} %w_second_hbm.1, bf16[256]{0:T(256)(128)(2,1)} %b_second.1, s32[1024]{0:T(1024)} %dest_part.1, s32[1024]{0:T(1024)} %dest_slot.1, ...), custom_call_target="tpu_custom_call" | custom-call | flops 2684354560 | bytes 8388608 | tf_op jit(solution)/shard_map/project/pallas_call | solution.py:131
  10.5 0.0 copy-start.2
  10.5 0.0 copy-start.1
  10.5 7.3 %all-to-all-start = ((bf16[32,208,128]{2,1,0:T(8,128)(2,1)}), bf16[32,208,128]{2,1,0:T(8,128)(2,1)S(1)}, u32[]{:S(2)}, u32[]{:S(2)}) async-start(bf16[32,208,128]{2,1,0:T(8,128)(2,1)} %project.1), calls=%async_computation | async-start | bytes 3407872 | tf_op jit(solution)/shard_map/all_to_all | solution.py:378
  17.8 0.0 copy-done.2
  17.8 0.1 copy.13
  17.9 0.1 reshape.6.coords.refs_1_
  18.0 41.4 %all-to-all-done.arrived = bf16[32,208,128]{2,1,0:T(8,128)(2,1)S(1)} async-done(((bf16[32,208,128]{2,1,0:T(8,128)(2,1)}), bf16[32,208,128]{2,1,0:T(8,128)(2,1)S(1)}, u32[]{:S(2)}, u32[]{:S(2)}) %all-to-all-start) | async-done | bytes 1703968 | tf_op jit(solution)/shard_map/all_to_all | solution.py:378
  59.4 0.0 copy-done.1
  59.4 4.0 %listed.1 = (bf16[2,8,128,128]{3,2,1,0:T(8,128)(2,1)S(1)}, bf16[2,8,128,128]{3,2,1,0:T(8,128)(2,1)S(1)}) custom-call(bf16[32,208,128]{2,1,0:T(8,128)(2,1)S(1)} %all-to-all-done.arrived, s32[2,8]{1,0:T(2,128)S(1)} %bitcast.18), custom_call_target="tpu_custom_call" | custom-call | flops 3221225472 | bytes 4194304 | tf_op jit(solution)/shard_map/listed/pallas_call | solution.py:211
  63.4 0.4 collective-permute-start.4
  63.9 4.4 %collective-permute-start.5 = (bf16[8,128,128]{2,1,0:T(8,128)(2,1)S(1)}, bf16[8,128,128]{2,1,0:T(8,128)(2,1)S(1)}, u32[]{:S(2)}, u32[]{:S(2)}) collective-permute-start(bf16[8,128,128]{2,1,0:T(8,128)(2,1)S(1)} %get-tuple-element.25), channel_id=1, source_target_pairs={{1,0},{2,1},{3,2},{4,3},{5,4},{6,5},{7,6},{0,7},{9,8},{10,9},{11,1... | collective-permute-start | bytes 786440 | tf_op jit(solution)/shard_map/ppermute | solution.py:385
  68.3 0.1 collective-permute-start
  68.3 0.0 copy-start
  68.3 4.7 %collective-permute-start.1 = (bf16[8,128,128]{2,1,0:T(8,128)(2,1)S(1)}, bf16[8,128,128]{2,1,0:T(8,128)(2,1)S(1)}, u32[]{:S(2)}, u32[]{:S(2)}) collective-permute-start(bf16[8,128,128]{2,1,0:T(8,128)(2,1)S(1)} %get-tuple-element.29), channel_id=1, source_target_pairs={{1,0},{2,1},{3,2},{4,3},{5,4},{6,5},{7,6},{0,7},{9,8},{10,9},{11,1... | collective-permute-start | bytes 786440 | tf_op jit(solution)/shard_map/ppermute | solution.py:385
  73.0 5.5 %place.1 = (s32[1]{0:T(128)}, bf16[24,128,128]{2,1,0:T(8,128)(2,1)S(1)}, bf16[24,128,128]{2,1,0:T(8,128)(2,1)S(1)}) custom-call(bf16[32,208,128]{2,1,0:T(8,128)(2,1)S(1)} %all-to-all-done.arrived), custom_call_target="tpu_custom_call" | custom-call | flops 4831838208 | bytes 4194304 | tf_op jit(solution)/shard_map/place/pallas_call | solution.py:228
  78.6 0.0 copy-done
  78.6 1.0 inner.6.refs_4_
  79.6 1.0 inner.4.refs_4_
  80.6 1.1 collective-permute-done.4.refs_5_
  81.7 2.5 %collective-permute-done.5.refs_6_ = bf16[8,128,128]{2,1,0:T(8,128)(2,1)S(1)} collective-permute-done((bf16[8,128,128]{2,1,0:T(8,128)(2,1)S(1)}, bf16[8,128,128]{2,1,0:T(8,128)(2,1)S(1)}, u32[]{:S(2)}, u32[]{:S(2)}) %collective-permute-start.5) | collective-permute-done | bytes 262176 | tf_op jit(solution)/shard_map/ppermute | solution.py:385
  84.2 1.9 %outer.5 = (bf16[24,128,128]{2,1,0:T(8,128)(2,1)S(1)}, bf16[2,8,128,128]{3,2,1,0:T(8,128)(2,1)S(1)}) custom-call(bf16[48,128,128]{2,1,0:T(8,128)(2,1)S(1)} %copy-done, s32[96]{0:T(128)S(1)} %reshape.6.coords.refs_1_, s32[2,8]{1,0:T(2,128)S(1)} %bitcast.19, s32[1]{0:T(128)} %get-tuple-element.14.refs_3_, f32[24,128,128]{2,1,0:T(8,128)S(1)} %inner.6.refs_4_, ...), custom_call_target="tpu_custom_call" | custom-call | flops 100663296 | bytes 4194304 | tf_op jit(solution)/shard_map/outer/pallas_call | solution.py:335
  86.1 0.1 collective-permute-start.6
  86.2 4.7 %collective-permute-start.7 = (bf16[8,128,128]{2,1,0:T(8,128)(2,1)S(1)}, bf16[8,128,128]{2,1,0:T(8,128)(2,1)S(1)}, u32[]{:S(2)}, u32[]{:S(2)}) collective-permute-start(bf16[8,128,128]{2,1,0:T(8,128)(2,1)S(1)} %get-tuple-element.23), channel_id=1, source_target_pairs={{1,0},{2,1},{3,2},{4,3},{5,4},{6,5},{7,6},{0,7},{9,8},{10,9},{11,1... | collective-permute-start | bytes 786440 | tf_op jit(solution)/shard_map/ppermute | solution.py:385
  90.9 0.0 collective-permute-done.refs_5_
  90.9 0.0 collective-permute-done.1.refs_6_
  90.9 1.9 %outer.4 = (bf16[24,128,128]{2,1,0:T(8,128)(2,1)S(1)}, bf16[2,8,128,128]{3,2,1,0:T(8,128)(2,1)S(1)}) custom-call(bf16[48,128,128]{2,1,0:T(8,128)(2,1)S(1)} %copy-done, s32[96]{0:T(128)S(1)} %reshape.6.coords.refs_1_, s32[2,8]{1,0:T(2,128)S(1)} %bitcast.20, s32[1]{0:T(128)} %get-tuple-element.14.refs_3_, f32[24,128,128]{2,1,0:T(8,128)S(1)} %inner.4.refs_4_, ...), custom_call_target="tpu_custom_call" | custom-call | flops 100663296 | bytes 4194304 | tf_op jit(solution)/shard_map/outer/pallas_call | solution.py:335
  92.9 0.1 collective-permute-start.2
  92.9 4.7 %collective-permute-start.3 = (bf16[8,128,128]{2,1,0:T(8,128)(2,1)S(1)}, bf16[8,128,128]{2,1,0:T(8,128)(2,1)S(1)}, u32[]{:S(2)}, u32[]{:S(2)}) collective-permute-start(bf16[8,128,128]{2,1,0:T(8,128)(2,1)S(1)} %get-tuple-element.27), channel_id=1, source_target_pairs={{1,0},{2,1},{3,2},{4,3},{5,4},{6,5},{7,6},{0,7},{9,8},{10,9},{11,1... | collective-permute-start | bytes 786440 | tf_op jit(solution)/shard_map/ppermute | solution.py:385
  97.6 1.0 inner.7.refs_4_
  98.7 1.0 inner.5.refs_4_
  99.7 1.7 %collective-permute-done.6.refs_5_ = bf16[8,128,128]{2,1,0:T(8,128)(2,1)S(1)} collective-permute-done((bf16[8,128,128]{2,1,0:T(8,128)(2,1)S(1)}, bf16[8,128,128]{2,1,0:T(8,128)(2,1)S(1)}, u32[]{:S(2)}, u32[]{:S(2)}) %collective-permute-start.6) | collective-permute-done | bytes 262176 | tf_op jit(solution)/shard_map/ppermute | solution.py:385
  101.4 5.3 %collective-permute-done.7.refs_6_ = bf16[8,128,128]{2,1,0:T(8,128)(2,1)S(1)} collective-permute-done((bf16[8,128,128]{2,1,0:T(8,128)(2,1)S(1)}, bf16[8,128,128]{2,1,0:T(8,128)(2,1)S(1)}, u32[]{:S(2)}, u32[]{:S(2)}) %collective-permute-start.7) | collective-permute-done | bytes 262176 | tf_op jit(solution)/shard_map/ppermute | solution.py:385
  106.7 2.7 %outer.6.refs_7_ = bf16[3072,256]{1,0:T(8,128)(2,1)} custom-call(bf16[48,128,128]{2,1,0:T(8,128)(2,1)S(1)} %copy-done, s32[96]{0:T(128)S(1)} %reshape.6.coords.refs_1_, s32[2,8]{1,0:T(2,128)S(1)} %bitcast.21, s32[1]{0:T(128)} %get-tuple-element.14.refs_3_, f32[24,128,128]{2,1,0:T(8,128)S(1)} %inner.7.refs_4_, ...), custom_call_target="tpu_custom_call" | custom-call | flops 100663296 | bytes 4194304 | tf_op jit(solution)/shard_map/outer/pallas_call | solution.py:335
  109.4 0.0 collective-permute-done.2.refs_5_
  109.4 2.2 %collective-permute-done.3.refs_6_ = bf16[8,128,128]{2,1,0:T(8,128)(2,1)S(1)} collective-permute-done((bf16[8,128,128]{2,1,0:T(8,128)(2,1)S(1)}, bf16[8,128,128]{2,1,0:T(8,128)(2,1)S(1)}, u32[]{:S(2)}, u32[]{:S(2)}) %collective-permute-start.3) | collective-permute-done | bytes 262176 | tf_op jit(solution)/shard_map/ppermute | solution.py:385
  111.6 2.7 %outer.7 = bf16[3072,256]{1,0:T(8,128)(2,1)} custom-call(bf16[48,128,128]{2,1,0:T(8,128)(2,1)S(1)} %copy-done, s32[96]{0:T(128)S(1)} %reshape.6.coords.refs_1_, s32[2,8]{1,0:T(2,128)S(1)} %bitcast.22, s32[1]{0:T(128)} %get-tuple-element.14.refs_3_, f32[24,128,128]{2,1,0:T(8,128)S(1)} %inner.5.refs_4_, ...), custom_call_target="tpu_custom_call", output_to_operand_aliasing={{}: (7, {})} | custom-call | flops 100663296 | bytes 4194304 | tf_op jit(solution)/shard_map/outer/pallas_call | solution.py:335
  (4 shorter events, 0.2 us)
Async XLA Ops:
  10.5 7.3 %copy-start.2 = (s32[48,2]{0,1:T(2,128)S(1)}, s32[48,2]{0,1:T(2,128)}, u32[]{:S(2)}) copy-start(s32[48,2]{0,1:T(2,128)} %param.17) | copy-start | bytes 1156
  10.5 48.9 %copy-start.1 = (s32[1,2,8]{2,1,0:T(2,128)S(1)}, s32[1,2,8]{2,1,0:T(2,128)}, u32[]{:S(2)}) copy-start(s32[1,2,8]{2,1,0:T(2,128)} %param.19) | copy-start | bytes 196
  10.5 48.9 %all-to-all-start = ((bf16[32,208,128]{2,1,0:T(8,128)(2,1)}), bf16[32,208,128]{2,1,0:T(8,128)(2,1)S(1)}, u32[]{:S(2)}, u32[]{:S(2)}) async-start(bf16[32,208,128]{2,1,0:T(8,128)(2,1)} %project.1), calls=%async_computation | async-start | bytes 3407872 | tf_op jit(solution)/shard_map/all_to_all | solution.py:378
  63.4 18.3 %collective-permute-start.4 = (bf16[8,128,128]{2,1,0:T(8,128)(2,1)S(1)}, bf16[8,128,128]{2,1,0:T(8,128)(2,1)S(1)}, u32[]{:S(2)}, u32[]{:S(2)}) collective-permute-start(bf16[8,128,128]{2,1,0:T(8,128)(2,1)S(1)} %get-tuple-element.26), channel_id=1, source_target_pairs={{0,1},{1,2},{2,3},{3,4},{4,5},{5,6},{6,7},{7,0},{8,9},{9,10},{10,1... | collective-permute-start | bytes 786440 | tf_op jit(solution)/shard_map/ppermute | solution.py:385
  63.9 20.4 %collective-permute-start.5 = (bf16[8,128,128]{2,1,0:T(8,128)(2,1)S(1)}, bf16[8,128,128]{2,1,0:T(8,128)(2,1)S(1)}, u32[]{:S(2)}, u32[]{:S(2)}) collective-permute-start(bf16[8,128,128]{2,1,0:T(8,128)(2,1)S(1)} %get-tuple-element.25), channel_id=1, source_target_pairs={{1,0},{2,1},{3,2},{4,3},{5,4},{6,5},{7,6},{0,7},{9,8},{10,9},{11,1... | collective-permute-start | bytes 786440 | tf_op jit(solution)/shard_map/ppermute | solution.py:385
  68.3 22.7 %collective-permute-start = (bf16[8,128,128]{2,1,0:T(8,128)(2,1)S(1)}, bf16[8,128,128]{2,1,0:T(8,128)(2,1)S(1)}, u32[]{:S(2)}, u32[]{:S(2)}) collective-permute-start(bf16[8,128,128]{2,1,0:T(8,128)(2,1)S(1)} %get-tuple-element.30), channel_id=1, source_target_pairs={{0,1},{1,2},{2,3},{3,4},{4,5},{5,6},{6,7},{7,0},{8,9},{9,10},{10,1... | collective-permute-start | bytes 786440 | tf_op jit(solution)/shard_map/ppermute | solution.py:385
  68.3 10.2 %copy-start = (bf16[48,128,128]{2,1,0:T(8,128)(2,1)S(1)}, bf16[48,128,128]{2,1,0:T(8,128)(2,1)}, u32[]{:S(2)}) copy-start(bf16[48,128,128]{2,1,0:T(8,128)(2,1)} %refs_0_.7) | copy-start | bytes 4718596
  68.3 22.6 %collective-permute-start.1 = (bf16[8,128,128]{2,1,0:T(8,128)(2,1)S(1)}, bf16[8,128,128]{2,1,0:T(8,128)(2,1)S(1)}, u32[]{:S(2)}, u32[]{:S(2)}) collective-permute-start(bf16[8,128,128]{2,1,0:T(8,128)(2,1)S(1)} %get-tuple-element.29), channel_id=1, source_target_pairs={{1,0},{2,1},{3,2},{4,3},{5,4},{6,5},{7,6},{0,7},{9,8},{10,9},{11,1... | collective-permute-start | bytes 786440 | tf_op jit(solution)/shard_map/ppermute | solution.py:385
  86.1 15.2 %collective-permute-start.6 = (bf16[8,128,128]{2,1,0:T(8,128)(2,1)S(1)}, bf16[8,128,128]{2,1,0:T(8,128)(2,1)S(1)}, u32[]{:S(2)}, u32[]{:S(2)}) collective-permute-start(bf16[8,128,128]{2,1,0:T(8,128)(2,1)S(1)} %get-tuple-element.24), channel_id=1, source_target_pairs={{0,1},{1,2},{2,3},{3,4},{4,5},{5,6},{6,7},{7,0},{8,9},{9,10},{10,1... | collective-permute-start | bytes 786440 | tf_op jit(solution)/shard_map/ppermute | solution.py:385
  86.2 20.5 %collective-permute-start.7 = (bf16[8,128,128]{2,1,0:T(8,128)(2,1)S(1)}, bf16[8,128,128]{2,1,0:T(8,128)(2,1)S(1)}, u32[]{:S(2)}, u32[]{:S(2)}) collective-permute-start(bf16[8,128,128]{2,1,0:T(8,128)(2,1)S(1)} %get-tuple-element.23), channel_id=1, source_target_pairs={{1,0},{2,1},{3,2},{4,3},{5,4},{6,5},{7,6},{0,7},{9,8},{10,9},{11,1... | collective-permute-start | bytes 786440 | tf_op jit(solution)/shard_map/ppermute | solution.py:385
  92.9 16.6 %collective-permute-start.2 = (bf16[8,128,128]{2,1,0:T(8,128)(2,1)S(1)}, bf16[8,128,128]{2,1,0:T(8,128)(2,1)S(1)}, u32[]{:S(2)}, u32[]{:S(2)}) collective-permute-start(bf16[8,128,128]{2,1,0:T(8,128)(2,1)S(1)} %get-tuple-element.28), channel_id=1, source_target_pairs={{0,1},{1,2},{2,3},{3,4},{4,5},{5,6},{6,7},{7,0},{8,9},{9,10},{10,1... | collective-permute-start | bytes 786440 | tf_op jit(solution)/shard_map/ppermute | solution.py:385
  92.9 18.7 %collective-permute-start.3 = (bf16[8,128,128]{2,1,0:T(8,128)(2,1)S(1)}, bf16[8,128,128]{2,1,0:T(8,128)(2,1)S(1)}, u32[]{:S(2)}, u32[]{:S(2)}) collective-permute-start(bf16[8,128,128]{2,1,0:T(8,128)(2,1)S(1)} %get-tuple-element.27), channel_id=1, source_target_pairs={{1,0},{2,1},{3,2},{4,3},{5,4},{6,5},{7,6},{0,7},{9,8},{10,9},{11,1... | collective-permute-start | bytes 786440 | tf_op jit(solution)/shard_map/ppermute | solution.py:385

commit v2 on v1

--- a/solution.py
+++ b/solution.py
@@ -12,6 +12,7 @@
 LANES = 128
 PACK = 16
 GROUP = LANES // PACK
+FLAG = 7
 VMEM_LIMIT = 48 * 1024 * 1024
 PROJECT_VMEM = 62 * 1024 * 1024
 
@@ -29,7 +30,8 @@
 
 def project_kernel(
     parts,
-    slots,
+    mate,
+    sizes,
     features_hbm,
     w_first_hbm,
     b_first,
@@ -39,6 +41,7 @@
     dest_slot,
     lane_base,
     out,
+    embedded_out,
     features,
     w_first,
     w_second,
@@ -47,6 +50,9 @@
     arrival,
     leaving,
 ):
+    direct, shared = sizes
+    room = direct + shared
+    slots = room + shared
     copies = [
         pltpu.make_async_copy(source, held, arrival.at[index])
         for index, (source, held) in enumerate(
@@ -71,7 +77,16 @@
         pieces.append(jnp.sum(before * piece, axis=0, keepdims=True))
         offset = offset + jnp.sum(piece, axis=1, keepdims=True)
     position = jnp.concatenate(pieces, axis=1).astype(jnp.int32)
-    target = part * slots + position
+    counts = offset
+    swapped = []
+    for at in range(0, parts, 2 * mate):
+        swapped += [counts[at + mate : at + 2 * mate], counts[at : at + mate]]
+    free = (jnp.concatenate(swapped, axis=0) <= direct).astype(F32)
+    crowded = jnp.max(jnp.where(counts > room, 1.0 - free, 0.0), axis=0, keepdims=True)
+    mate_free = jnp.sum(onehot * free, axis=0, keepdims=True) > 0.5
+    over = position - room
+    other = jnp.bitwise_xor(part, mate) * room + direct + over
+    target = jnp.where(over < 0, part * room + position, jnp.where(mate_free, other, -1))
 
     coded = dest_slot[...][None, :] + 1
     high = jnp.right_shift(coded, 6)
@@ -93,8 +108,9 @@
             turned = pltpu.roll(digit, lax.rem(base - j * PACK + LANES, LANES), 1)
             turned = jnp.where(mine, turned, 0.0)
             listed = jnp.where(row == at + j, turned[:, None, :], listed)
+    listed = jnp.where(row == FLAG, crowded[None], listed)
     halves = width // LANES
-    packed[:, halves * slots :, :] = listed.astype(BF16)
+    packed[:, halves * room :, :] = listed.astype(BF16)
 
     copies[0].wait()
     copies[1].wait()
@@ -104,35 +120,45 @@
     total = jnp.dot(hidden, w_second[...], preferred_element_type=F32)
     embedded[...] = (total + b_second[...].astype(F32)[None, :]).astype(BF16)
 
-    size = GROUP * slots
+    keep = pltpu.make_async_copy(embedded, embedded_out, leaving.at[parts // GROUP])
+    keep.start()
+    size = GROUP * room
     slot = iota((size, count), 0)
-    sends = []
+    sends = [keep]
     for group in range(parts // GROUP):
         select = (slot == target - group * size).astype(BF16)
-        moved = jnp.dot(select, embedded[...], preferred_element_type=F32).astype(BF16)
+        moved = jnp.dot(select, embedded[...], preferred_element_type=F32)
         dests = slice(group * GROUP, (group + 1) * GROUP)
+        rest = []
         for half in range(halves):
-            piece = moved[:, half * LANES : (half + 1) * LANES]
-            packed[dests, half * slots : (half + 1) * slots, :] = piece.reshape(
-                GROUP, slots, LANES
-            )
+            piece = moved[:, half * LANES : (half + 1) * LANES].reshape(GROUP, room, LANES)
+            packed[dests, half * direct : (half + 1) * direct, :] = piece[:, :direct].astype(BF16)
+            rest.append(piece[:, direct:])
+        packed[dests, halves * direct : halves * room, :] = jnp.concatenate(rest, axis=1).astype(
+            BF16
+        )
         sends.append(pltpu.make_async_copy(packed.at[dests], out.at[dests], leaving.at[group]))
         sends[-1].start()
     for send in sends:
         send.wait()
 
 
-def project(parts, slots, features, w_first, b_first, w_second, b_second, part, slot, lane_base):
+def project(
+    parts, mate, sizes, features, w_first, b_first, w_second, b_second, part, slot, lane_base
+):
     rows, depth = features.shape
     hidden, width = w_second.shape
-    length = (width // LANES) * slots + PACK
+    length = (width // LANES) * sum(sizes) + PACK
     vmem = pl.BlockSpec(memory_space=pltpu.VMEM)
     hbm = pl.BlockSpec(memory_space=pl.ANY)
     return pl.pallas_call(
-        functools.partial(project_kernel, parts, slots),
-        out_shape=jax.ShapeDtypeStruct((parts, length, LANES), BF16),
+        functools.partial(project_kernel, parts, mate, sizes),
+        out_shape=[
+            jax.ShapeDtypeStruct((parts, length, LANES), BF16),
+            jax.ShapeDtypeStruct((rows, width), BF16),
+        ],
         in_specs=[hbm, hbm, vmem, hbm, vmem, vmem, vmem, pl.BlockSpec(memory_space=pltpu.SMEM)],
-        out_specs=hbm,
+        out_specs=[hbm, hbm],
         scratch_shapes=[
             pltpu.VMEM((rows, depth), BF16),
             pltpu.VMEM((depth, hidden), BF16),
@@ -140,7 +166,7 @@
             pltpu.VMEM((rows, width), BF16),
             pltpu.VMEM((parts, length, LANES), BF16),
             pltpu.SemaphoreType.DMA((3,)),
-            pltpu.SemaphoreType.DMA((parts // GROUP,)),
+            pltpu.SemaphoreType.DMA((parts // GROUP + 1,)),
         ],
         compiler_params=pltpu.CompilerParams(vmem_limit_bytes=PROJECT_VMEM),
         cost_estimate=pl.CostEstimate(
@@ -150,24 +176,36 @@
     )(features, w_first, b_first, w_second, b_second, part, slot, lane_base)
 
 
-def arrived_rows(slots, halves, arrived):
+def arrived_rows(sizes, halves, arrived, extra):
+    direct, shared = sizes
+    room = direct + shared
     ids, rows = [], []
     for first in range(0, arrived.shape[0], GROUP):
         sources = slice(first, first + GROUP)
-        listed = jnp.sum(arrived[sources, halves * slots :, :].astype(F32), axis=0)
+        listed = jnp.sum(arrived[sources, halves * room :, :].astype(F32), axis=0)
         coded = (listed[:8] * 64.0 + listed[8:]).astype(jnp.int32)
-        for j in range(slots // PACK):
+        own = arrived[sources, halves * direct : halves * room, :].astype(F32)
+        more = extra[sources].astype(F32)
+        rest = []
+        for half in range(halves):
+            part = slice(half * shared, (half + 1) * shared)
+            rest.append(jnp.concatenate([own[:, part], more[:, part]], axis=1).astype(BF16))
+        for j in range((room + shared) // PACK):
             ids.append(coded[j : j + 1, :] - 1)
             pieces = []
             for half in range(halves):
-                at = half * slots + j * PACK
-                pieces.append(arrived[sources, at : at + PACK, :].reshape(LANES, LANES))
+                at = j * PACK
+                if at < direct:
+                    piece = arrived[sources, half * direct + at : half * direct + at + PACK, :]
+                else:
+                    piece = rest[half][:, at - direct : at - direct + PACK, :]
+                pieces.append(piece.reshape(LANES, LANES))
             rows.append(jnp.concatenate(pieces, axis=1))
     return jnp.concatenate(ids, axis=1), jnp.concatenate(rows, axis=0)
 
 
-def listed_kernel(slots, halves, arrived, halo_send, *sends):
-    ids, rows = arrived_rows(slots, halves, arrived)
+def listed_kernel(sizes, halves, arrived, extra, halo_send, *sends):
+    ids, rows = arrived_rows(sizes, halves, arrived, extra)
     _, listed, block_rows, _ = sends[0].shape
     slot = iota((block_rows, ids.shape[1]), 0)
     several = 4
@@ -183,8 +221,8 @@
                 send[side, first : first + several] = piece.reshape(several, block_rows, LANES)
 
 
-def place_kernel(slots, halves, arrived, size, *starts):
-    ids, rows = arrived_rows(slots, halves, arrived)
+def place_kernel(sizes, halves, arrived, extra, size, *starts):
+    ids, rows = arrived_rows(sizes, halves, arrived, extra)
     size[0] = jnp.sum((ids >= 0).astype(jnp.int32))
     block_count, block_rows, _ = starts[0].shape
     several = 4
@@ -205,13 +243,13 @@
     return pl.BlockSpec(memory_space=pltpu.SMEM)
 
 
-def listed_blocks(slots, halves, block_rows, arrived, halo_send):
+def listed_blocks(sizes, halves, block_rows, arrived, extra, halo_send):
     listed = halo_send.shape[1]
-    depth = arrived.shape[0] * slots
+    depth = arrived.shape[0] * (sizes[0] + 2 * sizes[1])
     return pl.pallas_call(
-        functools.partial(listed_kernel, slots, halves),
+        functools.partial(listed_kernel, sizes, halves),
         out_shape=[jax.ShapeDtypeStruct((2, listed, block_rows, LANES), BF16)] * halves,
-        in_specs=[vmem_spec(), smem_spec()],
+        in_specs=[vmem_spec(), vmem_spec(), smem_spec()],
         out_specs=[vmem_spec()] * halves,
         compiler_params=pltpu.CompilerParams(vmem_limit_bytes=VMEM_LIMIT),
         cost_estimate=pl.CostEstimate(
@@ -220,16 +258,16 @@
             transcendentals=0,
         ),
         name="listed",
-    )(arrived, halo_send)
-
-
-def place(slots, halves, block_count, block_rows, arrived):
-    depth = arrived.shape[0] * slots
+    )(arrived, extra, halo_send)
+
+
+def place(sizes, halves, block_count, block_rows, arrived, extra):
+    depth = arrived.shape[0] * (sizes[0] + 2 * sizes[1])
     return pl.pallas_call(
-        functools.partial(place_kernel, slots, halves),
+        functools.partial(place_kernel, sizes, halves),
         out_shape=[jax.ShapeDtypeStruct((1,), jnp.int32)]
         + [jax.ShapeDtypeStruct((block_count, block_rows, LANES), BF16)] * halves,
-        in_specs=[vmem_spec()],
+        in_specs=[vmem_spec()] * 2,
         out_specs=[smem_spec()] + [vmem_spec()] * halves,
         compiler_params=pltpu.CompilerParams(vmem_limit_bytes=VMEM_LIMIT),
         cost_estimate=pl.CostEstimate(
@@ -238,7 +276,7 @@
             transcendentals=0,
         ),
         name="place",
-    )(arrived)
+    )(arrived, extra)
 
 
 def inner_kernel(halo, tiles, coords, start, current, partial):
@@ -348,6 +386,26 @@
     )(*operands)
 
 
+def all_to_all(payload):
+    return lax.all_to_all(payload, ("dp", "dom"), split_axis=0, concat_axis=0, tiled=True)
+
+
+def late_rows(parts, sizes, embedded, dest_part):
+    direct, shared = sizes
+    count, width = embedded.shape
+    onehot = (dest_part[:, None] == jnp.arange(parts, dtype=jnp.int32)[None, :]).astype(BF16)
+    row = jnp.arange(count, dtype=jnp.int32)
+    earlier = (row[None, :] < row[:, None]).astype(BF16)
+    before = jnp.dot(earlier, onehot, preferred_element_type=F32)
+    position = jnp.sum(before * onehot.astype(F32), axis=1).astype(jnp.int32)
+    over = position - (direct + shared)
+    target = jnp.where(over < 0, -1, dest_part * shared + over)
+    select = (jnp.arange(parts * shared, dtype=jnp.int32)[:, None] == target[None, :]).astype(BF16)
+    moved = jnp.dot(select, embedded, preferred_element_type=F32).astype(BF16)
+    moved = moved.reshape(parts, shared, width // LANES, LANES)
+    return jnp.swapaxes(moved, 1, 2).reshape(parts, width // LANES * shared, LANES)
+
+
 def local(
     features,
     w_first,
@@ -365,17 +423,41 @@
     parts = count_dp * count_dom
     row_count = features.shape[0]
     capacity = 3 * row_count
-    slots = -(-capacity // parts // PACK) * PACK
+    most = -(-capacity // parts)
+    direct = -(-most // (2 * PACK)) * PACK
+    shared = max(-(-(most - direct) // 16) * 8, 8)
+    sizes = direct, shared
     width = w_second.shape[1]
     halves = width // LANES
     block_rows = tile_values.shape[1]
     block_count = capacity // block_rows
     me = lax.axis_index("dp") * count_dom + lax.axis_index("dom")
     lane_base = (lax.rem(me, GROUP) * PACK).astype(jnp.int32).reshape(1)
-    outgoing = project(
-        parts, slots, features, w_first, b_first, w_second, b_second, dest_part, dest_slot, lane_base
+    outgoing, embedded = project(
+        parts,
+        count_dom,
+        sizes,
+        features,
+        w_first,
+        b_first,
+        w_second,
+        b_second,
+        dest_part,
+        dest_slot,
+        lane_base,
     )
-    arrived = lax.all_to_all(outgoing, ("dp", "dom"), split_axis=0, concat_axis=0, tiled=True)
+    arrived = all_to_all(outgoing)
+    crowded = jnp.any(arrived[:, halves * sum(sizes) + FLAG, :] > 0.5)
+    from_mate = lax.ppermute(
+        arrived[:, halves * direct : halves * sum(sizes), :],
+        "dp",
+        [(i, i ^ 1) for i in range(count_dp)],
+    )
+    extra = lax.cond(
+        crowded,
+        lambda: all_to_all(late_rows(parts, sizes, embedded, dest_part)),
+        lambda: from_mate,
+    )
     coords = tile_coords.reshape(-1)
     lists = halo_send[0]
     forward = [(i, (i + 1) % count_dom) for i in range(count_dom)]
@@ -385,9 +467,9 @@
         return lax.ppermute(send[0], "dom", forward), lax.ppermute(send[1], "dom", backward)
 
     halos = [
-        exchange(send) for send in listed_blocks(slots, halves, block_rows, arrived, lists)
+        exchange(send) for send in listed_blocks(sizes, halves, block_rows, arrived, extra, lists)
     ]
-    size, *starts = place(slots, halves, block_count, block_rows, arrived)
+    size, *starts = place(sizes, halves, block_count, block_rows, arrived, extra)
     fields = list(starts)
     held = None
     for repeat in range(HOPS):

time: 115 us -> 109 us (0.948)
  waiting for transfers between devices: 54.2 us -> 13 us
  blocking collectives: 0 us -> 40.5 us
  starting transfers between devices: 26.3 us -> 19.1 us
    all_to_all x1 -> x0, waiting for transfers between devices: 41.4 us -> none  [local(): lax.all_to_all(outgoing, ('dp', 'dom'), split_axis=0, concat_axis=0, tile...]
    all_to_all x0 -> x1, blocking collectives: none -> 40.5 us  [all_to_all(): lax.all_to_all(payload, ('dp', 'dom'), split_axis=0, concat_axis=0, tiled...]
    all_to_all x1 -> x0, starting transfers between devices: 7.28 us -> none  [local(): lax.all_to_all(outgoing, ('dp', 'dom'), split_axis=0, concat_axis=0, tile...]
  transfers between devices with their start and end apart: 9 -> 9, of which waited for: 6 -> 6; matrix products, arithmetic and copies ran while one was open for 0% -> 1% of each run, Pallas kernels for 14% -> 15%
where the time goes in v2:
time: 109 us
  blocking collectives  40.5 us (37%)
  Pallas kernels  33.5 us (31%)
  starting transfers between devices  19.1 us (18%)
  waiting for transfers between devices  13 us (12%)
    all_to_all x1, blocking collectives, all_to_all(): lax.all_to_all(payload, ('dp', 'dom'), split_axis=0, concat_axis=0, tiled...  40.5 us
    ppermute x4, starting transfers between devices, exchange(): lax.ppermute(send[1], 'dom', backward)  17.8 us
    pallas_call x1, Pallas kernels, project(): pl.pallas_call(functools.partial(project_kernel, parts, mate, sizes), out...  10 us
    pallas_call x4, Pallas kernels, outer(): pl.pallas_call(functools.partial(outer_kernel, last), out_shape=out_shape...  9.82 us
    ppermute x4, waiting for transfers between devices, exchange(): lax.ppermute(send[1], 'dom', backward)  9.53 us
    pallas_call x1, Pallas kernels, place(): pl.pallas_call(functools.partial(place_kernel, sizes, halves), out_shape=...  5.5 us
    pallas_call x4, Pallas kernels, inner(): pl.pallas_call(functools.partial(inner_kernel, halo), out_shape=jax.Shape...  4.15 us
    pallas_call x1, Pallas kernels, listed_blocks(): pl.pallas_call(functools.partial(listed_kernel, sizes, halves), out_shape...  3.95 us
  transfers between devices with their start and end apart: 9, of which 6 were waited for; matrix products, arithmetic and copies ran while one was open for 1% of the time, Pallas kernels for 15%

profile of v2, /device:TPU:0, one launch (start us, length us, event | category | flops | bytes accessed | tf_op | source)
XLA Modules:
  0.0 108.5 jit_solution(16874527061001134423)
XLA Ops:
  0.0 10.0 %project.1 = (bf16[32,160,128]{2,1,0:T(8,128)(2,1)}, bf16[1024,256]{1,0:T(8,128)(2,1)S(1)}) custom-call(bf16[1024,1024]{1,0:T(8,128)(2,1)} %features_hbm.1, bf16[1024,1024]{1,0:T(8,128)(2,1)} %w_first_hbm.1, bf16[1024]{0:T(1024)(128)(2,1)} %b_first.1, bf16[1024,256]{1,0:T(8,128)(2,1)} %w_second_hbm.1, bf16[256]{0:T(256)(128)(2,1)} %b_second.1, ...), custom_call_target="tpu_custom_call" | custom-call | flops 2684354560 | bytes 8388608 | tf_op jit(solution)/shard_map/project/pallas_call | solution.py:154
  10.0 0.0 copy-start.3
  10.1 0.0 copy-start.2
  10.1 40.5 %all_to_all.10.arrived = bf16[32,160,128]{2,1,0:T(8,128)(2,1)S(1)} all-to-all(bf16[32,160,128]{2,1,0:T(8,128)(2,1)} %get-tuple-element.26), channel_id=1, replica_groups=mesh['dp'=4,'dom'=8] {'dp','dom'}, dimensions={0} | all-to-all | bytes 2621440 | tf_op jit(solution)/shard_map/all_to_all | solution.py:390
  50.6 0.1 collective-permute-start
  50.7 0.0 copy-done.3
  50.7 0.1 copy.15
  50.8 0.1 reshape.16.coords.refs_1_
  50.9 0.7 compare_reduce_fusion
  52.2 0.0 copy-done.2
  52.2 0.0 copy-start.1
  52.3 0.1 collective-permute-done
  52.4 0.5 copy-done.1
  52.9 4.0 %listed.1 = (bf16[2,8,128,128]{3,2,1,0:T(8,128)(2,1)S(1)}, bf16[2,8,128,128]{3,2,1,0:T(8,128)(2,1)S(1)}) custom-call(bf16[32,160,128]{2,1,0:T(8,128)(2,1)S(1)} %all_to_all.10.arrived, bf16[32,48,128]{2,1,0:T(8,128)(2,1)S(1)} %get-tuple-element.45.extra, s32[2,8]{1,0:T(2,128)S(1)} %bitcast.21), custom_call_target="tpu_custom_call" | custom-call | flops 3221225472 | bytes 4194304 | tf_op jit(solution)/shard_map/listed/pallas_call | solution.py:249
  56.9 1.1 %collective-permute-start.5 = (bf16[8,128,128]{2,1,0:T(8,128)(2,1)S(1)}, bf16[8,128,128]{2,1,0:T(8,128)(2,1)S(1)}, u32[]{:S(2)}, u32[]{:S(2)}) collective-permute-start(bf16[8,128,128]{2,1,0:T(8,128)(2,1)S(1)} %get-tuple-element.40), channel_id=1, source_target_pairs={{0,1},{1,2},{2,3},{3,4},{4,5},{5,6},{6,7},{7,0},{8,9},{9,10},{10,1... | collective-permute-start | bytes 786440 | tf_op jit(solution)/shard_map/ppermute | solution.py:467
  58.1 3.7 %collective-permute-start.6 = (bf16[8,128,128]{2,1,0:T(8,128)(2,1)S(1)}, bf16[8,128,128]{2,1,0:T(8,128)(2,1)S(1)}, u32[]{:S(2)}, u32[]{:S(2)}) collective-permute-start(bf16[8,128,128]{2,1,0:T(8,128)(2,1)S(1)} %get-tuple-element.39), channel_id=1, source_target_pairs={{1,0},{2,1},{3,2},{4,3},{5,4},{6,5},{7,6},{0,7},{9,8},{10,9},{11,1... | collective-permute-start | bytes 786440 | tf_op jit(solution)/shard_map/ppermute | solution.py:467
  61.8 0.1 collective-permute-start.1
  61.8 0.0 copy-start
  61.8 4.7 %collective-permute-start.2 = (bf16[8,128,128]{2,1,0:T(8,128)(2,1)S(1)}, bf16[8,128,128]{2,1,0:T(8,128)(2,1)S(1)}, u32[]{:S(2)}, u32[]{:S(2)}) collective-permute-start(bf16[8,128,128]{2,1,0:T(8,128)(2,1)S(1)} %get-tuple-element.43), channel_id=1, source_target_pairs={{1,0},{2,1},{3,2},{4,3},{5,4},{6,5},{7,6},{0,7},{9,8},{10,9},{11,1... | collective-permute-start | bytes 786440 | tf_op jit(solution)/shard_map/ppermute | solution.py:467
  66.5 5.5 %place.1 = (s32[1]{0:T(128)}, bf16[24,128,128]{2,1,0:T(8,128)(2,1)S(1)}, bf16[24,128,128]{2,1,0:T(8,128)(2,1)S(1)}) custom-call(bf16[32,160,128]{2,1,0:T(8,128)(2,1)S(1)} %all_to_all.10.arrived, bf16[32,48,128]{2,1,0:T(8,128)(2,1)S(1)} %get-tuple-element.45.extra), custom_call_target="tpu_custom_call" | custom-call | flops 4831838208 | bytes 4194304 | tf_op jit(solution)/shard_map/place/pallas_call | solution.py:266
  72.0 0.0 copy-done
  72.0 1.0 inner.6.refs_4_
  73.1 1.0 inner.4.refs_4_
  74.1 1.8 %collective-permute-done.5.refs_5_ = bf16[8,128,128]{2,1,0:T(8,128)(2,1)S(1)} collective-permute-done((bf16[8,128,128]{2,1,0:T(8,128)(2,1)S(1)}, bf16[8,128,128]{2,1,0:T(8,128)(2,1)S(1)}, u32[]{:S(2)}, u32[]{:S(2)}) %collective-permute-start.5) | collective-permute-done | bytes 262176 | tf_op jit(solution)/shard_map/ppermute | solution.py:467
  75.9 2.5 %collective-permute-done.6.refs_6_ = bf16[8,128,128]{2,1,0:T(8,128)(2,1)S(1)} collective-permute-done((bf16[8,128,128]{2,1,0:T(8,128)(2,1)S(1)}, bf16[8,128,128]{2,1,0:T(8,128)(2,1)S(1)}, u32[]{:S(2)}, u32[]{:S(2)}) %collective-permute-start.6) | collective-permute-done | bytes 262176 | tf_op jit(solution)/shard_map/ppermute | solution.py:467
  78.4 2.0 %outer.5 = (bf16[24,128,128]{2,1,0:T(8,128)(2,1)S(1)}, bf16[2,8,128,128]{3,2,1,0:T(8,128)(2,1)S(1)}) custom-call(bf16[48,128,128]{2,1,0:T(8,128)(2,1)S(1)} %copy-done, s32[96]{0:T(128)S(1)} %reshape.16.coords.refs_1_, s32[2,8]{1,0:T(2,128)S(1)} %bitcast.22, s32[1]{0:T(128)} %get-tuple-element.28.refs_3_, f32[24,128,128]{2,1,0:T(8,128)S(1)} %inner.6.refs_4_, ...), custom_call_target="tpu_custom_call" | custom-call | flops 100663296 | bytes 4194304 | tf_op jit(solution)/shard_map/outer/pallas_call | solution.py:373
  80.5 0.1 collective-permute-start.7
  80.6 4.7 %collective-permute-start.8 = (bf16[8,128,128]{2,1,0:T(8,128)(2,1)S(1)}, bf16[8,128,128]{2,1,0:T(8,128)(2,1)S(1)}, u32[]{:S(2)}, u32[]{:S(2)}) collective-permute-start(bf16[8,128,128]{2,1,0:T(8,128)(2,1)S(1)} %get-tuple-element.37), channel_id=1, source_target_pairs={{1,0},{2,1},{3,2},{4,3},{5,4},{6,5},{7,6},{0,7},{9,8},{10,9},{11,1... | collective-permute-start | bytes 786440 | tf_op jit(solution)/shard_map/ppermute | solution.py:467
  85.3 0.0 collective-permute-done.1.refs_5_
  85.3 0.0 collective-permute-done.2.refs_6_
  85.3 2.0 %outer.4 = (bf16[24,128,128]{2,1,0:T(8,128)(2,1)S(1)}, bf16[2,8,128,128]{3,2,1,0:T(8,128)(2,1)S(1)}) custom-call(bf16[48,128,128]{2,1,0:T(8,128)(2,1)S(1)} %copy-done, s32[96]{0:T(128)S(1)} %reshape.16.coords.refs_1_, s32[2,8]{1,0:T(2,128)S(1)} %bitcast.23, s32[1]{0:T(128)} %get-tuple-element.28.refs_3_, f32[24,128,128]{2,1,0:T(8,128)S(1)} %inner.4.refs_4_, ...), custom_call_target="tpu_custom_call" | custom-call | flops 100663296 | bytes 4194304 | tf_op jit(solution)/shard_map/outer/pallas_call | solution.py:373
  87.4 0.1 collective-permute-start.3
  87.5 4.7 %collective-permute-start.4 = (bf16[8,128,128]{2,1,0:T(8,128)(2,1)S(1)}, bf16[8,128,128]{2,1,0:T(8,128)(2,1)S(1)}, u32[]{:S(2)}, u32[]{:S(2)}) collective-permute-start(bf16[8,128,128]{2,1,0:T(8,128)(2,1)S(1)} %get-tuple-element.41), channel_id=1, source_target_pairs={{1,0},{2,1},{3,2},{4,3},{5,4},{6,5},{7,6},{0,7},{9,8},{10,9},{11,1... | collective-permute-start | bytes 786440 | tf_op jit(solution)/shard_map/ppermute | solution.py:467
  92.2 1.1 inner.7.refs_4_
  93.2 1.0 inner.5.refs_4_
  94.3 1.5 %collective-permute-done.7.refs_5_ = bf16[8,128,128]{2,1,0:T(8,128)(2,1)S(1)} collective-permute-done((bf16[8,128,128]{2,1,0:T(8,128)(2,1)S(1)}, bf16[8,128,128]{2,1,0:T(8,128)(2,1)S(1)}, u32[]{:S(2)}, u32[]{:S(2)}) %collective-permute-start.7) | collective-permute-done | bytes 262176 | tf_op jit(solution)/shard_map/ppermute | solution.py:467
  95.8 5.4 %collective-permute-done.8.refs_6_ = bf16[8,128,128]{2,1,0:T(8,128)(2,1)S(1)} collective-permute-done((bf16[8,128,128]{2,1,0:T(8,128)(2,1)S(1)}, bf16[8,128,128]{2,1,0:T(8,128)(2,1)S(1)}, u32[]{:S(2)}, u32[]{:S(2)}) %collective-permute-start.8) | collective-permute-done | bytes 262176 | tf_op jit(solution)/shard_map/ppermute | solution.py:467
  101.1 2.9 %outer.6.refs_7_ = bf16[3072,256]{1,0:T(8,128)(2,1)} custom-call(bf16[48,128,128]{2,1,0:T(8,128)(2,1)S(1)} %copy-done, s32[96]{0:T(128)S(1)} %reshape.16.coords.refs_1_, s32[2,8]{1,0:T(2,128)S(1)} %bitcast.24, s32[1]{0:T(128)} %get-tuple-element.28.refs_3_, f32[24,128,128]{2,1,0:T(8,128)S(1)} %inner.7.refs_4_, ...), custom_call_target="tpu_custom_call" | custom-call | flops 100663296 | bytes 4194304 | tf_op jit(solution)/shard_map/outer/pallas_call | solution.py:373
  104.0 0.0 collective-permute-done.3.refs_5_
  104.0 1.6 %collective-permute-done.4.refs_6_ = bf16[8,128,128]{2,1,0:T(8,128)(2,1)S(1)} collective-permute-done((bf16[8,128,128]{2,1,0:T(8,128)(2,1)S(1)}, bf16[8,128,128]{2,1,0:T(8,128)(2,1)S(1)}, u32[]{:S(2)}, u32[]{:S(2)}) %collective-permute-start.4) | collective-permute-done | bytes 262176 | tf_op jit(solution)/shard_map/ppermute | solution.py:467
  105.7 2.9 %outer.7 = bf16[3072,256]{1,0:T(8,128)(2,1)} custom-call(bf16[48,128,128]{2,1,0:T(8,128)(2,1)S(1)} %copy-done, s32[96]{0:T(128)S(1)} %reshape.16.coords.refs_1_, s32[2,8]{1,0:T(2,128)S(1)} %bitcast.25, s32[1]{0:T(128)} %get-tuple-element.28.refs_3_, f32[24,128,128]{2,1,0:T(8,128)S(1)} %inner.5.refs_4_, ...), custom_call_target="tpu_custom_call", output_to_operand_aliasing={{}: (7, {})} | custom-call | flops 100663296 | bytes 4194304 | tf_op jit(solution)/shard_map/outer/pallas_call | solution.py:373
  (6 shorter events, 0.2 us)
Async XLA Ops:
  10.0 40.6 %copy-start.3 = (s32[48,2]{0,1:T(2,128)S(1)}, s32[48,2]{0,1:T(2,128)}, u32[]{:S(2)}) copy-start(s32[48,2]{0,1:T(2,128)} %param.19) | copy-start | bytes 1156
  10.1 42.2 %copy-start.2 = (s32[1024]{0:T(1024)S(1)}, s32[1024]{0:T(1024)}, u32[]{:S(2)}) copy-start(s32[1024]{0:T(1024)} %dest_part.1) | copy-start | bytes 12292
  50.6 1.8 %collective-permute-start = (bf16[32,48,128]{2,1,0:T(8,128)(2,1)S(1)}, bf16[32,48,128]{2,1,0:T(8,128)(2,1)S(1)}, u32[]{:S(2)}, u32[]{:S(2)}) collective-permute-start(bf16[32,48,128]{2,1,0:T(8,128)(2,1)S(1)} %slice.41), channel_id=1, source_target_pairs={{0,8},{8,0},{16,24},{24,16},{1,9},{9,1},{17,25},{25,17},{2,10},{10... | collective-permute-start | bytes 1179656 | tf_op jit(solution)/shard_map/ppermute | solution.py:451
  52.2 0.7 copy-start.1
  56.9 19.0 %collective-permute-start.5 = (bf16[8,128,128]{2,1,0:T(8,128)(2,1)S(1)}, bf16[8,128,128]{2,1,0:T(8,128)(2,1)S(1)}, u32[]{:S(2)}, u32[]{:S(2)}) collective-permute-start(bf16[8,128,128]{2,1,0:T(8,128)(2,1)S(1)} %get-tuple-element.40), channel_id=1, source_target_pairs={{0,1},{1,2},{2,3},{3,4},{4,5},{5,6},{6,7},{7,0},{8,9},{9,10},{10,1... | collective-permute-start | bytes 786440 | tf_op jit(solution)/shard_map/ppermute | solution.py:467
  58.1 20.4 %collective-permute-start.6 = (bf16[8,128,128]{2,1,0:T(8,128)(2,1)S(1)}, bf16[8,128,128]{2,1,0:T(8,128)(2,1)S(1)}, u32[]{:S(2)}, u32[]{:S(2)}) collective-permute-start(bf16[8,128,128]{2,1,0:T(8,128)(2,1)S(1)} %get-tuple-element.39), channel_id=1, source_target_pairs={{1,0},{2,1},{3,2},{4,3},{5,4},{6,5},{7,6},{0,7},{9,8},{10,9},{11,1... | collective-permute-start | bytes 786440 | tf_op jit(solution)/shard_map/ppermute | solution.py:467
  61.8 23.6 %collective-permute-start.1 = (bf16[8,128,128]{2,1,0:T(8,128)(2,1)S(1)}, bf16[8,128,128]{2,1,0:T(8,128)(2,1)S(1)}, u32[]{:S(2)}, u32[]{:S(2)}) collective-permute-start(bf16[8,128,128]{2,1,0:T(8,128)(2,1)S(1)} %get-tuple-element.44), channel_id=1, source_target_pairs={{0,1},{1,2},{2,3},{3,4},{4,5},{5,6},{6,7},{7,0},{8,9},{9,10},{10,1... | collective-permute-start | bytes 786440 | tf_op jit(solution)/shard_map/ppermute | solution.py:467
  61.8 10.2 %copy-start = (bf16[48,128,128]{2,1,0:T(8,128)(2,1)S(1)}, bf16[48,128,128]{2,1,0:T(8,128)(2,1)}, u32[]{:S(2)}) copy-start(bf16[48,128,128]{2,1,0:T(8,128)(2,1)} %refs_0_.7) | copy-start | bytes 4718596
  61.8 23.5 %collective-permute-start.2 = (bf16[8,128,128]{2,1,0:T(8,128)(2,1)S(1)}, bf16[8,128,128]{2,1,0:T(8,128)(2,1)S(1)}, u32[]{:S(2)}, u32[]{:S(2)}) collective-permute-start(bf16[8,128,128]{2,1,0:T(8,128)(2,1)S(1)} %get-tuple-element.43), channel_id=1, source_target_pairs={{1,0},{2,1},{3,2},{4,3},{5,4},{6,5},{7,6},{0,7},{9,8},{10,9},{11,1... | collective-permute-start | bytes 786440 | tf_op jit(solution)/shard_map/ppermute | solution.py:467
  80.5 15.2 %collective-permute-start.7 = (bf16[8,128,128]{2,1,0:T(8,128)(2,1)S(1)}, bf16[8,128,128]{2,1,0:T(8,128)(2,1)S(1)}, u32[]{:S(2)}, u32[]{:S(2)}) collective-permute-start(bf16[8,128,128]{2,1,0:T(8,128)(2,1)S(1)} %get-tuple-element.38), channel_id=1, source_target_pairs={{0,1},{1,2},{2,3},{3,4},{4,5},{5,6},{6,7},{7,0},{8,9},{9,10},{10,1... | collective-permute-start | bytes 786440 | tf_op jit(solution)/shard_map/ppermute | solution.py:467
  80.6 20.5 %collective-permute-start.8 = (bf16[8,128,128]{2,1,0:T(8,128)(2,1)S(1)}, bf16[8,128,128]{2,1,0:T(8,128)(2,1)S(1)}, u32[]{:S(2)}, u32[]{:S(2)}) collective-permute-start(bf16[8,128,128]{2,1,0:T(8,128)(2,1)S(1)} %get-tuple-element.37), channel_id=1, source_target_pairs={{1,0},{2,1},{3,2},{4,3},{5,4},{6,5},{7,6},{0,7},{9,8},{10,9},{11,1... | collective-permute-start | bytes 786440 | tf_op jit(solution)/shard_map/ppermute | solution.py:467
  87.4 16.6 %collective-permute-start.3 = (bf16[8,128,128]{2,1,0:T(8,128)(2,1)S(1)}, bf16[8,128,128]{2,1,0:T(8,128)(2,1)S(1)}, u32[]{:S(2)}, u32[]{:S(2)}) collective-permute-start(bf16[8,128,128]{2,1,0:T(8,128)(2,1)S(1)} %get-tuple-element.42), channel_id=1, source_target_pairs={{0,1},{1,2},{2,3},{3,4},{4,5},{5,6},{6,7},{7,0},{8,9},{9,10},{10,1... | collective-permute-start | bytes 786440 | tf_op jit(solution)/shard_map/ppermute | solution.py:467
  87.5 18.2 %collective-permute-start.4 = (bf16[8,128,128]{2,1,0:T(8,128)(2,1)S(1)}, bf16[8,128,128]{2,1,0:T(8,128)(2,1)S(1)}, u32[]{:S(2)}, u32[]{:S(2)}) collective-permute-start(bf16[8,128,128]{2,1,0:T(8,128)(2,1)S(1)} %get-tuple-element.41), channel_id=1, source_target_pairs={{1,0},{2,1},{3,2},{4,3},{5,4},{6,5},{7,6},{0,7},{9,8},{10,9},{11,1... | collective-permute-start | bytes 786440 | tf_op jit(solution)/shard_map/ppermute | solution.py:467

commit v3 on v2

v3 whole, which is shorter than its diff:
```python
import functools

import jax
import jax.numpy as jnp
from jax import lax
from jax.experimental import pallas as pl
from jax.experimental.pallas import tpu as pltpu
from jax.sharding import PartitionSpec as P

HOPS = 2
ALPHA = 0.1
LANES = 128
PIECE = 8
GROUP = LANES // PIECE
DESTS = 8
FLAG = LANES - 1
POWERS = 16, 8, 4, 2, 1
OUT_BLOCKS = 6
VMEM_LIMIT = 48 * 1024 * 1024
PROJECT_VMEM = 62 * 1024 * 1024

BF16 = jnp.bfloat16
F32 = jnp.float32


def iota(shape, dim):
    return lax.broadcasted_iota(jnp.int32, shape, dim)


def gelu(value):
    return 0.5 * value * (1.0 + lax.erf(value * (0.5**0.5)))


def project_kernel(parts, mate, sizes, *refs):
    given, (out, embedded_out) = refs[:7], refs[7:9]
    held = refs[9:16]
    features, w_first, dest_part, dest_slot, b_first, w_second, b_second = held
    embedded, packed, arrival, leaving = refs[16:]
    room, direct, aligned = sizes
    own = room - 1
    copies = [
        pltpu.make_async_copy(source, kept, arrival.at[index])
        for index, (source, kept) in enumerate(zip(given, held))
    ]
    for index in (2, 3, 0, 1, 4, 5, 6):
        copies[index].start()
    copies[2].wait()
    copies[3].wait()
    width = w_second.shape[1]
    count = dest_part.shape[0]
    part = dest_part[...][None, :]
    onehot = (iota((parts, count), 0) == part).astype(F32)
    blocks = [onehot[:, at : at + LANES] for at in range(0, count, LANES)]
    earlier = (iota((LANES, LANES), 0) < iota((LANES, LANES), 1)).astype(BF16)
    within = jnp.dot(
        jnp.concatenate(blocks, axis=0).astype(BF16), earlier, preferred_element_type=F32
    )
    offset = jnp.zeros((parts, 1), F32)
    pieces = []
    for index, piece in enumerate(blocks):
        before = within[index * parts : (index + 1) * parts, :] + offset
        pieces.append(jnp.sum(before * piece, axis=0, keepdims=True))
        offset = offset + jnp.sum(piece, axis=1, keepdims=True)
    position = jnp.concatenate(pieces, axis=1).astype(jnp.int32)
    counts = offset
    swapped = []
    for at in range(0, parts, 2 * mate):
        swapped += [counts[at + mate : at + 2 * mate], counts[at : at + mate]]
    free = (jnp.concatenate(swapped, axis=0) <= direct).astype(F32)
    crowded = jnp.max(jnp.where(counts > own, 1.0 - free, 0.0), axis=0, keepdims=True)
    mate_free = jnp.sum(onehot * free, axis=0, keepdims=True) > 0.5
    over = position - own
    other = jnp.bitwise_xor(part, mate) * room + direct + over
    target = jnp.where(over < 0, part * room + position, jnp.where(mate_free, other, -1))

    slot = dest_slot[...][None, :]
    power = jnp.right_shift(slot, 7)
    code = (slot - power * 128 + 128).astype(F32)
    for bit in POWERS:
        code = jnp.where(jnp.bitwise_and(power, bit) > 0, code * 2.0**bit, code)
    place_of = jnp.where(over < 0, position, room + direct - aligned + over)
    spot = (iota((LANES, count), 0) == place_of).astype(BF16)
    coded = lax.dot_general(
        (onehot * code).astype(BF16), spot, (((1,), (1,)), ((), ())), preferred_element_type=F32
    )
    coded = jnp.where(iota((parts, LANES), 1) == FLAG, crowded, coded)

    copies[0].wait()
    copies[1].wait()
    copies[4].wait()
    hidden = jnp.dot(features[...], w_first[...], preferred_element_type=F32)
    hidden = gelu(hidden + b_first[...].astype(F32)[None, :]).astype(BF16)
    copies[5].wait()
    copies[6].wait()
    total = jnp.dot(hidden, w_second[...], preferred_element_type=F32)
    embedded[...] = (total + b_second[...].astype(F32)[None, :]).astype(BF16)

    keep = pltpu.make_async_copy(embedded, embedded_out, leaving.at[parts // DESTS])
    keep.start()
    size = DESTS * room
    halves = width // LANES
    slot = iota((size, count), 0)
    last = iota((DESTS, room, LANES), 1) == own
    sends = [keep]
    for group in range(parts // DESTS):
        select = (slot == target - group * size).astype(BF16)
        moved = jnp.dot(select, embedded[...], preferred_element_type=F32)
        dests = slice(group * DESTS, (group + 1) * DESTS)
        head, tail = [], []
        for half in range(halves):
            piece = moved[:, half * LANES : (half + 1) * LANES].reshape(DESTS, room, LANES)
            if half == 0:
                piece = jnp.where(last, coded[dests][:, None, :], piece)
            head.append(piece[:, :aligned])
            tail.append(piece[:, aligned:])
        packed[dests] = jnp.concatenate(head + tail, axis=1).astype(BF16)
        sends.append(pltpu.make_async_copy(packed.at[dests], out.at[dests], leaving.at[group]))
        sends[-1].start()
    for send in sends:
        send.wait()


def project(
    parts, mate, sizes, features, w_first, b_first, w_second, b_second, part, slot
):
    rows, depth = features.shape
    hidden, width = w_second.shape
    length = (width // LANES) * sizes[0]
    given = features, w_first, part, slot, b_first, w_second, b_second
    hbm = pl.BlockSpec(memory_space=pl.ANY)
    return pl.pallas_call(
        functools.partial(project_kernel, parts, mate, sizes),
        out_shape=[
            jax.ShapeDtypeStruct((parts, length, LANES), BF16),
            jax.ShapeDtypeStruct((rows, width), BF16),
        ],
        in_specs=[hbm] * len(given),
        out_specs=[hbm, hbm],
        scratch_shapes=[pltpu.VMEM(array.shape, array.dtype) for array in given]
        + [
            pltpu.VMEM((rows, width), BF16),
            pltpu.VMEM((parts, length, LANES), BF16),
            pltpu.SemaphoreType.DMA((len(given),)),
            pltpu.SemaphoreType.DMA((parts // DESTS + 1,)),
        ],
        compiler_params=pltpu.CompilerParams(vmem_limit_bytes=PROJECT_VMEM),
        cost_estimate=pl.CostEstimate(
            flops=2 * rows * hidden * (depth + width), bytes_accessed=8 << 20, transcendentals=0
        ),
        name="project",
    )(*given)


def arrived_rows(sizes, halves, arrived, extra):
    room, _, aligned = sizes
    beyond = room - aligned
    main = -(-2 * room // (3 * PIECE)) * PIECE
    parts = arrived.shape[0]
    found = ([], []), ([], [])
    lane = iota((GROUP, LANES), 1) // PIECE
    source = iota((GROUP, LANES), 0)
    for first in range(0, parts, GROUP):
        sources = slice(first, first + GROUP)
        got = arrived[sources].astype(F32)
        more = extra[sources].astype(F32)
        fields = []
        for half in range(halves):
            at = halves * aligned + half * beyond
            fields.append(
                jnp.concatenate(
                    [
                        got[:, half * aligned : (half + 1) * aligned],
                        got[:, at : at + beyond],
                        more[:, half * beyond : (half + 1) * beyond],
                    ],
                    axis=1,
                )
            )
        code = fields[0][:, room - 1, :]
        power = jnp.zeros_like(code)
        for bit in POWERS:
            big = code >= 128.0 * 2.0**bit
            code = jnp.where(big, code * 2.0**-bit, code)
            power = jnp.where(big, power + bit, power)
        code = jnp.where(code >= 128.0, code + 128.0 * power - 128.0, -1.0)
        turned = pltpu.roll(code, 0, 1, stride=PIECE, stride_axis=0)
        for j in range((room + beyond) // PIECE):
            row = jnp.where(lane == lax.rem(source + j, GROUP), turned, 0.0)
            row = jnp.sum(row, axis=0, keepdims=True)
            row = pltpu.roll(row, (LANES - j * PIECE) % LANES, 1)
            rows = [
                field[:, j * PIECE : (j + 1) * PIECE, :].reshape(LANES, LANES) for field in fields
            ]
            ids, kept = found[0 if (j + 1) * PIECE <= main else 1]
            ids.append(row.astype(jnp.int32))
            kept.append(jnp.concatenate(rows, axis=1).astype(BF16))
    return [(jnp.concatenate(ids, axis=1), jnp.concatenate(rows, axis=0)) for ids, rows in found]


def fill(found, refs, blocks_of):
    for turn, (ids, rows) in enumerate(found):

        def write(turn=turn, ids=ids, rows=rows):
            for places, bases in blocks_of(refs[0]):
                block_rows = refs[0].shape[-2]
                slot = iota((block_rows, ids.shape[1]), 0)
                select = [(slot == ids - base * block_rows).astype(BF16) for base in bases]
                placed = jnp.dot(
                    jnp.concatenate(select, axis=0), rows, preferred_element_type=F32
                ).astype(BF16)
                for half, ref in enumerate(refs):
                    piece = placed[:, half * LANES : (half + 1) * LANES]
                    piece = piece.reshape(len(bases), block_rows, LANES)
                    ref[places] = piece if turn == 0 else ref[places] + piece

        if turn == 0:
            write()
        else:
            pl.when(jnp.max(ids) >= 0)(write)


def listed_kernel(sizes, halves, arrived, extra, halo_send, *sends):
    def blocks_of(send):
        for side in range(2):
            for first in range(0, send.shape[1], 4):
                bases = [halo_send[side, k] for k in range(first, first + 4)]
                yield (side, slice(first, first + 4)), bases

    fill(arrived_rows(sizes, halves, arrived, extra), sends, blocks_of)


def place_kernel(sizes, halves, arrived, extra, size, *starts):
    found = arrived_rows(sizes, halves, arrived, extra)
    size[0] = sum(jnp.sum((ids >= 0).astype(jnp.int32)) for ids, _ in found)

    def blocks_of(start):
        for first in range(0, start.shape[0], 4):
            yield slice(first, first + 4), range(first, first + 4)

    fill(found, starts, blocks_of)


def vmem_spec():
    return pl.BlockSpec(memory_space=pltpu.VMEM)


def smem_spec():
    return pl.BlockSpec(memory_space=pltpu.SMEM)


def listed_blocks(sizes, halves, block_rows, arrived, extra, halo_send):
    listed = halo_send.shape[1]
    depth = arrived.shape[0] * (2 * sizes[0] - sizes[2])
    return pl.pallas_call(
        functools.partial(listed_kernel, sizes, halves),
        out_shape=[jax.ShapeDtypeStruct((2, listed, block_rows, LANES), BF16)] * halves,
        in_specs=[vmem_spec(), vmem_spec(), smem_spec()],
        out_specs=[vmem_spec()] * halves,
        compiler_params=pltpu.CompilerParams(vmem_limit_bytes=VMEM_LIMIT),
        cost_estimate=pl.CostEstimate(
            flops=4 * listed * block_rows * depth * halves * LANES,
            bytes_accessed=4 << 20,
            transcendentals=0,
        ),
        name="listed",
    )(arrived, extra, halo_send)


def place(sizes, halves, block_count, block_rows, arrived, extra):
    depth = arrived.shape[0] * (2 * sizes[0] - sizes[2])
    return pl.pallas_call(
        functools.partial(place_kernel, sizes, halves),
        out_shape=[jax.ShapeDtypeStruct((1,), jnp.int32)]
        + [jax.ShapeDtypeStruct((block_count, block_rows, LANES), BF16)] * halves,
        in_specs=[vmem_spec()] * 2,
        out_specs=[smem_spec()] + [vmem_spec()] * halves,
        compiler_params=pltpu.CompilerParams(vmem_limit_bytes=VMEM_LIMIT),
        cost_estimate=pl.CostEstimate(
            flops=2 * block_count * block_rows * depth * halves * LANES,
            bytes_accessed=4 << 20,
            transcendentals=0,
        ),
        name="place",
    )(arrived, extra)


def inner_kernel(halo, tiles, coords, start, current, partial):
    block_count = start.shape[0]
    for b in range(block_count):
        term = jnp.dot(tiles[b], current[b], preferred_element_type=F32)
        partial[b] = (1.0 - ALPHA) * term + ALPHA * start[b].astype(F32)
    for t in range(block_count + 2 * halo, tiles.shape[0]):
        index = coords[2 * t + 1]
        source = current[jnp.minimum(index, block_count - 1)]
        source = jnp.where(index < block_count, source, jnp.zeros_like(source))
        term = jnp.dot(tiles[t], source, preferred_element_type=F32)
        partial[coords[2 * t]] += (1.0 - ALPHA) * term


def outer_kernel(half, *refs):
    tiles, coords, halo_send, size, partial, low, high = refs[:7]
    if half is None:
        out, send, terms, summed = refs[-4:]
    else:
        out, terms, summed, rounded, leaving = refs[-5:]
    block_count, block_rows, width = partial.shape
    listed = low.shape[0]
    own = block_count
    for t in range(own, tiles.shape[0]):
        if t < own + listed:
            source = low[t - own]
        elif t < own + 2 * listed:
            source = high[t - own - listed]
        else:
            index = coords[2 * t + 1]
            below = low[jnp.clip(index - own, 0, listed - 1)]
            above = high[jnp.clip(index - own - listed, 0, listed - 1)]
            source = jnp.where(index < own + listed, below, above)
            source = jnp.where(index < own, jnp.zeros_like(source), source)
        terms[t - own] = jnp.dot(tiles[t], source, preferred_element_type=F32)
    summed[...] = partial[...]
    for t in range(own, tiles.shape[0]):
        summed[coords[2 * t]] += (1.0 - ALPHA) * terms[t - own]
    row = iota((block_rows, width), 0)
    copies = []
    for b in range(block_count):
        mixed = jnp.where(row < size[0] - b * block_rows, summed[b], 0.0).astype(BF16)
        if half is None:
            out[b] = mixed
            continue
        rounded[b * block_rows : (b + 1) * block_rows, :] = mixed
        if (b + 1) % OUT_BLOCKS == 0:
            rows = slice((b + 1 - OUT_BLOCKS) * block_rows, (b + 1) * block_rows)
            columns = slice(half * width, (half + 1) * width)
            copies.append(
                pltpu.make_async_copy(
                    rounded.at[rows], out.at[rows, columns], leaving.at[len(copies)]
                )
            )
            copies[-1].start()
    for copy in copies:
        copy.wait()
    if half is None:
        for side in range(2):
            for k in range(listed):
                send[side, k] = out[halo_send[side, k]]


def inner(halo, tiles, coords, start, current):
    return pl.pallas_call(
        functools.partial(inner_kernel, halo),
        out_shape=jax.ShapeDtypeStruct(start.shape, F32),
        in_specs=[vmem_spec(), smem_spec(), vmem_spec(), vmem_spec()],
        out_specs=vmem_spec(),
        compiler_params=pltpu.CompilerParams(vmem_limit_bytes=VMEM_LIMIT),
        cost_estimate=pl.CostEstimate(
            flops=tiles.size * LANES, bytes_accessed=4 << 20, transcendentals=0
        ),
        name="inner",
    )(tiles, coords, start, current)


def outer(tiles, coords, halo_send, size, partial, low, high, half=None, halves=1, held=None):
    block_count, block_rows, width = partial.shape
    listed = low.shape[0]
    operands = [tiles, coords, halo_send, size, partial, low, high]
    vmem = vmem_spec()
    in_specs = [vmem, smem_spec(), smem_spec(), smem_spec(), vmem, vmem, vmem]
    scratch = [
        pltpu.VMEM((tiles.shape[0] - block_count, block_rows, width), F32),
        pltpu.VMEM((block_count, block_rows, width), F32),
    ]
    aliases = {}
    if half is None:
        out_shape = [
            jax.ShapeDtypeStruct((block_count, block_rows, width), BF16),
            jax.ShapeDtypeStruct((2, listed, block_rows, width), BF16),
        ]
        out_specs = [vmem, vmem]
    else:
        capacity = block_count * block_rows
        out_shape = jax.ShapeDtypeStruct((capacity, width * halves), BF16)
        out_specs = pl.BlockSpec(memory_space=pl.ANY)
        scratch += [
            pltpu.VMEM((capacity, width), BF16),
            pltpu.SemaphoreType.DMA((block_count // OUT_BLOCKS,)),
        ]
        if held is not None:
            aliases = {len(operands): 0}
            operands.append(held)
            in_specs.append(pl.BlockSpec(memory_space=pl.ANY))
    return pl.pallas_call(
        functools.partial(outer_kernel, half),
        out_shape=out_shape,
        in_specs=in_specs,
        out_specs=out_specs,
        scratch_shapes=scratch,
        input_output_aliases=aliases,
        compiler_params=pltpu.CompilerParams(vmem_limit_bytes=VMEM_LIMIT),
        cost_estimate=pl.CostEstimate(
            flops=tiles.size * width, bytes_accessed=4 << 20, transcendentals=0
        ),
        name="outer",
    )(*operands)


def all_to_all(payload):
    return lax.all_to_all(payload, ("dp", "dom"), split_axis=0, concat_axis=0, tiled=True)


def late_rows(parts, sizes, embedded, dest_part):
    room, direct, aligned = sizes
    shared = room - aligned
    count, width = embedded.shape
    onehot = (dest_part[:, None] == jnp.arange(parts, dtype=jnp.int32)[None, :]).astype(BF16)
    row = jnp.arange(count, dtype=jnp.int32)
    earlier = (row[None, :] < row[:, None]).astype(BF16)
    before = jnp.dot(earlier, onehot, preferred_element_type=F32)
    position = jnp.sum(before * onehot.astype(F32), axis=1).astype(jnp.int32)
    over = position - (room - 1)
    target = jnp.where(over < 0, -1, dest_part * shared + direct - aligned + over)
    select = (jnp.arange(parts * shared, dtype=jnp.int32)[:, None] == target[None, :]).astype(BF16)
    moved = jnp.dot(select, embedded, preferred_element_type=F32).astype(BF16)
    moved = moved.reshape(parts, shared, width // LANES, LANES)
    return jnp.swapaxes(moved, 1, 2).reshape(parts, width // LANES * shared, LANES)


def local(
    features,
    w_first,
    b_first,
    w_second,
    b_second,
    dest_part,
    dest_slot,
    tile_coords,
    tile_values,
    halo_send,
):
    count_dp = lax.axis_size("dp")
    count_dom = lax.axis_size("dom")
    parts = count_dp * count_dom
    row_count = features.shape[0]
    capacity = 3 * row_count
    most = -(-capacity // parts)
    room = -(-3 * most // 32) * 8
    direct = 2 * (room - 1) - most
    sizes = room, direct, direct // 8 * 8
    width = w_second.shape[1]
    halves = width // LANES
    block_rows = tile_values.shape[1]
    block_count = capacity // block_rows
    outgoing, embedded = project(
        parts,
        count_dom,
        sizes,
        features,
        w_first,
        b_first,
        w_second,
        b_second,
        dest_part,
        dest_slot,
    )
    arrived = all_to_all(outgoing)
    codes = halves * sizes[2] + (room - sizes[2]) - 1
    crowded = jnp.any(arrived[:, codes, FLAG] > 0.5)
    from_mate = lax.ppermute(
        arrived[:, halves * sizes[2] :, :],
        "dp",
        [(i, i ^ 1) for i in range(count_dp)],
    )
    extra = lax.cond(
        crowded,
        lambda: all_to_all(late_rows(parts, sizes, embedded, dest_part)),
        lambda: from_mate,
    )
    coords = tile_coords.reshape(-1)
    lists = halo_send[0]
    forward = [(i, (i + 1) % count_dom) for i in range(count_dom)]
    backward = [((i + 1) % count_dom, i) for i in range(count_dom)]

    def exchange(send):
        return lax.ppermute(send[0], "dom", forward), lax.ppermute(send[1], "dom", backward)

    halos = [
        exchange(send) for send in listed_blocks(sizes, halves, block_rows, arrived, extra, lists)
    ]
    size, *starts = place(sizes, halves, block_count, block_rows, arrived, extra)
    fields = list(starts)
    held = None
    for repeat in range(HOPS):
        for half in range(halves):
            partial = inner(lists.shape[1], tile_values, coords, starts[half], fields[half])
            operands = tile_values, coords, lists, size, partial, *halos[half]
            if repeat < HOPS - 1:
                fields[half], send = outer(*operands)
                halos[half] = exchange(send)
            else:
                held = outer(*operands, half=half, halves=halves, held=held)
    return held


def solution(mesh):
    placed = (
        P(("dp", "dom"), None),
        P(),
        P(),
        P(),
        P(),
        P(("dp", "dom")),
        P(("dp", "dom")),
        P(("dp", "dom"), None),
        P(("dp", "dom"), None, None),
        P(("dp", "dom"), None, None),
    )
    return jax.shard_map(
        local, mesh=mesh, in_specs=placed, out_specs=P(("dp", "dom"), None), check_vma=False
    )
```

time: 109 us -> 104 us (0.954)
  Pallas kernels: 33.5 us -> 28.5 us
  blocking collectives: 40.5 us -> 37.7 us
  waiting for transfers between devices: 13 us -> 15.4 us
    all_to_all x1, blocking collectives: 40.5 us -> 37.7 us  [all_to_all(): lax.all_to_all(payload, ('dp', 'dom'), split_axis=0, concat_axis=0, tiled...]
    pallas_call x1, Pallas kernels: 5.5 us -> 3.37 us  [place(): pl.pallas_call(functools.partial(place_kernel, sizes, halves), out_shape=...]
    ppermute x4, waiting for transfers between devices: 3.3 us -> 5.4 us  [exchange(): lax.ppermute(send[0], 'dom', forward)]
    pallas_call x1, Pallas kernels: 3.95 us -> 2.59 us  [listed_blocks(): pl.pallas_call(functools.partial(listed_kernel, sizes, halves), out_shape...]
    pallas_call x1, Pallas kernels: 10 us -> 8.88 us  [project(): pl.pallas_call(functools.partial(project_kernel, parts, mate, sizes), out...]
  transfers between devices with their start and end apart: 9 -> 9, of which waited for: 6 -> 6; matrix products, arithmetic and copies ran while one was open for 1% -> 1% of each run, Pallas kernels for 15% -> 14%
where the time goes in v3:
time: 104 us; the launch traced here: 103 us
  blocking collectives  37.7 us (36%)
  Pallas kernels  28.5 us (27%)
  starting transfers between devices  19.1 us (18%)
  waiting for transfers between devices  15.4 us (15%)
    all_to_all x1, blocking collectives, all_to_all(): lax.all_to_all(payload, ('dp', 'dom'), split_axis=0, concat_axis=0, tiled...  37.7 us
    ppermute x4, starting transfers between devices, exchange(): lax.ppermute(send[1], 'dom', backward)  17.8 us
    ppermute x4, waiting for transfers between devices, exchange(): lax.ppermute(send[1], 'dom', backward)  9.74 us
    pallas_call x4, Pallas kernels, outer(): pl.pallas_call(functools.partial(outer_kernel, half), out_shape=out_shape...  9.55 us
    pallas_call x1, Pallas kernels, project(): pl.pallas_call(functools.partial(project_kernel, parts, mate, sizes), out...  8.88 us
    ppermute x4, waiting for transfers between devices, exchange(): lax.ppermute(send[0], 'dom', forward)  5.4 us
    pallas_call x4, Pallas kernels, inner(): pl.pallas_call(functools.partial(inner_kernel, halo), out_shape=jax.Shape...  4.15 us
    pallas_call x1, Pallas kernels, place(): pl.pallas_call(functools.partial(place_kernel, sizes, halves), out_shape=...  3.37 us
  transfers between devices with their start and end apart: 9, of which 6 were waited for; matrix products, arithmetic and copies ran while one was open for 1% of the time, Pallas kernels for 14%

profile of v3, /device:TPU:0, one launch (start us, length us, event | category | flops | bytes accessed | tf_op | source)
XLA Modules:
  0.0 103.4 jit_solution(12993868932249252839)
XLA Ops:
  0.0 8.9 %project.1 = (bf16[32,144,128]{2,1,0:T(8,128)(2,1)}, bf16[1024,256]{1,0:T(8,128)(2,1)S(1)}) custom-call(bf16[1024,1024]{1,0:T(8,128)(2,1)} %refs_0_.5, bf16[1024,1024]{1,0:T(8,128)(2,1)} %refs_1_.1, s32[1024]{0:T(1024)} %refs_2_.1, s32[1024]{0:T(1024)} %refs_3_.1, bf16[1024]{0:T(1024)(128)(2,1)} %refs_4_.1, bf16[1024,256]{1,0:T(8,128)(2,1)} %refs_5_.1, ...), custom_call_target="tpu_custom_call" | custom-call | flops 2684354560 | bytes 8388608 | tf_op jit(solution)/shard_map/project/pallas_call | solution.py:131
  8.9 0.0 copy-start.3
  8.9 0.0 copy-start.2
  8.9 37.7 %all_to_all.10.arrived = bf16[32,144,128]{2,1,0:T(8,128)(2,1)S(1)} all-to-all(bf16[32,144,128]{2,1,0:T(8,128)(2,1)} %get-tuple-element.26), channel_id=1, replica_groups=mesh['dp'=4,'dom'=8] {'dp','dom'}, dimensions={0} | all-to-all | bytes 2359296 | tf_op jit(solution)/shard_map/all_to_all | solution.py:408
  46.6 0.1 slice.41
  46.7 0.1 collective-permute-start
  46.8 0.0 copy-done.3
  46.8 0.1 copy.15
  46.9 0.1 reshape.13.coords.refs_1_
  47.0 0.7 compare_reduce_fusion
  48.4 0.0 copy-done.2
  48.4 0.0 copy-start.1
  48.4 0.3 collective-permute-done
  48.7 0.4 copy-done.1
  49.1 2.6 %listed.1 = (bf16[2,8,128,128]{3,2,1,0:T(8,128)(2,1)S(1)}, bf16[2,8,128,128]{3,2,1,0:T(8,128)(2,1)S(1)}) custom-call(bf16[32,144,128]{2,1,0:T(8,128)(2,1)S(1)} %all_to_all.10.arrived, bf16[32,64,128]{2,1,0:T(8,128)(2,1)S(1)} %get-tuple-element.45.extra, s32[2,8]{1,0:T(2,128)S(1)} %bitcast.20), custom_call_target="tpu_custom_call" | custom-call | flops 3489660928 | bytes 4194304 | tf_op jit(solution)/shard_map/listed/pallas_call | solution.py:254
  51.7 1.1 %collective-permute-start.5 = (bf16[8,128,128]{2,1,0:T(8,128)(2,1)S(1)}, bf16[8,128,128]{2,1,0:T(8,128)(2,1)S(1)}, u32[]{:S(2)}, u32[]{:S(2)}) collective-permute-start(bf16[8,128,128]{2,1,0:T(8,128)(2,1)S(1)} %get-tuple-element.40), channel_id=1, source_target_pairs={{0,1},{1,2},{2,3},{3,4},{4,5},{5,6},{6,7},{7,0},{8,9},{9,10},{10,1... | collective-permute-start | bytes 786440 | tf_op jit(solution)/shard_map/ppermute | solution.py:484
  52.8 3.7 %collective-permute-start.6 = (bf16[8,128,128]{2,1,0:T(8,128)(2,1)S(1)}, bf16[8,128,128]{2,1,0:T(8,128)(2,1)S(1)}, u32[]{:S(2)}, u32[]{:S(2)}) collective-permute-start(bf16[8,128,128]{2,1,0:T(8,128)(2,1)S(1)} %get-tuple-element.39), channel_id=1, source_target_pairs={{1,0},{2,1},{3,2},{4,3},{5,4},{6,5},{7,6},{0,7},{9,8},{10,9},{11,1... | collective-permute-start | bytes 786440 | tf_op jit(solution)/shard_map/ppermute | solution.py:484
  56.5 0.1 collective-permute-start.1
  56.6 0.0 copy-start
  56.6 4.7 %collective-permute-start.2 = (bf16[8,128,128]{2,1,0:T(8,128)(2,1)S(1)}, bf16[8,128,128]{2,1,0:T(8,128)(2,1)S(1)}, u32[]{:S(2)}, u32[]{:S(2)}) collective-permute-start(bf16[8,128,128]{2,1,0:T(8,128)(2,1)S(1)} %get-tuple-element.43), channel_id=1, source_target_pairs={{1,0},{2,1},{3,2},{4,3},{5,4},{6,5},{7,6},{0,7},{9,8},{10,9},{11,1... | collective-permute-start | bytes 786440 | tf_op jit(solution)/shard_map/ppermute | solution.py:484
  61.3 3.4 %place.1 = (s32[1]{0:T(128)}, bf16[24,128,128]{2,1,0:T(8,128)(2,1)S(1)}, bf16[24,128,128]{2,1,0:T(8,128)(2,1)S(1)}) custom-call(bf16[32,144,128]{2,1,0:T(8,128)(2,1)S(1)} %all_to_all.10.arrived, bf16[32,64,128]{2,1,0:T(8,128)(2,1)S(1)} %get-tuple-element.45.extra), custom_call_target="tpu_custom_call" | custom-call | flops 5234491392 | bytes 4194304 | tf_op jit(solution)/shard_map/place/pallas_call | solution.py:271
  64.7 0.0 copy-done
  64.7 1.0 inner.6.refs_4_
  65.8 1.0 inner.4.refs_4_
  66.8 3.9 %collective-permute-done.5.refs_5_ = bf16[8,128,128]{2,1,0:T(8,128)(2,1)S(1)} collective-permute-done((bf16[8,128,128]{2,1,0:T(8,128)(2,1)S(1)}, bf16[8,128,128]{2,1,0:T(8,128)(2,1)S(1)}, u32[]{:S(2)}, u32[]{:S(2)}) %collective-permute-start.5) | collective-permute-done | bytes 262176 | tf_op jit(solution)/shard_map/ppermute | solution.py:484
  70.7 2.5 %collective-permute-done.6.refs_6_ = bf16[8,128,128]{2,1,0:T(8,128)(2,1)S(1)} collective-permute-done((bf16[8,128,128]{2,1,0:T(8,128)(2,1)S(1)}, bf16[8,128,128]{2,1,0:T(8,128)(2,1)S(1)}, u32[]{:S(2)}, u32[]{:S(2)}) %collective-permute-start.6) | collective-permute-done | bytes 262176 | tf_op jit(solution)/shard_map/ppermute | solution.py:484
  73.2 2.0 %outer.5 = (bf16[24,128,128]{2,1,0:T(8,128)(2,1)S(1)}, bf16[2,8,128,128]{3,2,1,0:T(8,128)(2,1)S(1)}) custom-call(bf16[48,128,128]{2,1,0:T(8,128)(2,1)S(1)} %copy-done, s32[96]{0:T(128)S(1)} %reshape.13.coords.refs_1_, s32[2,8]{1,0:T(2,128)S(1)} %bitcast.21, s32[1]{0:T(128)} %get-tuple-element.28.refs_3_, f32[24,128,128]{2,1,0:T(8,128)S(1)} %inner.6.refs_4_, ...), custom_call_target="tpu_custom_call" | custom-call | flops 100663296 | bytes 4194304 | tf_op jit(solution)/shard_map/outer/pallas_call | solution.py:392
  75.3 0.1 collective-permute-start.7
  75.4 4.7 %collective-permute-start.8 = (bf16[8,128,128]{2,1,0:T(8,128)(2,1)S(1)}, bf16[8,128,128]{2,1,0:T(8,128)(2,1)S(1)}, u32[]{:S(2)}, u32[]{:S(2)}) collective-permute-start(bf16[8,128,128]{2,1,0:T(8,128)(2,1)S(1)} %get-tuple-element.37), channel_id=1, source_target_pairs={{1,0},{2,1},{3,2},{4,3},{5,4},{6,5},{7,6},{0,7},{9,8},{10,9},{11,1... | collective-permute-start | bytes 786440 | tf_op jit(solution)/shard_map/ppermute | solution.py:484
  80.1 0.0 collective-permute-done.1.refs_5_
  80.1 0.0 collective-permute-done.2.refs_6_
  80.1 2.0 %outer.4 = (bf16[24,128,128]{2,1,0:T(8,128)(2,1)S(1)}, bf16[2,8,128,128]{3,2,1,0:T(8,128)(2,1)S(1)}) custom-call(bf16[48,128,128]{2,1,0:T(8,128)(2,1)S(1)} %copy-done, s32[96]{0:T(128)S(1)} %reshape.13.coords.refs_1_, s32[2,8]{1,0:T(2,128)S(1)} %bitcast.22, s32[1]{0:T(128)} %get-tuple-element.28.refs_3_, f32[24,128,128]{2,1,0:T(8,128)S(1)} %inner.4.refs_4_, ...), custom_call_target="tpu_custom_call" | custom-call | flops 100663296 | bytes 4194304 | tf_op jit(solution)/shard_map/outer/pallas_call | solution.py:392
  82.2 0.1 collective-permute-start.3
  82.3 4.7 %collective-permute-start.4 = (bf16[8,128,128]{2,1,0:T(8,128)(2,1)S(1)}, bf16[8,128,128]{2,1,0:T(8,128)(2,1)S(1)}, u32[]{:S(2)}, u32[]{:S(2)}) collective-permute-start(bf16[8,128,128]{2,1,0:T(8,128)(2,1)S(1)} %get-tuple-element.41), channel_id=1, source_target_pairs={{1,0},{2,1},{3,2},{4,3},{5,4},{6,5},{7,6},{0,7},{9,8},{10,9},{11,1... | collective-permute-start | bytes 786440 | tf_op jit(solution)/shard_map/ppermute | solution.py:484
  87.0 1.1 %inner.7.refs_4_ = f32[24,128,128]{2,1,0:T(8,128)S(1)} custom-call(bf16[48,128,128]{2,1,0:T(8,128)(2,1)S(1)} %copy-done, s32[96]{0:T(128)S(1)} %reshape.13.coords.refs_1_, bf16[24,128,128]{2,1,0:T(8,128)(2,1)S(1)} %get-tuple-element.33.start.current, bf16[24,128,128]{2,1,0:T(8,128)(2,1)S(1)} %get-tuple-element.35.current), custom_call_target="tpu_custom_call" | custom-call | flops 100663296 | bytes 4194304 | tf_op jit(solution)/shard_map/inner/pallas_call | solution.py:350
  88.0 1.0 inner.5.refs_4_
  89.1 1.5 %collective-permute-done.7.refs_5_ = bf16[8,128,128]{2,1,0:T(8,128)(2,1)S(1)} collective-permute-done((bf16[8,128,128]{2,1,0:T(8,128)(2,1)S(1)}, bf16[8,128,128]{2,1,0:T(8,128)(2,1)S(1)}, u32[]{:S(2)}, u32[]{:S(2)}) %collective-permute-start.7) | collective-permute-done | bytes 262176 | tf_op jit(solution)/shard_map/ppermute | solution.py:484
  90.6 5.4 %collective-permute-done.8.refs_6_ = bf16[8,128,128]{2,1,0:T(8,128)(2,1)S(1)} collective-permute-done((bf16[8,128,128]{2,1,0:T(8,128)(2,1)S(1)}, bf16[8,128,128]{2,1,0:T(8,128)(2,1)S(1)}, u32[]{:S(2)}, u32[]{:S(2)}) %collective-permute-start.8) | collective-permute-done | bytes 262176 | tf_op jit(solution)/shard_map/ppermute | solution.py:484
  95.9 2.7 %outer.6.refs_7_ = bf16[3072,256]{1,0:T(8,128)(2,1)} custom-call(bf16[48,128,128]{2,1,0:T(8,128)(2,1)S(1)} %copy-done, s32[96]{0:T(128)S(1)} %reshape.13.coords.refs_1_, s32[2,8]{1,0:T(2,128)S(1)} %bitcast.23, s32[1]{0:T(128)} %get-tuple-element.28.refs_3_, f32[24,128,128]{2,1,0:T(8,128)S(1)} %inner.7.refs_4_, ...), custom_call_target="tpu_custom_call" | custom-call | flops 100663296 | bytes 4194304 | tf_op jit(solution)/shard_map/outer/pallas_call | solution.py:392
  98.7 0.0 collective-permute-done.3.refs_5_
  98.7 1.8 %collective-permute-done.4.refs_6_ = bf16[8,128,128]{2,1,0:T(8,128)(2,1)S(1)} collective-permute-done((bf16[8,128,128]{2,1,0:T(8,128)(2,1)S(1)}, bf16[8,128,128]{2,1,0:T(8,128)(2,1)S(1)}, u32[]{:S(2)}, u32[]{:S(2)}) %collective-permute-start.4) | collective-permute-done | bytes 262176 | tf_op jit(solution)/shard_map/ppermute | solution.py:484
  100.5 2.7 %outer.7 = bf16[3072,256]{1,0:T(8,128)(2,1)} custom-call(bf16[48,128,128]{2,1,0:T(8,128)(2,1)S(1)} %copy-done, s32[96]{0:T(128)S(1)} %reshape.13.coords.refs_1_, s32[2,8]{1,0:T(2,128)S(1)} %bitcast.24, s32[1]{0:T(128)} %get-tuple-element.28.refs_3_, f32[24,128,128]{2,1,0:T(8,128)S(1)} %inner.5.refs_4_, ...), custom_call_target="tpu_custom_call", output_to_operand_aliasing={{}: (7, {})} | custom-call | flops 100663296 | bytes 4194304 | tf_op jit(solution)/shard_map/outer/pallas_call | solution.py:392
  (5 shorter events, 0.2 us)
Async XLA Ops:
  8.9 37.9 %copy-start.3 = (s32[48,2]{0,1:T(2,128)S(1)}, s32[48,2]{0,1:T(2,128)}, u32[]{:S(2)}) copy-start(s32[48,2]{0,1:T(2,128)} %param.19) | copy-start | bytes 1156
  8.9 39.5 %copy-start.2 = (s32[1024]{0:T(1024)S(1)}, s32[1024]{0:T(1024)}, u32[]{:S(2)}) copy-start(s32[1024]{0:T(1024)} %refs_2_.1) | copy-start | bytes 12292
  46.7 2.0 %collective-permute-start = (bf16[32,64,128]{2,1,0:T(8,128)(2,1)S(1)}, bf16[32,64,128]{2,1,0:T(8,128)(2,1)S(1)}, u32[]{:S(2)}, u32[]{:S(2)}) collective-permute-start(bf16[32,64,128]{2,1,0:T(8,128)(2,1)S(1)} %slice.41), channel_id=1, source_target_pairs={{0,8},{8,0},{16,24},{24,16},{1,9},{9,1},{17,25},{25,17},{2,10},{10... | collective-permute-start | bytes 1572872 | tf_op jit(solution)/shard_map/ppermute | solution.py:468
  48.4 0.7 copy-start.1
  51.7 19.0 %collective-permute-start.5 = (bf16[8,128,128]{2,1,0:T(8,128)(2,1)S(1)}, bf16[8,128,128]{2,1,0:T(8,128)(2,1)S(1)}, u32[]{:S(2)}, u32[]{:S(2)}) collective-permute-start(bf16[8,128,128]{2,1,0:T(8,128)(2,1)S(1)} %get-tuple-element.40), channel_id=1, source_target_pairs={{0,1},{1,2},{2,3},{3,4},{4,5},{5,6},{6,7},{7,0},{8,9},{9,10},{10,1... | collective-permute-start | bytes 786440 | tf_op jit(solution)/shard_map/ppermute | solution.py:484
  52.8 20.4 %collective-permute-start.6 = (bf16[8,128,128]{2,1,0:T(8,128)(2,1)S(1)}, bf16[8,128,128]{2,1,0:T(8,128)(2,1)S(1)}, u32[]{:S(2)}, u32[]{:S(2)}) collective-permute-start(bf16[8,128,128]{2,1,0:T(8,128)(2,1)S(1)} %get-tuple-element.39), channel_id=1, source_target_pairs={{1,0},{2,1},{3,2},{4,3},{5,4},{6,5},{7,6},{0,7},{9,8},{10,9},{11,1... | collective-permute-start | bytes 786440 | tf_op jit(solution)/shard_map/ppermute | solution.py:484
  56.5 23.6 %collective-permute-start.1 = (bf16[8,128,128]{2,1,0:T(8,128)(2,1)S(1)}, bf16[8,128,128]{2,1,0:T(8,128)(2,1)S(1)}, u32[]{:S(2)}, u32[]{:S(2)}) collective-permute-start(bf16[8,128,128]{2,1,0:T(8,128)(2,1)S(1)} %get-tuple-element.44), channel_id=1, source_target_pairs={{0,1},{1,2},{2,3},{3,4},{4,5},{5,6},{6,7},{7,0},{8,9},{9,10},{10,1... | collective-permute-start | bytes 786440 | tf_op jit(solution)/shard_map/ppermute | solution.py:484
  56.6 8.1 %copy-start = (bf16[48,128,128]{2,1,0:T(8,128)(2,1)S(1)}, bf16[48,128,128]{2,1,0:T(8,128)(2,1)}, u32[]{:S(2)}) copy-start(bf16[48,128,128]{2,1,0:T(8,128)(2,1)} %refs_0_.9) | copy-start | bytes 4718596
  56.6 23.5 %collective-permute-start.2 = (bf16[8,128,128]{2,1,0:T(8,128)(2,1)S(1)}, bf16[8,128,128]{2,1,0:T(8,128)(2,1)S(1)}, u32[]{:S(2)}, u32[]{:S(2)}) collective-permute-start(bf16[8,128,128]{2,1,0:T(8,128)(2,1)S(1)} %get-tuple-element.43), channel_id=1, source_target_pairs={{1,0},{2,1},{3,2},{4,3},{5,4},{6,5},{7,6},{0,7},{9,8},{10,9},{11,1... | collective-permute-start | bytes 786440 | tf_op jit(solution)/shard_map/ppermute | solution.py:484
  75.3 15.2 %collective-permute-start.7 = (bf16[8,128,128]{2,1,0:T(8,128)(2,1)S(1)}, bf16[8,128,128]{2,1,0:T(8,128)(2,1)S(1)}, u32[]{:S(2)}, u32[]{:S(2)}) collective-permute-start(bf16[8,128,128]{2,1,0:T(8,128)(2,1)S(1)} %get-tuple-element.38), channel_id=1, source_target_pairs={{0,1},{1,2},{2,3},{3,4},{4,5},{5,6},{6,7},{7,0},{8,9},{9,10},{10,1... | collective-permute-start | bytes 786440 | tf_op jit(solution)/shard_map/ppermute | solution.py:484
  75.4 20.5 %collective-permute-start.8 = (bf16[8,128,128]{2,1,0:T(8,128)(2,1)S(1)}, bf16[8,128,128]{2,1,0:T(8,128)(2,1)S(1)}, u32[]{:S(2)}, u32[]{:S(2)}) collective-permute-start(bf16[8,128,128]{2,1,0:T(8,128)(2,1)S(1)} %get-tuple-element.37), channel_id=1, source_target_pairs={{1,0},{2,1},{3,2},{4,3},{5,4},{6,5},{7,6},{0,7},{9,8},{10,9},{11,1... | collective-permute-start | bytes 786440 | tf_op jit(solution)/shard_map/ppermute | solution.py:484
  82.2 16.5 %collective-permute-start.3 = (bf16[8,128,128]{2,1,0:T(8,128)(2,1)S(1)}, bf16[8,128,128]{2,1,0:T(8,128)(2,1)S(1)}, u32[]{:S(2)}, u32[]{:S(2)}) collective-permute-start(bf16[8,128,128]{2,1,0:T(8,128)(2,1)S(1)} %get-tuple-element.42), channel_id=1, source_target_pairs={{0,1},{1,2},{2,3},{3,4},{4,5},{5,6},{6,7},{7,0},{8,9},{9,10},{10,1... | collective-permute-start | bytes 786440 | tf_op jit(solution)/shard_map/ppermute | solution.py:484
  82.3 18.3 %collective-permute-start.4 = (bf16[8,128,128]{2,1,0:T(8,128)(2,1)S(1)}, bf16[8,128,128]{2,1,0:T(8,128)(2,1)S(1)}, u32[]{:S(2)}, u32[]{:S(2)}) collective-permute-start(bf16[8,128,128]{2,1,0:T(8,128)(2,1)S(1)} %get-tuple-element.41), channel_id=1, source_target_pairs={{1,0},{2,1},{3,2},{4,3},{5,4},{6,5},{7,6},{0,7},{9,8},{10,9},{11,1... | collective-permute-start | bytes 786440 | tf_op jit(solution)/shard_map/ppermute | solution.py:484

commit v4 on v3

--- a/solution.py
+++ b/solution.py
@@ -89,10 +89,15 @@
     copies[1].wait()
     copies[4].wait()
     hidden = jnp.dot(features[...], w_first[...], preferred_element_type=F32)
-    hidden = gelu(hidden + b_first[...].astype(F32)[None, :]).astype(BF16)
     copies[5].wait()
     copies[6].wait()
-    total = jnp.dot(hidden, w_second[...], preferred_element_type=F32)
+    totals = []
+    half_rows = count // 2
+    for first in range(0, count, half_rows):
+        piece = hidden[first : first + half_rows] + b_first[...].astype(F32)[None, :]
+        piece = gelu(piece).astype(BF16)
+        totals.append(jnp.dot(piece, w_second[...], preferred_element_type=F32))
+    total = jnp.concatenate(totals, axis=0)
     embedded[...] = (total + b_second[...].astype(F32)[None, :]).astype(BF16)
 
     keep = pltpu.make_async_copy(embedded, embedded_out, leaving.at[parts // DESTS])

time: 104 us -> 103 us (level)
    ppermute x4, waiting for transfers between devices: 5.4 us -> 3.98 us  [exchange(): lax.ppermute(send[0], 'dom', forward)]
    ppermute x4, waiting for transfers between devices: 9.74 us -> 11.1 us  [exchange(): lax.ppermute(send[1], 'dom', backward)]
where the time goes in v4:
time: 103 us
  blocking collectives  37.7 us (37%)
  Pallas kernels  27.7 us (27%)
  starting transfers between devices  19.1 us (19%)
  waiting for transfers between devices  15.4 us (15%)
  between operations  1.04 us (1%)
    all_to_all x1, blocking collectives, all_to_all(): lax.all_to_all(payload, ('dp', 'dom'), split_axis=0, concat_axis=0, tiled...  37.7 us
    ppermute x4, starting transfers between devices, exchange(): lax.ppermute(send[1], 'dom', backward)  17.7 us
    ppermute x4, waiting for transfers between devices, exchange(): lax.ppermute(send[1], 'dom', backward)  11.1 us
    pallas_call x4, Pallas kernels, outer(): pl.pallas_call(functools.partial(outer_kernel, half), out_shape=out_shape...  9.53 us
    pallas_call x1, Pallas kernels, project(): pl.pallas_call(functools.partial(project_kernel, parts, mate, sizes), out...  8.1 us
    pallas_call x4, Pallas kernels, inner(): pl.pallas_call(functools.partial(inner_kernel, halo), out_shape=jax.Shape...  4.14 us
    ppermute x4, waiting for transfers between devices, exchange(): lax.ppermute(send[0], 'dom', forward)  3.98 us
    pallas_call x1, Pallas kernels, place(): pl.pallas_call(functools.partial(place_kernel, sizes, halves), out_shape=...  3.37 us
  transfers between devices with their start and end apart: 9, of which 6 were waited for; matrix products, arithmetic and copies ran while one was open for 1% of the time, Pallas kernels for 14%

profile of v4, /device:TPU:0, one launch (start us, length us, event | category | flops | bytes accessed | tf_op | source)
XLA Modules:
  0.0 102.6 jit_solution(4367323093615253448)
XLA Ops:
  0.0 8.1 %project.1 = (bf16[32,144,128]{2,1,0:T(8,128)(2,1)}, bf16[1024,256]{1,0:T(8,128)(2,1)S(1)}) custom-call(bf16[1024,1024]{1,0:T(8,128)(2,1)} %refs_0_.5, bf16[1024,1024]{1,0:T(8,128)(2,1)} %refs_1_.1, s32[1024]{0:T(1024)} %refs_2_.1, s32[1024]{0:T(1024)} %refs_3_.1, bf16[1024]{0:T(1024)(128)(2,1)} %refs_4_.1, bf16[1024,256]{1,0:T(8,128)(2,1)} %refs_5_.1, ...), custom_call_target="tpu_custom_call" | custom-call | flops 2684354560 | bytes 8388608 | tf_op jit(solution)/shard_map/project/pallas_call | solution.py:136
  8.1 0.0 copy-start.3
  8.1 0.0 copy-start.2
  8.1 37.7 %all_to_all.10.arrived = bf16[32,144,128]{2,1,0:T(8,128)(2,1)S(1)} all-to-all(bf16[32,144,128]{2,1,0:T(8,128)(2,1)} %get-tuple-element.26), channel_id=1, replica_groups=mesh['dp'=4,'dom'=8] {'dp','dom'}, dimensions={0} | all-to-all | bytes 2359296 | tf_op jit(solution)/shard_map/all_to_all | solution.py:413
  45.8 0.1 slice.41
  45.9 0.1 collective-permute-start
  46.0 0.0 copy-done.3
  46.0 0.1 copy.15
  46.1 0.1 reshape.13.coords.refs_1_
  46.2 0.7 compare_reduce_fusion
  47.6 0.0 copy-done.2
  47.6 0.0 copy-start.1
  47.6 0.3 collective-permute-done
  47.9 0.4 copy-done.1
  48.3 2.6 %listed.1 = (bf16[2,8,128,128]{3,2,1,0:T(8,128)(2,1)S(1)}, bf16[2,8,128,128]{3,2,1,0:T(8,128)(2,1)S(1)}) custom-call(bf16[32,144,128]{2,1,0:T(8,128)(2,1)S(1)} %all_to_all.10.arrived, bf16[32,64,128]{2,1,0:T(8,128)(2,1)S(1)} %get-tuple-element.45.extra, s32[2,8]{1,0:T(2,128)S(1)} %bitcast.20), custom_call_target="tpu_custom_call" | custom-call | flops 3489660928 | bytes 4194304 | tf_op jit(solution)/shard_map/listed/pallas_call | solution.py:259
  50.9 1.2 %collective-permute-start.5 = (bf16[8,128,128]{2,1,0:T(8,128)(2,1)S(1)}, bf16[8,128,128]{2,1,0:T(8,128)(2,1)S(1)}, u32[]{:S(2)}, u32[]{:S(2)}) collective-permute-start(bf16[8,128,128]{2,1,0:T(8,128)(2,1)S(1)} %get-tuple-element.40), channel_id=1, source_target_pairs={{0,1},{1,2},{2,3},{3,4},{4,5},{5,6},{6,7},{7,0},{8,9},{9,10},{10,1... | collective-permute-start | bytes 786440 | tf_op jit(solution)/shard_map/ppermute | solution.py:489
  52.1 3.6 %collective-permute-start.6 = (bf16[8,128,128]{2,1,0:T(8,128)(2,1)S(1)}, bf16[8,128,128]{2,1,0:T(8,128)(2,1)S(1)}, u32[]{:S(2)}, u32[]{:S(2)}) collective-permute-start(bf16[8,128,128]{2,1,0:T(8,128)(2,1)S(1)} %get-tuple-element.39), channel_id=1, source_target_pairs={{1,0},{2,1},{3,2},{4,3},{5,4},{6,5},{7,6},{0,7},{9,8},{10,9},{11,1... | collective-permute-start | bytes 786440 | tf_op jit(solution)/shard_map/ppermute | solution.py:489
  55.7 0.1 collective-permute-start.1
  55.8 0.0 copy-start
  55.8 4.7 %collective-permute-start.2 = (bf16[8,128,128]{2,1,0:T(8,128)(2,1)S(1)}, bf16[8,128,128]{2,1,0:T(8,128)(2,1)S(1)}, u32[]{:S(2)}, u32[]{:S(2)}) collective-permute-start(bf16[8,128,128]{2,1,0:T(8,128)(2,1)S(1)} %get-tuple-element.43), channel_id=1, source_target_pairs={{1,0},{2,1},{3,2},{4,3},{5,4},{6,5},{7,6},{0,7},{9,8},{10,9},{11,1... | collective-permute-start | bytes 786440 | tf_op jit(solution)/shard_map/ppermute | solution.py:489
  60.5 3.4 %place.1 = (s32[1]{0:T(128)}, bf16[24,128,128]{2,1,0:T(8,128)(2,1)S(1)}, bf16[24,128,128]{2,1,0:T(8,128)(2,1)S(1)}) custom-call(bf16[32,144,128]{2,1,0:T(8,128)(2,1)S(1)} %all_to_all.10.arrived, bf16[32,64,128]{2,1,0:T(8,128)(2,1)S(1)} %get-tuple-element.45.extra), custom_call_target="tpu_custom_call" | custom-call | flops 5234491392 | bytes 4194304 | tf_op jit(solution)/shard_map/place/pallas_call | solution.py:276
  63.9 0.0 copy-done
  63.9 1.0 %inner.6.refs_4_ = f32[24,128,128]{2,1,0:T(8,128)S(1)} custom-call(bf16[48,128,128]{2,1,0:T(8,128)(2,1)S(1)} %copy-done, s32[96]{0:T(128)S(1)} %reshape.13.coords.refs_1_, bf16[24,128,128]{2,1,0:T(8,128)(2,1)S(1)} %get-tuple-element.33.start.current, bf16[24,128,128]{2,1,0:T(8,128)(2,1)S(1)} %get-tuple-element.33.start.current), custom_call_target="tpu_custom_call" | custom-call | flops 100663296 | bytes 4194304 | tf_op jit(solution)/shard_map/inner/pallas_call | solution.py:355
  64.9 1.0 %inner.4.refs_4_ = f32[24,128,128]{2,1,0:T(8,128)S(1)} custom-call(bf16[48,128,128]{2,1,0:T(8,128)(2,1)S(1)} %copy-done, s32[96]{0:T(128)S(1)} %reshape.13.coords.refs_1_, bf16[24,128,128]{2,1,0:T(8,128)(2,1)S(1)} %get-tuple-element.29.start.current, bf16[24,128,128]{2,1,0:T(8,128)(2,1)S(1)} %get-tuple-element.29.start.current), custom_call_target="tpu_custom_call" | custom-call | flops 100663296 | bytes 4194304 | tf_op jit(solution)/shard_map/inner/pallas_call | solution.py:355
  66.0 4.0 %collective-permute-done.5.refs_5_ = bf16[8,128,128]{2,1,0:T(8,128)(2,1)S(1)} collective-permute-done((bf16[8,128,128]{2,1,0:T(8,128)(2,1)S(1)}, bf16[8,128,128]{2,1,0:T(8,128)(2,1)S(1)}, u32[]{:S(2)}, u32[]{:S(2)}) %collective-permute-start.5) | collective-permute-done | bytes 262176 | tf_op jit(solution)/shard_map/ppermute | solution.py:489
  70.0 3.8 %collective-permute-done.6.refs_6_ = bf16[8,128,128]{2,1,0:T(8,128)(2,1)S(1)} collective-permute-done((bf16[8,128,128]{2,1,0:T(8,128)(2,1)S(1)}, bf16[8,128,128]{2,1,0:T(8,128)(2,1)S(1)}, u32[]{:S(2)}, u32[]{:S(2)}) %collective-permute-start.6) | collective-permute-done | bytes 262176 | tf_op jit(solution)/shard_map/ppermute | solution.py:489
  73.8 2.0 %outer.5 = (bf16[24,128,128]{2,1,0:T(8,128)(2,1)S(1)}, bf16[2,8,128,128]{3,2,1,0:T(8,128)(2,1)S(1)}) custom-call(bf16[48,128,128]{2,1,0:T(8,128)(2,1)S(1)} %copy-done, s32[96]{0:T(128)S(1)} %reshape.13.coords.refs_1_, s32[2,8]{1,0:T(2,128)S(1)} %bitcast.21, s32[1]{0:T(128)} %get-tuple-element.28.refs_3_, f32[24,128,128]{2,1,0:T(8,128)S(1)} %inner.6.refs_4_, ...), custom_call_target="tpu_custom_call" | custom-call | flops 100663296 | bytes 4194304 | tf_op jit(solution)/shard_map/outer/pallas_call | solution.py:397
  75.9 0.1 collective-permute-start.7
  75.9 4.7 %collective-permute-start.8 = (bf16[8,128,128]{2,1,0:T(8,128)(2,1)S(1)}, bf16[8,128,128]{2,1,0:T(8,128)(2,1)S(1)}, u32[]{:S(2)}, u32[]{:S(2)}) collective-permute-start(bf16[8,128,128]{2,1,0:T(8,128)(2,1)S(1)} %get-tuple-element.37), channel_id=1, source_target_pairs={{1,0},{2,1},{3,2},{4,3},{5,4},{6,5},{7,6},{0,7},{9,8},{10,9},{11,1... | collective-permute-start | bytes 786440 | tf_op jit(solution)/shard_map/ppermute | solution.py:489
  80.6 0.0 collective-permute-done.1.refs_5_
  80.7 0.6 collective-permute-done.2.refs_6_
  81.3 2.0 %outer.4 = (bf16[24,128,128]{2,1,0:T(8,128)(2,1)S(1)}, bf16[2,8,128,128]{3,2,1,0:T(8,128)(2,1)S(1)}) custom-call(bf16[48,128,128]{2,1,0:T(8,128)(2,1)S(1)} %copy-done, s32[96]{0:T(128)S(1)} %reshape.13.coords.refs_1_, s32[2,8]{1,0:T(2,128)S(1)} %bitcast.22, s32[1]{0:T(128)} %get-tuple-element.28.refs_3_, f32[24,128,128]{2,1,0:T(8,128)S(1)} %inner.4.refs_4_, ...), custom_call_target="tpu_custom_call" | custom-call | flops 100663296 | bytes 4194304 | tf_op jit(solution)/shard_map/outer/pallas_call | solution.py:397
  83.4 0.1 collective-permute-start.3
  83.4 4.7 %collective-permute-start.4 = (bf16[8,128,128]{2,1,0:T(8,128)(2,1)S(1)}, bf16[8,128,128]{2,1,0:T(8,128)(2,1)S(1)}, u32[]{:S(2)}, u32[]{:S(2)}) collective-permute-start(bf16[8,128,128]{2,1,0:T(8,128)(2,1)S(1)} %get-tuple-element.41), channel_id=1, source_target_pairs={{1,0},{2,1},{3,2},{4,3},{5,4},{6,5},{7,6},{0,7},{9,8},{10,9},{11,1... | collective-permute-start | bytes 786440 | tf_op jit(solution)/shard_map/ppermute | solution.py:489
  88.1 1.0 %inner.7.refs_4_ = f32[24,128,128]{2,1,0:T(8,128)S(1)} custom-call(bf16[48,128,128]{2,1,0:T(8,128)(2,1)S(1)} %copy-done, s32[96]{0:T(128)S(1)} %reshape.13.coords.refs_1_, bf16[24,128,128]{2,1,0:T(8,128)(2,1)S(1)} %get-tuple-element.33.start.current, bf16[24,128,128]{2,1,0:T(8,128)(2,1)S(1)} %get-tuple-element.35.current), custom_call_target="tpu_custom_call" | custom-call | flops 100663296 | bytes 4194304 | tf_op jit(solution)/shard_map/inner/pallas_call | solution.py:355
  89.2 1.0 %inner.5.refs_4_ = f32[24,128,128]{2,1,0:T(8,128)S(1)} custom-call(bf16[48,128,128]{2,1,0:T(8,128)(2,1)S(1)} %copy-done, s32[96]{0:T(128)S(1)} %reshape.13.coords.refs_1_, bf16[24,128,128]{2,1,0:T(8,128)(2,1)S(1)} %get-tuple-element.29.start.current, bf16[24,128,128]{2,1,0:T(8,128)(2,1)S(1)} %get-tuple-element.31.current), custom_call_target="tpu_custom_call" | custom-call | flops 100663296 | bytes 4194304 | tf_op jit(solution)/shard_map/inner/pallas_call | solution.py:355
  90.2 0.0 collective-permute-done.7.refs_5_
  90.2 5.1 %collective-permute-done.8.refs_6_ = bf16[8,128,128]{2,1,0:T(8,128)(2,1)S(1)} collective-permute-done((bf16[8,128,128]{2,1,0:T(8,128)(2,1)S(1)}, bf16[8,128,128]{2,1,0:T(8,128)(2,1)S(1)}, u32[]{:S(2)}, u32[]{:S(2)}) %collective-permute-start.8) | collective-permute-done | bytes 262176 | tf_op jit(solution)/shard_map/ppermute | solution.py:489
  95.3 2.7 %outer.6.refs_7_ = bf16[3072,256]{1,0:T(8,128)(2,1)} custom-call(bf16[48,128,128]{2,1,0:T(8,128)(2,1)S(1)} %copy-done, s32[96]{0:T(128)S(1)} %reshape.13.coords.refs_1_, s32[2,8]{1,0:T(2,128)S(1)} %bitcast.23, s32[1]{0:T(128)} %get-tuple-element.28.refs_3_, f32[24,128,128]{2,1,0:T(8,128)S(1)} %inner.7.refs_4_, ...), custom_call_target="tpu_custom_call" | custom-call | flops 100663296 | bytes 4194304 | tf_op jit(solution)/shard_map/outer/pallas_call | solution.py:397
  98.1 0.0 collective-permute-done.3.refs_5_
  98.1 1.6 %collective-permute-done.4.refs_6_ = bf16[8,128,128]{2,1,0:T(8,128)(2,1)S(1)} collective-permute-done((bf16[8,128,128]{2,1,0:T(8,128)(2,1)S(1)}, bf16[8,128,128]{2,1,0:T(8,128)(2,1)S(1)}, u32[]{:S(2)}, u32[]{:S(2)}) %collective-permute-start.4) | collective-permute-done | bytes 262176 | tf_op jit(solution)/shard_map/ppermute | solution.py:489
  99.7 2.7 %outer.7 = bf16[3072,256]{1,0:T(8,128)(2,1)} custom-call(bf16[48,128,128]{2,1,0:T(8,128)(2,1)S(1)} %copy-done, s32[96]{0:T(128)S(1)} %reshape.13.coords.refs_1_, s32[2,8]{1,0:T(2,128)S(1)} %bitcast.24, s32[1]{0:T(128)} %get-tuple-element.28.refs_3_, f32[24,128,128]{2,1,0:T(8,128)S(1)} %inner.5.refs_4_, ...), custom_call_target="tpu_custom_call", output_to_operand_aliasing={{}: (7, {})} | custom-call | flops 100663296 | bytes 4194304 | tf_op jit(solution)/shard_map/outer/pallas_call | solution.py:397
  (5 shorter events, 0.2 us)
Async XLA Ops:
  8.1 37.9 %copy-start.3 = (s32[48,2]{0,1:T(2,128)S(1)}, s32[48,2]{0,1:T(2,128)}, u32[]{:S(2)}) copy-start(s32[48,2]{0,1:T(2,128)} %param.19) | copy-start | bytes 1156
  8.1 39.5 %copy-start.2 = (s32[1024]{0:T(1024)S(1)}, s32[1024]{0:T(1024)}, u32[]{:S(2)}) copy-start(s32[1024]{0:T(1024)} %refs_2_.1) | copy-start | bytes 12292
  45.9 2.0 %collective-permute-start = (bf16[32,64,128]{2,1,0:T(8,128)(2,1)S(1)}, bf16[32,64,128]{2,1,0:T(8,128)(2,1)S(1)}, u32[]{:S(2)}, u32[]{:S(2)}) collective-permute-start(bf16[32,64,128]{2,1,0:T(8,128)(2,1)S(1)} %slice.41), channel_id=1, source_target_pairs={{0,8},{8,0},{16,24},{24,16},{1,9},{9,1},{17,25},{25,17},{2,10},{10... | collective-permute-start | bytes 1572872 | tf_op jit(solution)/shard_map/ppermute | solution.py:473
  47.6 0.7 copy-start.1
  50.9 19.0 %collective-permute-start.5 = (bf16[8,128,128]{2,1,0:T(8,128)(2,1)S(1)}, bf16[8,128,128]{2,1,0:T(8,128)(2,1)S(1)}, u32[]{:S(2)}, u32[]{:S(2)}) collective-permute-start(bf16[8,128,128]{2,1,0:T(8,128)(2,1)S(1)} %get-tuple-element.40), channel_id=1, source_target_pairs={{0,1},{1,2},{2,3},{3,4},{4,5},{5,6},{6,7},{7,0},{8,9},{9,10},{10,1... | collective-permute-start | bytes 786440 | tf_op jit(solution)/shard_map/ppermute | solution.py:489
  52.1 21.7 %collective-permute-start.6 = (bf16[8,128,128]{2,1,0:T(8,128)(2,1)S(1)}, bf16[8,128,128]{2,1,0:T(8,128)(2,1)S(1)}, u32[]{:S(2)}, u32[]{:S(2)}) collective-permute-start(bf16[8,128,128]{2,1,0:T(8,128)(2,1)S(1)} %get-tuple-element.39), channel_id=1, source_target_pairs={{1,0},{2,1},{3,2},{4,3},{5,4},{6,5},{7,6},{0,7},{9,8},{10,9},{11,1... | collective-permute-start | bytes 786440 | tf_op jit(solution)/shard_map/ppermute | solution.py:489
  55.7 24.9 %collective-permute-start.1 = (bf16[8,128,128]{2,1,0:T(8,128)(2,1)S(1)}, bf16[8,128,128]{2,1,0:T(8,128)(2,1)S(1)}, u32[]{:S(2)}, u32[]{:S(2)}) collective-permute-start(bf16[8,128,128]{2,1,0:T(8,128)(2,1)S(1)} %get-tuple-element.44), channel_id=1, source_target_pairs={{0,1},{1,2},{2,3},{3,4},{4,5},{5,6},{6,7},{7,0},{8,9},{9,10},{10,1... | collective-permute-start | bytes 786440 | tf_op jit(solution)/shard_map/ppermute | solution.py:489
  55.8 8.1 %copy-start = (bf16[48,128,128]{2,1,0:T(8,128)(2,1)S(1)}, bf16[48,128,128]{2,1,0:T(8,128)(2,1)}, u32[]{:S(2)}) copy-start(bf16[48,128,128]{2,1,0:T(8,128)(2,1)} %refs_0_.9) | copy-start | bytes 4718596
  55.8 25.5 %collective-permute-start.2 = (bf16[8,128,128]{2,1,0:T(8,128)(2,1)S(1)}, bf16[8,128,128]{2,1,0:T(8,128)(2,1)S(1)}, u32[]{:S(2)}, u32[]{:S(2)}) collective-permute-start(bf16[8,128,128]{2,1,0:T(8,128)(2,1)S(1)} %get-tuple-element.43), channel_id=1, source_target_pairs={{1,0},{2,1},{3,2},{4,3},{5,4},{6,5},{7,6},{0,7},{9,8},{10,9},{11,1... | collective-permute-start | bytes 786440 | tf_op jit(solution)/shard_map/ppermute | solution.py:489
  75.9 14.4 %collective-permute-start.7 = (bf16[8,128,128]{2,1,0:T(8,128)(2,1)S(1)}, bf16[8,128,128]{2,1,0:T(8,128)(2,1)S(1)}, u32[]{:S(2)}, u32[]{:S(2)}) collective-permute-start(bf16[8,128,128]{2,1,0:T(8,128)(2,1)S(1)} %get-tuple-element.38), channel_id=1, source_target_pairs={{0,1},{1,2},{2,3},{3,4},{4,5},{5,6},{6,7},{7,0},{8,9},{9,10},{10,1... | collective-permute-start | bytes 786440 | tf_op jit(solution)/shard_map/ppermute | solution.py:489
  75.9 19.4 %collective-permute-start.8 = (bf16[8,128,128]{2,1,0:T(8,128)(2,1)S(1)}, bf16[8,128,128]{2,1,0:T(8,128)(2,1)S(1)}, u32[]{:S(2)}, u32[]{:S(2)}) collective-permute-start(bf16[8,128,128]{2,1,0:T(8,128)(2,1)S(1)} %get-tuple-element.37), channel_id=1, source_target_pairs={{1,0},{2,1},{3,2},{4,3},{5,4},{6,5},{7,6},{0,7},{9,8},{10,9},{11,1... | collective-permute-start | bytes 786440 | tf_op jit(solution)/shard_map/ppermute | solution.py:489
  83.4 14.7 %collective-permute-start.3 = (bf16[8,128,128]{2,1,0:T(8,128)(2,1)S(1)}, bf16[8,128,128]{2,1,0:T(8,128)(2,1)S(1)}, u32[]{:S(2)}, u32[]{:S(2)}) collective-permute-start(bf16[8,128,128]{2,1,0:T(8,128)(2,1)S(1)} %get-tuple-element.42), channel_id=1, source_target_pairs={{0,1},{1,2},{2,3},{3,4},{4,5},{5,6},{6,7},{7,0},{8,9},{9,10},{10,1... | collective-permute-start | bytes 786440 | tf_op jit(solution)/shard_map/ppermute | solution.py:489
  83.4 16.3 %collective-permute-start.4 = (bf16[8,128,128]{2,1,0:T(8,128)(2,1)S(1)}, bf16[8,128,128]{2,1,0:T(8,128)(2,1)S(1)}, u32[]{:S(2)}, u32[]{:S(2)}) collective-permute-start(bf16[8,128,128]{2,1,0:T(8,128)(2,1)S(1)} %get-tuple-element.41), channel_id=1, source_target_pairs={{1,0},{2,1},{3,2},{4,3},{5,4},{6,5},{7,6},{0,7},{9,8},{10,9},{11,1... | collective-permute-start | bytes 786440 | tf_op jit(solution)/shard_map/ppermute | solution.py:489

commit v5 on v4

--- a/solution.py
+++ b/solution.py
@@ -37,7 +37,6 @@
     features, w_first, dest_part, dest_slot, b_first, w_second, b_second = held
     embedded, packed, arrival, leaving = refs[16:]
     room, direct, aligned = sizes
-    own = room - 1
     copies = [
         pltpu.make_async_copy(source, kept, arrival.at[index])
         for index, (source, kept) in enumerate(zip(given, held))
@@ -67,9 +66,9 @@
     for at in range(0, parts, 2 * mate):
         swapped += [counts[at + mate : at + 2 * mate], counts[at : at + mate]]
     free = (jnp.concatenate(swapped, axis=0) <= direct).astype(F32)
-    crowded = jnp.max(jnp.where(counts > own, 1.0 - free, 0.0), axis=0, keepdims=True)
+    crowded = jnp.max(jnp.where(counts > room, 1.0 - free, 0.0), axis=0, keepdims=True)
     mate_free = jnp.sum(onehot * free, axis=0, keepdims=True) > 0.5
-    over = position - own
+    over = position - room
     other = jnp.bitwise_xor(part, mate) * room + direct + over
     target = jnp.where(over < 0, part * room + position, jnp.where(mate_free, other, -1))
 
@@ -105,7 +104,7 @@
     size = DESTS * room
     halves = width // LANES
     slot = iota((size, count), 0)
-    last = iota((DESTS, room, LANES), 1) == own
+    leads = iota((DESTS, PIECE, LANES), 1) == 0
     sends = [keep]
     for group in range(parts // DESTS):
         select = (slot == target - group * size).astype(BF16)
@@ -114,11 +113,10 @@
         head, tail = [], []
         for half in range(halves):
             piece = moved[:, half * LANES : (half + 1) * LANES].reshape(DESTS, room, LANES)
-            if half == 0:
-                piece = jnp.where(last, coded[dests][:, None, :], piece)
             head.append(piece[:, :aligned])
             tail.append(piece[:, aligned:])
-        packed[dests] = jnp.concatenate(head + tail, axis=1).astype(BF16)
+        codes = jnp.where(leads, coded[dests][:, None, :], 0.0)
+        packed[dests] = jnp.concatenate(head + tail + [codes], axis=1).astype(BF16)
         sends.append(pltpu.make_async_copy(packed.at[dests], out.at[dests], leaving.at[group]))
         sends[-1].start()
     for send in sends:
@@ -130,7 +128,7 @@
 ):
     rows, depth = features.shape
     hidden, width = w_second.shape
-    length = (width // LANES) * sizes[0]
+    length = (width // LANES) * sizes[0] + PIECE
     given = features, w_first, part, slot, b_first, w_second, b_second
     hbm = pl.BlockSpec(memory_space=pl.ANY)
     return pl.pallas_call(
@@ -181,7 +179,7 @@
                     axis=1,
                 )
             )
-        code = fields[0][:, room - 1, :]
+        code = got[:, halves * room, :]
         power = jnp.zeros_like(code)
         for bit in POWERS:
             big = code >= 128.0 * 2.0**bit
@@ -422,7 +420,7 @@
     earlier = (row[None, :] < row[:, None]).astype(BF16)
     before = jnp.dot(earlier, onehot, preferred_element_type=F32)
     position = jnp.sum(before * onehot.astype(F32), axis=1).astype(jnp.int32)
-    over = position - (room - 1)
+    over = position - room
     target = jnp.where(over < 0, -1, dest_part * shared + direct - aligned + over)
     select = (jnp.arange(parts * shared, dtype=jnp.int32)[:, None] == target[None, :]).astype(BF16)
     moved = jnp.dot(select, embedded, preferred_element_type=F32).astype(BF16)
@@ -449,8 +447,8 @@
     capacity = 3 * row_count
     most = -(-capacity // parts)
     room = -(-3 * most // 32) * 8
-    direct = 2 * (room - 1) - most
-    sizes = room, direct, direct // 8 * 8
+    direct = 2 * room - most
+    sizes = room, direct, min(direct // 8 * 8, room - 8)
     width = w_second.shape[1]
     halves = width // LANES
     block_rows = tile_values.shape[1]
@@ -468,10 +466,9 @@
         dest_slot,
     )
     arrived = all_to_all(outgoing)
-    codes = halves * sizes[2] + (room - sizes[2]) - 1
-    crowded = jnp.any(arrived[:, codes, FLAG] > 0.5)
+    crowded = jnp.any(arrived[:, halves * room, FLAG] > 0.5)
     from_mate = lax.ppermute(
-        arrived[:, halves * sizes[2] :, :],
+        arrived[:, halves * sizes[2] : halves * room, :],
         "dp",
         [(i, i ^ 1) for i in range(count_dp)],
     )

time: 103 us -> 104 us (level)
  waiting for transfers between devices: 15.4 us -> 10.8 us
  Pallas kernels: 27.7 us -> 32.2 us
  blocking collectives: 37.7 us -> 39.1 us
    ppermute x4, waiting for transfers between devices: 11.1 us -> 4.77 us  [exchange(): lax.ppermute(send[1], 'dom', backward)]
    pallas_call x1, Pallas kernels: 3.37 us -> 6 us  [place(): pl.pallas_call(functools.partial(place_kernel, sizes, halves), out_shape=...]
    ppermute x4, waiting for transfers between devices: 3.98 us -> 5.92 us  [exchange(): lax.ppermute(send[0], 'dom', forward)]
    pallas_call x1, Pallas kernels: 2.58 us -> 4.36 us  [listed_blocks(): pl.pallas_call(functools.partial(listed_kernel, sizes, halves), out_shape...]
    ppermute x4, starting transfers between devices: 1.33 us -> 2.85 us  [exchange(): lax.ppermute(send[0], 'dom', forward)]
    ppermute x4, starting transfers between devices: 17.7 us -> 16.2 us  [exchange(): lax.ppermute(send[1], 'dom', backward)]
    all_to_all x1, blocking collectives: 37.7 us -> 39.1 us  [all_to_all(): lax.all_to_all(payload, ('dp', 'dom'), split_axis=0, concat_axis=0, tiled...]
  transfers between devices with their start and end apart: 9 -> 9, of which waited for: 6 -> 6; matrix products, arithmetic and copies ran while one was open for 1% -> 1% of each run, Pallas kernels for 14% -> 16%
where the time goes in v5:
time: 104 us
  blocking collectives  39.1 us (38%)
  Pallas kernels  32.2 us (31%)
  starting transfers between devices  19.1 us (18%)
  waiting for transfers between devices  10.8 us (10%)
  between operations  1.04 us (1%)
    all_to_all x1, blocking collectives, all_to_all(): lax.all_to_all(payload, ('dp', 'dom'), split_axis=0, concat_axis=0, tiled...  39.1 us
    ppermute x4, starting transfers between devices, exchange(): lax.ppermute(send[1], 'dom', backward)  16.2 us
    pallas_call x4, Pallas kernels, outer(): pl.pallas_call(functools.partial(outer_kernel, half), out_shape=out_shape...  9.54 us
    pallas_call x1, Pallas kernels, project(): pl.pallas_call(functools.partial(project_kernel, parts, mate, sizes), out...  8.11 us
    pallas_call x1, Pallas kernels, place(): pl.pallas_call(functools.partial(place_kernel, sizes, halves), out_shape=...  6 us
    ppermute x4, waiting for transfers between devices, exchange(): lax.ppermute(send[0], 'dom', forward)  5.92 us
    ppermute x4, waiting for transfers between devices, exchange(): lax.ppermute(send[1], 'dom', backward)  4.77 us
    pallas_call x1, Pallas kernels, listed_blocks(): pl.pallas_call(functools.partial(listed_kernel, sizes, halves), out_shape...  4.36 us
  transfers between devices with their start and end apart: 9, of which 6 were waited for; matrix products, arithmetic and copies ran while one was open for 1% of the time, Pallas kernels for 16%

profile of v5, /device:TPU:0, one launch (start us, length us, event | category | flops | bytes accessed | tf_op | source)
XLA Modules:
  0.0 104.0 jit_solution(9839097133970685174)
XLA Ops:
  0.0 8.1 %project.1 = (bf16[32,152,128]{2,1,0:T(8,128)(2,1)}, bf16[1024,256]{1,0:T(8,128)(2,1)S(1)}) custom-call(bf16[1024,1024]{1,0:T(8,128)(2,1)} %refs_0_.5, bf16[1024,1024]{1,0:T(8,128)(2,1)} %refs_1_.1, s32[1024]{0:T(1024)} %refs_2_.1, s32[1024]{0:T(1024)} %refs_3_.1, bf16[1024]{0:T(1024)(128)(2,1)} %refs_4_.1, bf16[1024,256]{1,0:T(8,128)(2,1)} %refs_5_.1, ...), custom_call_target="tpu_custom_call" | custom-call | flops 2684354560 | bytes 8388608 | tf_op jit(solution)/shard_map/project/pallas_call | solution.py:134
  8.1 0.0 copy-start.3
  8.1 0.0 copy-start.2
  8.1 39.1 %all_to_all.10.arrived = bf16[32,152,128]{2,1,0:T(8,128)(2,1)S(1)} all-to-all(bf16[32,152,128]{2,1,0:T(8,128)(2,1)} %get-tuple-element.26), channel_id=1, replica_groups=mesh['dp'=4,'dom'=8] {'dp','dom'}, dimensions={0} | all-to-all | bytes 2490368 | tf_op jit(solution)/shard_map/all_to_all | solution.py:411
  47.3 0.1 collective-permute-start
  47.4 0.0 copy-done.3
  47.4 0.1 copy.15
  47.5 0.1 reshape.13.coords.refs_1_
  47.6 0.7 compare_reduce_fusion
  49.0 0.0 copy-done.2
  49.0 0.0 copy-start.1
  49.0 0.1 collective-permute-done
  49.1 0.6 copy-done.1
  49.7 4.4 %listed.1 = (bf16[2,8,128,128]{3,2,1,0:T(8,128)(2,1)S(1)}, bf16[2,8,128,128]{3,2,1,0:T(8,128)(2,1)S(1)}) custom-call(bf16[32,152,128]{2,1,0:T(8,128)(2,1)S(1)} %all_to_all.10.arrived, bf16[32,48,128]{2,1,0:T(8,128)(2,1)S(1)} %get-tuple-element.45.extra, s32[2,8]{1,0:T(2,128)S(1)} %bitcast.20), custom_call_target="tpu_custom_call" | custom-call | flops 3221225472 | bytes 4194304 | tf_op jit(solution)/shard_map/listed/pallas_call | solution.py:257
  54.1 0.1 collective-permute-start.5
  54.2 4.7 %collective-permute-start.6 = (bf16[8,128,128]{2,1,0:T(8,128)(2,1)S(1)}, bf16[8,128,128]{2,1,0:T(8,128)(2,1)S(1)}, u32[]{:S(2)}, u32[]{:S(2)}) collective-permute-start(bf16[8,128,128]{2,1,0:T(8,128)(2,1)S(1)} %get-tuple-element.39), channel_id=1, source_target_pairs={{1,0},{2,1},{3,2},{4,3},{5,4},{6,5},{7,6},{0,7},{9,8},{10,9},{11,1... | collective-permute-start | bytes 786440 | tf_op jit(solution)/shard_map/ppermute | solution.py:486
  58.9 0.1 collective-permute-start.1
  59.0 0.0 copy-start
  59.0 4.7 %collective-permute-start.2 = (bf16[8,128,128]{2,1,0:T(8,128)(2,1)S(1)}, bf16[8,128,128]{2,1,0:T(8,128)(2,1)S(1)}, u32[]{:S(2)}, u32[]{:S(2)}) collective-permute-start(bf16[8,128,128]{2,1,0:T(8,128)(2,1)S(1)} %get-tuple-element.43), channel_id=1, source_target_pairs={{1,0},{2,1},{3,2},{4,3},{5,4},{6,5},{7,6},{0,7},{9,8},{10,9},{11,1... | collective-permute-start | bytes 786440 | tf_op jit(solution)/shard_map/ppermute | solution.py:486
  63.7 6.0 %place.1 = (s32[1]{0:T(128)}, bf16[24,128,128]{2,1,0:T(8,128)(2,1)S(1)}, bf16[24,128,128]{2,1,0:T(8,128)(2,1)S(1)}) custom-call(bf16[32,152,128]{2,1,0:T(8,128)(2,1)S(1)} %all_to_all.10.arrived, bf16[32,48,128]{2,1,0:T(8,128)(2,1)S(1)} %get-tuple-element.45.extra), custom_call_target="tpu_custom_call" | custom-call | flops 4831838208 | bytes 4194304 | tf_op jit(solution)/shard_map/place/pallas_call | solution.py:274
  69.7 0.0 copy-done
  69.7 1.0 inner.6.refs_4_
  70.7 1.0 inner.4.refs_4_
  71.8 0.3 collective-permute-done.5.refs_5_
  72.1 2.6 %collective-permute-done.6.refs_6_ = bf16[8,128,128]{2,1,0:T(8,128)(2,1)S(1)} collective-permute-done((bf16[8,128,128]{2,1,0:T(8,128)(2,1)S(1)}, bf16[8,128,128]{2,1,0:T(8,128)(2,1)S(1)}, u32[]{:S(2)}, u32[]{:S(2)}) %collective-permute-start.6) | collective-permute-done | bytes 262176 | tf_op jit(solution)/shard_map/ppermute | solution.py:486
  74.7 2.0 %outer.5 = (bf16[24,128,128]{2,1,0:T(8,128)(2,1)S(1)}, bf16[2,8,128,128]{3,2,1,0:T(8,128)(2,1)S(1)}) custom-call(bf16[48,128,128]{2,1,0:T(8,128)(2,1)S(1)} %copy-done, s32[96]{0:T(128)S(1)} %reshape.13.coords.refs_1_, s32[2,8]{1,0:T(2,128)S(1)} %bitcast.21, s32[1]{0:T(128)} %get-tuple-element.28.refs_3_, f32[24,128,128]{2,1,0:T(8,128)S(1)} %inner.6.refs_4_, ...), custom_call_target="tpu_custom_call" | custom-call | flops 100663296 | bytes 4194304 | tf_op jit(solution)/shard_map/outer/pallas_call | solution.py:395
  76.8 0.1 collective-permute-start.7
  76.8 4.7 %collective-permute-start.8 = (bf16[8,128,128]{2,1,0:T(8,128)(2,1)S(1)}, bf16[8,128,128]{2,1,0:T(8,128)(2,1)S(1)}, u32[]{:S(2)}, u32[]{:S(2)}) collective-permute-start(bf16[8,128,128]{2,1,0:T(8,128)(2,1)S(1)} %get-tuple-element.37), channel_id=1, source_target_pairs={{1,0},{2,1},{3,2},{4,3},{5,4},{6,5},{7,6},{0,7},{9,8},{10,9},{11,1... | collective-permute-start | bytes 786440 | tf_op jit(solution)/shard_map/ppermute | solution.py:486
  81.6 4.5 %collective-permute-done.1.refs_5_ = bf16[8,128,128]{2,1,0:T(8,128)(2,1)S(1)} collective-permute-done((bf16[8,128,128]{2,1,0:T(8,128)(2,1)S(1)}, bf16[8,128,128]{2,1,0:T(8,128)(2,1)S(1)}, u32[]{:S(2)}, u32[]{:S(2)}) %collective-permute-start.1) | collective-permute-done | bytes 262176 | tf_op jit(solution)/shard_map/ppermute | solution.py:486
  86.0 0.0 collective-permute-done.2.refs_6_
  86.0 2.0 %outer.4 = (bf16[24,128,128]{2,1,0:T(8,128)(2,1)S(1)}, bf16[2,8,128,128]{3,2,1,0:T(8,128)(2,1)S(1)}) custom-call(bf16[48,128,128]{2,1,0:T(8,128)(2,1)S(1)} %copy-done, s32[96]{0:T(128)S(1)} %reshape.13.coords.refs_1_, s32[2,8]{1,0:T(2,128)S(1)} %bitcast.22, s32[1]{0:T(128)} %get-tuple-element.28.refs_3_, f32[24,128,128]{2,1,0:T(8,128)S(1)} %inner.4.refs_4_, ...), custom_call_target="tpu_custom_call" | custom-call | flops 100663296 | bytes 4194304 | tf_op jit(solution)/shard_map/outer/pallas_call | solution.py:395
  88.1 2.7 %collective-permute-start.3 = (bf16[8,128,128]{2,1,0:T(8,128)(2,1)S(1)}, bf16[8,128,128]{2,1,0:T(8,128)(2,1)S(1)}, u32[]{:S(2)}, u32[]{:S(2)}) collective-permute-start(bf16[8,128,128]{2,1,0:T(8,128)(2,1)S(1)} %get-tuple-element.42), channel_id=1, source_target_pairs={{0,1},{1,2},{2,3},{3,4},{4,5},{5,6},{6,7},{7,0},{8,9},{9,10},{10,1... | collective-permute-start | bytes 786440 | tf_op jit(solution)/shard_map/ppermute | solution.py:486
  90.8 2.1 %collective-permute-start.4 = (bf16[8,128,128]{2,1,0:T(8,128)(2,1)S(1)}, bf16[8,128,128]{2,1,0:T(8,128)(2,1)S(1)}, u32[]{:S(2)}, u32[]{:S(2)}) collective-permute-start(bf16[8,128,128]{2,1,0:T(8,128)(2,1)S(1)} %get-tuple-element.41), channel_id=1, source_target_pairs={{1,0},{2,1},{3,2},{4,3},{5,4},{6,5},{7,6},{0,7},{9,8},{10,9},{11,1... | collective-permute-start | bytes 786440 | tf_op jit(solution)/shard_map/ppermute | solution.py:486
  92.9 1.1 %inner.7.refs_4_ = f32[24,128,128]{2,1,0:T(8,128)S(1)} custom-call(bf16[48,128,128]{2,1,0:T(8,128)(2,1)S(1)} %copy-done, s32[96]{0:T(128)S(1)} %reshape.13.coords.refs_1_, bf16[24,128,128]{2,1,0:T(8,128)(2,1)S(1)} %get-tuple-element.33.start.current, bf16[24,128,128]{2,1,0:T(8,128)(2,1)S(1)} %get-tuple-element.35.current), custom_call_target="tpu_custom_call" | custom-call | flops 100663296 | bytes 4194304 | tf_op jit(solution)/shard_map/inner/pallas_call | solution.py:353
  94.0 1.0 inner.5.refs_4_
  95.0 0.0 collective-permute-done.7.refs_5_
  95.0 0.0 collective-permute-done.8.refs_6_
  95.0 2.7 %outer.6.refs_7_ = bf16[3072,256]{1,0:T(8,128)(2,1)} custom-call(bf16[48,128,128]{2,1,0:T(8,128)(2,1)S(1)} %copy-done, s32[96]{0:T(128)S(1)} %reshape.13.coords.refs_1_, s32[2,8]{1,0:T(2,128)S(1)} %bitcast.23, s32[1]{0:T(128)} %get-tuple-element.28.refs_3_, f32[24,128,128]{2,1,0:T(8,128)S(1)} %inner.7.refs_4_, ...), custom_call_target="tpu_custom_call" | custom-call | flops 100663296 | bytes 4194304 | tf_op jit(solution)/shard_map/outer/pallas_call | solution.py:395
  97.8 1.1 %collective-permute-done.3.refs_5_ = bf16[8,128,128]{2,1,0:T(8,128)(2,1)S(1)} collective-permute-done((bf16[8,128,128]{2,1,0:T(8,128)(2,1)S(1)}, bf16[8,128,128]{2,1,0:T(8,128)(2,1)S(1)}, u32[]{:S(2)}, u32[]{:S(2)}) %collective-permute-start.3) | collective-permute-done | bytes 262176 | tf_op jit(solution)/shard_map/ppermute | solution.py:486
  98.9 2.2 %collective-permute-done.4.refs_6_ = bf16[8,128,128]{2,1,0:T(8,128)(2,1)S(1)} collective-permute-done((bf16[8,128,128]{2,1,0:T(8,128)(2,1)S(1)}, bf16[8,128,128]{2,1,0:T(8,128)(2,1)S(1)}, u32[]{:S(2)}, u32[]{:S(2)}) %collective-permute-start.4) | collective-permute-done | bytes 262176 | tf_op jit(solution)/shard_map/ppermute | solution.py:486
  101.1 2.7 %outer.7 = bf16[3072,256]{1,0:T(8,128)(2,1)} custom-call(bf16[48,128,128]{2,1,0:T(8,128)(2,1)S(1)} %copy-done, s32[96]{0:T(128)S(1)} %reshape.13.coords.refs_1_, s32[2,8]{1,0:T(2,128)S(1)} %bitcast.24, s32[1]{0:T(128)} %get-tuple-element.28.refs_3_, f32[24,128,128]{2,1,0:T(8,128)S(1)} %inner.5.refs_4_, ...), custom_call_target="tpu_custom_call", output_to_operand_aliasing={{}: (7, {})} | custom-call | flops 100663296 | bytes 4194304 | tf_op jit(solution)/shard_map/outer/pallas_call | solution.py:395
  (6 shorter events, 0.2 us)
Async XLA Ops:
  8.1 39.2 %copy-start.3 = (s32[48,2]{0,1:T(2,128)S(1)}, s32[48,2]{0,1:T(2,128)}, u32[]{:S(2)}) copy-start(s32[48,2]{0,1:T(2,128)} %param.19) | copy-start | bytes 1156
  8.1 40.9 %copy-start.2 = (s32[1024]{0:T(1024)S(1)}, s32[1024]{0:T(1024)}, u32[]{:S(2)}) copy-start(s32[1024]{0:T(1024)} %refs_2_.1) | copy-start | bytes 12292
  47.3 1.8 %collective-permute-start = (bf16[32,48,128]{2,1,0:T(8,128)(2,1)S(1)}, bf16[32,48,128]{2,1,0:T(8,128)(2,1)S(1)}, u32[]{:S(2)}, u32[]{:S(2)}) collective-permute-start(bf16[32,48,128]{2,1,0:T(8,128)(2,1)S(1)} %slice.41), channel_id=1, source_target_pairs={{0,8},{8,0},{16,24},{24,16},{1,9},{9,1},{17,25},{25,17},{2,10},{10... | collective-permute-start | bytes 1179656 | tf_op jit(solution)/shard_map/ppermute | solution.py:470
  49.0 0.7 copy-start.1
  54.1 18.0 %collective-permute-start.5 = (bf16[8,128,128]{2,1,0:T(8,128)(2,1)S(1)}, bf16[8,128,128]{2,1,0:T(8,128)(2,1)S(1)}, u32[]{:S(2)}, u32[]{:S(2)}) collective-permute-start(bf16[8,128,128]{2,1,0:T(8,128)(2,1)S(1)} %get-tuple-element.40), channel_id=1, source_target_pairs={{0,1},{1,2},{2,3},{3,4},{4,5},{5,6},{6,7},{7,0},{8,9},{9,10},{10,1... | collective-permute-start | bytes 786440 | tf_op jit(solution)/shard_map/ppermute | solution.py:486
  54.2 20.5 %collective-permute-start.6 = (bf16[8,128,128]{2,1,0:T(8,128)(2,1)S(1)}, bf16[8,128,128]{2,1,0:T(8,128)(2,1)S(1)}, u32[]{:S(2)}, u32[]{:S(2)}) collective-permute-start(bf16[8,128,128]{2,1,0:T(8,128)(2,1)S(1)} %get-tuple-element.39), channel_id=1, source_target_pairs={{1,0},{2,1},{3,2},{4,3},{5,4},{6,5},{7,6},{0,7},{9,8},{10,9},{11,1... | collective-permute-start | bytes 786440 | tf_op jit(solution)/shard_map/ppermute | solution.py:486
  58.9 27.1 %collective-permute-start.1 = (bf16[8,128,128]{2,1,0:T(8,128)(2,1)S(1)}, bf16[8,128,128]{2,1,0:T(8,128)(2,1)S(1)}, u32[]{:S(2)}, u32[]{:S(2)}) collective-permute-start(bf16[8,128,128]{2,1,0:T(8,128)(2,1)S(1)} %get-tuple-element.44), channel_id=1, source_target_pairs={{0,1},{1,2},{2,3},{3,4},{4,5},{5,6},{6,7},{7,0},{8,9},{9,10},{10,1... | collective-permute-start | bytes 786440 | tf_op jit(solution)/shard_map/ppermute | solution.py:486
  59.0 10.7 %copy-start = (bf16[48,128,128]{2,1,0:T(8,128)(2,1)S(1)}, bf16[48,128,128]{2,1,0:T(8,128)(2,1)}, u32[]{:S(2)}) copy-start(bf16[48,128,128]{2,1,0:T(8,128)(2,1)} %refs_0_.9) | copy-start | bytes 4718596
  59.0 27.0 %collective-permute-start.2 = (bf16[8,128,128]{2,1,0:T(8,128)(2,1)S(1)}, bf16[8,128,128]{2,1,0:T(8,128)(2,1)S(1)}, u32[]{:S(2)}, u32[]{:S(2)}) collective-permute-start(bf16[8,128,128]{2,1,0:T(8,128)(2,1)S(1)} %get-tuple-element.43), channel_id=1, source_target_pairs={{1,0},{2,1},{3,2},{4,3},{5,4},{6,5},{7,6},{0,7},{9,8},{10,9},{11,1... | collective-permute-start | bytes 786440 | tf_op jit(solution)/shard_map/ppermute | solution.py:486
  76.8 18.2 %collective-permute-start.7 = (bf16[8,128,128]{2,1,0:T(8,128)(2,1)S(1)}, bf16[8,128,128]{2,1,0:T(8,128)(2,1)S(1)}, u32[]{:S(2)}, u32[]{:S(2)}) collective-permute-start(bf16[8,128,128]{2,1,0:T(8,128)(2,1)S(1)} %get-tuple-element.38), channel_id=1, source_target_pairs={{0,1},{1,2},{2,3},{3,4},{4,5},{5,6},{6,7},{7,0},{8,9},{9,10},{10,1... | collective-permute-start | bytes 786440 | tf_op jit(solution)/shard_map/ppermute | solution.py:486
  76.8 18.2 %collective-permute-start.8 = (bf16[8,128,128]{2,1,0:T(8,128)(2,1)S(1)}, bf16[8,128,128]{2,1,0:T(8,128)(2,1)S(1)}, u32[]{:S(2)}, u32[]{:S(2)}) collective-permute-start(bf16[8,128,128]{2,1,0:T(8,128)(2,1)S(1)} %get-tuple-element.37), channel_id=1, source_target_pairs={{1,0},{2,1},{3,2},{4,3},{5,4},{6,5},{7,6},{0,7},{9,8},{10,9},{11,1... | collective-permute-start | bytes 786440 | tf_op jit(solution)/shard_map/ppermute | solution.py:486
  88.1 10.7 %collective-permute-start.3 = (bf16[8,128,128]{2,1,0:T(8,128)(2,1)S(1)}, bf16[8,128,128]{2,1,0:T(8,128)(2,1)S(1)}, u32[]{:S(2)}, u32[]{:S(2)}) collective-permute-start(bf16[8,128,128]{2,1,0:T(8,128)(2,1)S(1)} %get-tuple-element.42), channel_id=1, source_target_pairs={{0,1},{1,2},{2,3},{3,4},{4,5},{5,6},{6,7},{7,0},{8,9},{9,10},{10,1... | collective-permute-start | bytes 786440 | tf_op jit(solution)/shard_map/ppermute | solution.py:486
  90.8 10.3 %collective-permute-start.4 = (bf16[8,128,128]{2,1,0:T(8,128)(2,1)S(1)}, bf16[8,128,128]{2,1,0:T(8,128)(2,1)S(1)}, u32[]{:S(2)}, u32[]{:S(2)}) collective-permute-start(bf16[8,128,128]{2,1,0:T(8,128)(2,1)S(1)} %get-tuple-element.41), channel_id=1, source_target_pairs={{1,0},{2,1},{3,2},{4,3},{5,4},{6,5},{7,6},{0,7},{9,8},{10,9},{11,1... | collective-permute-start | bytes 786440 | tf_op jit(solution)/shard_map/ppermute | solution.py:486

commit v6 on v5

--- a/solution.py
+++ b/solution.py
@@ -293,11 +293,11 @@
         term = jnp.dot(tiles[b], current[b], preferred_element_type=F32)
         partial[b] = (1.0 - ALPHA) * term + ALPHA * start[b].astype(F32)
     for t in range(block_count + 2 * halo, tiles.shape[0]):
-        index = coords[2 * t + 1]
+        index = coords[1, t]
         source = current[jnp.minimum(index, block_count - 1)]
         source = jnp.where(index < block_count, source, jnp.zeros_like(source))
         term = jnp.dot(tiles[t], source, preferred_element_type=F32)
-        partial[coords[2 * t]] += (1.0 - ALPHA) * term
+        partial[coords[0, t]] += (1.0 - ALPHA) * term
 
 
 def outer_kernel(half, *refs):
@@ -315,7 +315,7 @@
         elif t < own + 2 * listed:
             source = high[t - own - listed]
         else:
-            index = coords[2 * t + 1]
+            index = coords[1, t]
             below = low[jnp.clip(index - own, 0, listed - 1)]
             above = high[jnp.clip(index - own - listed, 0, listed - 1)]
             source = jnp.where(index < own + listed, below, above)
@@ -323,7 +323,7 @@
         terms[t - own] = jnp.dot(tiles[t], source, preferred_element_type=F32)
     summed[...] = partial[...]
     for t in range(own, tiles.shape[0]):
-        summed[coords[2 * t]] += (1.0 - ALPHA) * terms[t - own]
+        summed[coords[0, t]] += (1.0 - ALPHA) * terms[t - own]
     row = iota((block_rows, width), 0)
     copies = []
     for b in range(block_count):
@@ -477,7 +477,7 @@
         lambda: all_to_all(late_rows(parts, sizes, embedded, dest_part)),
         lambda: from_mate,
     )
-    coords = tile_coords.reshape(-1)
+    coords = tile_coords.T
     lists = halo_send[0]
     forward = [(i, (i + 1) % count_dom) for i in range(count_dom)]
     backward = [((i + 1) % count_dom, i) for i in range(count_dom)]

time: 104 us -> 104 us (level)
  waiting for transfers between devices: 10.8 us -> 15.4 us
  Pallas kernels: 32.2 us -> 27.8 us
    pallas_call x1, Pallas kernels: 6 us -> 3.36 us  [place(): pl.pallas_call(functools.partial(place_kernel, sizes, halves), out_shape=...]
    ppermute x4, waiting for transfers between devices: 5.92 us -> 8.19 us  [exchange(): lax.ppermute(send[0], 'dom', forward)]
    ppermute x4, waiting for transfers between devices: 4.77 us -> 6.9 us  [exchange(): lax.ppermute(send[1], 'dom', backward)]
    pallas_call x1, Pallas kernels: 4.36 us -> 2.55 us  [listed_blocks(): pl.pallas_call(functools.partial(listed_kernel, sizes, halves), out_shape...]
    ppermute x4, starting transfers between devices: 2.85 us -> 1.29 us  [exchange(): lax.ppermute(send[0], 'dom', forward)]
    ppermute x4, starting transfers between devices: 16.2 us -> 17.8 us  [exchange(): lax.ppermute(send[1], 'dom', backward)]
  transfers between devices with their start and end apart: 9 -> 9, of which waited for: 6 -> 6; matrix products, arithmetic and copies ran while one was open for 1% -> 1% of each run, Pallas kernels for 16% -> 14%
where the time goes in v6:
time: 104 us
  blocking collectives  39.1 us (38%)
  Pallas kernels  27.8 us (27%)
  starting transfers between devices  19.1 us (18%)
  waiting for transfers between devices  15.4 us (15%)
    all_to_all x1, blocking collectives, all_to_all(): lax.all_to_all(payload, ('dp', 'dom'), split_axis=0, concat_axis=0, tiled...  39.1 us
    ppermute x4, starting transfers between devices, exchange(): lax.ppermute(send[1], 'dom', backward)  17.8 us
    pallas_call x4, Pallas kernels, outer(): pl.pallas_call(functools.partial(outer_kernel, half), out_shape=out_shape...  9.58 us
    ppermute x4, waiting for transfers between devices, exchange(): lax.ppermute(send[0], 'dom', forward)  8.19 us
    pallas_call x1, Pallas kernels, project(): pl.pallas_call(functools.partial(project_kernel, parts, mate, sizes), out...  8.11 us
    ppermute x4, waiting for transfers between devices, exchange(): lax.ppermute(send[1], 'dom', backward)  6.9 us
    pallas_call x4, Pallas kernels, inner(): pl.pallas_call(functools.partial(inner_kernel, halo), out_shape=jax.Shape...  4.18 us
    pallas_call x1, Pallas kernels, place(): pl.pallas_call(functools.partial(place_kernel, sizes, halves), out_shape=...  3.36 us
  transfers between devices with their start and end apart: 9, of which 6 were waited for; matrix products, arithmetic and copies ran while one was open for 1% of the time, Pallas kernels for 14%

profile of v6, /device:TPU:0, one launch (start us, length us, event | category | flops | bytes accessed | tf_op | source)
XLA Modules:
  0.0 103.7 jit_solution(9049104016719841223)
XLA Ops:
  0.0 8.1 %project.1 = (bf16[32,152,128]{2,1,0:T(8,128)(2,1)}, bf16[1024,256]{1,0:T(8,128)(2,1)S(1)}) custom-call(bf16[1024,1024]{1,0:T(8,128)(2,1)} %refs_0_.5, bf16[1024,1024]{1,0:T(8,128)(2,1)} %refs_1_.1, s32[1024]{0:T(1024)} %refs_2_.1, s32[1024]{0:T(1024)} %refs_3_.1, bf16[1024]{0:T(1024)(128)(2,1)} %refs_4_.1, bf16[1024,256]{1,0:T(8,128)(2,1)} %refs_5_.1, ...), custom_call_target="tpu_custom_call" | custom-call | flops 2684354560 | bytes 8388608 | tf_op jit(solution)/shard_map/project/pallas_call | solution.py:134
  8.1 0.0 copy-start.3
  8.1 39.1 %all_to_all.10.arrived = bf16[32,152,128]{2,1,0:T(8,128)(2,1)S(1)} all-to-all(bf16[32,152,128]{2,1,0:T(8,128)(2,1)} %get-tuple-element.26), channel_id=1, replica_groups=mesh['dp'=4,'dom'=8] {'dp','dom'}, dimensions={0} | all-to-all | bytes 2490368 | tf_op jit(solution)/shard_map/all_to_all | solution.py:411
  47.3 0.1 collective-permute-start
  47.4 0.7 compare_reduce_fusion
  48.7 0.0 copy-done.3
  48.8 0.0 copy-start.2
  48.8 0.3 collective-permute-done
  49.1 0.4 copy-done.2
  49.4 2.5 %listed.1 = (bf16[2,8,128,128]{3,2,1,0:T(8,128)(2,1)S(1)}, bf16[2,8,128,128]{3,2,1,0:T(8,128)(2,1)S(1)}) custom-call(bf16[32,152,128]{2,1,0:T(8,128)(2,1)S(1)} %all_to_all.10.arrived, bf16[32,48,128]{2,1,0:T(8,128)(2,1)S(1)} %get-tuple-element.45.extra, s32[2,8]{1,0:T(2,128)S(1)} %bitcast.29), custom_call_target="tpu_custom_call" | custom-call | flops 3221225472 | bytes 4194304 | tf_op jit(solution)/shard_map/listed/pallas_call | solution.py:257
  52.0 1.1 %collective-permute-start.5 = (bf16[8,128,128]{2,1,0:T(8,128)(2,1)S(1)}, bf16[8,128,128]{2,1,0:T(8,128)(2,1)S(1)}, u32[]{:S(2)}, u32[]{:S(2)}) collective-permute-start(bf16[8,128,128]{2,1,0:T(8,128)(2,1)S(1)} %get-tuple-element.40), channel_id=1, source_target_pairs={{0,1},{1,2},{2,3},{3,4},{4,5},{5,6},{6,7},{7,0},{8,9},{9,10},{10,1... | collective-permute-start | bytes 786440 | tf_op jit(solution)/shard_map/ppermute | solution.py:486
  53.1 3.7 %collective-permute-start.6 = (bf16[8,128,128]{2,1,0:T(8,128)(2,1)S(1)}, bf16[8,128,128]{2,1,0:T(8,128)(2,1)S(1)}, u32[]{:S(2)}, u32[]{:S(2)}) collective-permute-start(bf16[8,128,128]{2,1,0:T(8,128)(2,1)S(1)} %get-tuple-element.39), channel_id=1, source_target_pairs={{1,0},{2,1},{3,2},{4,3},{5,4},{6,5},{7,6},{0,7},{9,8},{10,9},{11,1... | collective-permute-start | bytes 786440 | tf_op jit(solution)/shard_map/ppermute | solution.py:486
  56.9 0.1 collective-permute-start.1
  56.9 0.0 copy-start
  56.9 0.0 copy-start.1
  56.9 4.7 %collective-permute-start.2 = (bf16[8,128,128]{2,1,0:T(8,128)(2,1)S(1)}, bf16[8,128,128]{2,1,0:T(8,128)(2,1)S(1)}, u32[]{:S(2)}, u32[]{:S(2)}) collective-permute-start(bf16[8,128,128]{2,1,0:T(8,128)(2,1)S(1)} %get-tuple-element.43), channel_id=1, source_target_pairs={{1,0},{2,1},{3,2},{4,3},{5,4},{6,5},{7,6},{0,7},{9,8},{10,9},{11,1... | collective-permute-start | bytes 786440 | tf_op jit(solution)/shard_map/ppermute | solution.py:486
  61.6 3.4 %place.1 = (s32[1]{0:T(128)}, bf16[24,128,128]{2,1,0:T(8,128)(2,1)S(1)}, bf16[24,128,128]{2,1,0:T(8,128)(2,1)S(1)}) custom-call(bf16[32,152,128]{2,1,0:T(8,128)(2,1)S(1)} %all_to_all.10.arrived, bf16[32,48,128]{2,1,0:T(8,128)(2,1)S(1)} %get-tuple-element.45.extra), custom_call_target="tpu_custom_call" | custom-call | flops 4831838208 | bytes 4194304 | tf_op jit(solution)/shard_map/place/pallas_call | solution.py:274
  65.0 0.0 copy-done
  65.0 0.0 copy-done.1
  65.0 1.0 %inner.6.refs_4_ = f32[24,128,128]{2,1,0:T(8,128)S(1)} custom-call(bf16[48,128,128]{2,1,0:T(8,128)(2,1)S(1)} %copy-done, s32[2,48]{1,0:T(2,128)S(1)} %bitcast.21, bf16[24,128,128]{2,1,0:T(8,128)(2,1)S(1)} %get-tuple-element.33.start.current, bf16[24,128,128]{2,1,0:T(8,128)(2,1)S(1)} %get-tuple-element.33.start.current), custom_call_target="tpu_custom_call" | custom-call | flops 100663296 | bytes 4194304 | tf_op jit(solution)/shard_map/inner/pallas_call | solution.py:353
  66.1 1.0 %inner.4.refs_4_ = f32[24,128,128]{2,1,0:T(8,128)S(1)} custom-call(bf16[48,128,128]{2,1,0:T(8,128)(2,1)S(1)} %copy-done, s32[2,48]{1,0:T(2,128)S(1)} %bitcast.22, bf16[24,128,128]{2,1,0:T(8,128)(2,1)S(1)} %get-tuple-element.29.start.current, bf16[24,128,128]{2,1,0:T(8,128)(2,1)S(1)} %get-tuple-element.29.start.current), custom_call_target="tpu_custom_call" | custom-call | flops 100663296 | bytes 4194304 | tf_op jit(solution)/shard_map/inner/pallas_call | solution.py:353
  67.1 3.9 %collective-permute-done.5.refs_5_ = bf16[8,128,128]{2,1,0:T(8,128)(2,1)S(1)} collective-permute-done((bf16[8,128,128]{2,1,0:T(8,128)(2,1)S(1)}, bf16[8,128,128]{2,1,0:T(8,128)(2,1)S(1)}, u32[]{:S(2)}, u32[]{:S(2)}) %collective-permute-start.5) | collective-permute-done | bytes 262176 | tf_op jit(solution)/shard_map/ppermute | solution.py:486
  71.0 2.5 %collective-permute-done.6.refs_6_ = bf16[8,128,128]{2,1,0:T(8,128)(2,1)S(1)} collective-permute-done((bf16[8,128,128]{2,1,0:T(8,128)(2,1)S(1)}, bf16[8,128,128]{2,1,0:T(8,128)(2,1)S(1)}, u32[]{:S(2)}, u32[]{:S(2)}) %collective-permute-start.6) | collective-permute-done | bytes 262176 | tf_op jit(solution)/shard_map/ppermute | solution.py:486
  73.5 2.0 %outer.5 = (bf16[24,128,128]{2,1,0:T(8,128)(2,1)S(1)}, bf16[2,8,128,128]{3,2,1,0:T(8,128)(2,1)S(1)}) custom-call(bf16[48,128,128]{2,1,0:T(8,128)(2,1)S(1)} %copy-done, s32[2,48]{1,0:T(2,128)S(1)} %bitcast.23, s32[2,8]{1,0:T(2,128)S(1)} %bitcast.30, s32[1]{0:T(128)} %get-tuple-element.28.refs_3_, f32[24,128,128]{2,1,0:T(8,128)S(1)} %inner.6.refs_4_, ...), custom_call_target="tpu_custom_call" | custom-call | flops 100663296 | bytes 4194304 | tf_op jit(solution)/shard_map/outer/pallas_call | solution.py:395
  75.6 0.1 collective-permute-start.7
  75.7 4.7 %collective-permute-start.8 = (bf16[8,128,128]{2,1,0:T(8,128)(2,1)S(1)}, bf16[8,128,128]{2,1,0:T(8,128)(2,1)S(1)}, u32[]{:S(2)}, u32[]{:S(2)}) collective-permute-start(bf16[8,128,128]{2,1,0:T(8,128)(2,1)S(1)} %get-tuple-element.37), channel_id=1, source_target_pairs={{1,0},{2,1},{3,2},{4,3},{5,4},{6,5},{7,6},{0,7},{9,8},{10,9},{11,1... | collective-permute-start | bytes 786440 | tf_op jit(solution)/shard_map/ppermute | solution.py:486
  80.4 0.0 collective-permute-done.1.refs_5_
  80.4 0.0 collective-permute-done.2.refs_6_
  80.4 2.0 %outer.4 = (bf16[24,128,128]{2,1,0:T(8,128)(2,1)S(1)}, bf16[2,8,128,128]{3,2,1,0:T(8,128)(2,1)S(1)}) custom-call(bf16[48,128,128]{2,1,0:T(8,128)(2,1)S(1)} %copy-done, s32[2,48]{1,0:T(2,128)S(1)} %bitcast.24, s32[2,8]{1,0:T(2,128)S(1)} %bitcast.31, s32[1]{0:T(128)} %get-tuple-element.28.refs_3_, f32[24,128,128]{2,1,0:T(8,128)S(1)} %inner.4.refs_4_, ...), custom_call_target="tpu_custom_call" | custom-call | flops 100663296 | bytes 4194304 | tf_op jit(solution)/shard_map/outer/pallas_call | solution.py:395
  82.5 0.1 collective-permute-start.3
  82.6 4.7 %collective-permute-start.4 = (bf16[8,128,128]{2,1,0:T(8,128)(2,1)S(1)}, bf16[8,128,128]{2,1,0:T(8,128)(2,1)S(1)}, u32[]{:S(2)}, u32[]{:S(2)}) collective-permute-start(bf16[8,128,128]{2,1,0:T(8,128)(2,1)S(1)} %get-tuple-element.41), channel_id=1, source_target_pairs={{1,0},{2,1},{3,2},{4,3},{5,4},{6,5},{7,6},{0,7},{9,8},{10,9},{11,1... | collective-permute-start | bytes 786440 | tf_op jit(solution)/shard_map/ppermute | solution.py:486
  87.3 1.1 %inner.7.refs_4_ = f32[24,128,128]{2,1,0:T(8,128)S(1)} custom-call(bf16[48,128,128]{2,1,0:T(8,128)(2,1)S(1)} %copy-done, s32[2,48]{1,0:T(2,128)S(1)} %bitcast.25, bf16[24,128,128]{2,1,0:T(8,128)(2,1)S(1)} %get-tuple-element.33.start.current, bf16[24,128,128]{2,1,0:T(8,128)(2,1)S(1)} %get-tuple-element.35.current), custom_call_target="tpu_custom_call" | custom-call | flops 100663296 | bytes 4194304 | tf_op jit(solution)/shard_map/inner/pallas_call | solution.py:353
  88.4 1.0 %inner.5.refs_4_ = f32[24,128,128]{2,1,0:T(8,128)S(1)} custom-call(bf16[48,128,128]{2,1,0:T(8,128)(2,1)S(1)} %copy-done, s32[2,48]{1,0:T(2,128)S(1)} %bitcast.26, bf16[24,128,128]{2,1,0:T(8,128)(2,1)S(1)} %get-tuple-element.29.start.current, bf16[24,128,128]{2,1,0:T(8,128)(2,1)S(1)} %get-tuple-element.31.current), custom_call_target="tpu_custom_call" | custom-call | flops 100663296 | bytes 4194304 | tf_op jit(solution)/shard_map/inner/pallas_call | solution.py:353
  89.4 4.3 %collective-permute-done.7.refs_5_ = bf16[8,128,128]{2,1,0:T(8,128)(2,1)S(1)} collective-permute-done((bf16[8,128,128]{2,1,0:T(8,128)(2,1)S(1)}, bf16[8,128,128]{2,1,0:T(8,128)(2,1)S(1)}, u32[]{:S(2)}, u32[]{:S(2)}) %collective-permute-start.7) | collective-permute-done | bytes 262176 | tf_op jit(solution)/shard_map/ppermute | solution.py:486
  93.7 2.5 %collective-permute-done.8.refs_6_ = bf16[8,128,128]{2,1,0:T(8,128)(2,1)S(1)} collective-permute-done((bf16[8,128,128]{2,1,0:T(8,128)(2,1)S(1)}, bf16[8,128,128]{2,1,0:T(8,128)(2,1)S(1)}, u32[]{:S(2)}, u32[]{:S(2)}) %collective-permute-start.8) | collective-permute-done | bytes 262176 | tf_op jit(solution)/shard_map/ppermute | solution.py:486
  96.2 2.7 %outer.6.refs_7_ = bf16[3072,256]{1,0:T(8,128)(2,1)} custom-call(bf16[48,128,128]{2,1,0:T(8,128)(2,1)S(1)} %copy-done, s32[2,48]{1,0:T(2,128)S(1)} %bitcast.27, s32[2,8]{1,0:T(2,128)S(1)} %bitcast.32, s32[1]{0:T(128)} %get-tuple-element.28.refs_3_, f32[24,128,128]{2,1,0:T(8,128)S(1)} %inner.7.refs_4_, ...), custom_call_target="tpu_custom_call" | custom-call | flops 100663296 | bytes 4194304 | tf_op jit(solution)/shard_map/outer/pallas_call | solution.py:395
  98.9 0.0 collective-permute-done.3.refs_5_
  98.9 1.9 %collective-permute-done.4.refs_6_ = bf16[8,128,128]{2,1,0:T(8,128)(2,1)S(1)} collective-permute-done((bf16[8,128,128]{2,1,0:T(8,128)(2,1)S(1)}, bf16[8,128,128]{2,1,0:T(8,128)(2,1)S(1)}, u32[]{:S(2)}, u32[]{:S(2)}) %collective-permute-start.4) | collective-permute-done | bytes 262176 | tf_op jit(solution)/shard_map/ppermute | solution.py:486
  100.8 2.7 %outer.7 = bf16[3072,256]{1,0:T(8,128)(2,1)} custom-call(bf16[48,128,128]{2,1,0:T(8,128)(2,1)S(1)} %copy-done, s32[2,48]{1,0:T(2,128)S(1)} %bitcast.28, s32[2,8]{1,0:T(2,128)S(1)} %bitcast.33, s32[1]{0:T(128)} %get-tuple-element.28.refs_3_, f32[24,128,128]{2,1,0:T(8,128)S(1)} %inner.5.refs_4_, ...), custom_call_target="tpu_custom_call", output_to_operand_aliasing={{}: (7, {})} | custom-call | flops 100663296 | bytes 4194304 | tf_op jit(solution)/shard_map/outer/pallas_call | solution.py:395
  (6 shorter events, 0.2 us)
Async XLA Ops:
  8.1 40.6 %copy-start.3 = (s32[1024]{0:T(1024)S(1)}, s32[1024]{0:T(1024)}, u32[]{:S(2)}) copy-start(s32[1024]{0:T(1024)} %refs_2_.1) | copy-start | bytes 12292
  47.3 1.8 %collective-permute-start = (bf16[32,48,128]{2,1,0:T(8,128)(2,1)S(1)}, bf16[32,48,128]{2,1,0:T(8,128)(2,1)S(1)}, u32[]{:S(2)}, u32[]{:S(2)}) collective-permute-start(bf16[32,48,128]{2,1,0:T(8,128)(2,1)S(1)} %slice.41), channel_id=1, source_target_pairs={{0,8},{8,0},{16,24},{24,16},{1,9},{9,1},{17,25},{25,17},{2,10},{10... | collective-permute-start | bytes 1179656 | tf_op jit(solution)/shard_map/ppermute | solution.py:470
  48.8 0.7 copy-start.2
  52.0 19.0 %collective-permute-start.5 = (bf16[8,128,128]{2,1,0:T(8,128)(2,1)S(1)}, bf16[8,128,128]{2,1,0:T(8,128)(2,1)S(1)}, u32[]{:S(2)}, u32[]{:S(2)}) collective-permute-start(bf16[8,128,128]{2,1,0:T(8,128)(2,1)S(1)} %get-tuple-element.40), channel_id=1, source_target_pairs={{0,1},{1,2},{2,3},{3,4},{4,5},{5,6},{6,7},{7,0},{8,9},{9,10},{10,1... | collective-permute-start | bytes 786440 | tf_op jit(solution)/shard_map/ppermute | solution.py:486
  53.1 20.4 %collective-permute-start.6 = (bf16[8,128,128]{2,1,0:T(8,128)(2,1)S(1)}, bf16[8,128,128]{2,1,0:T(8,128)(2,1)S(1)}, u32[]{:S(2)}, u32[]{:S(2)}) collective-permute-start(bf16[8,128,128]{2,1,0:T(8,128)(2,1)S(1)} %get-tuple-element.39), channel_id=1, source_target_pairs={{1,0},{2,1},{3,2},{4,3},{5,4},{6,5},{7,6},{0,7},{9,8},{10,9},{11,1... | collective-permute-start | bytes 786440 | tf_op jit(solution)/shard_map/ppermute | solution.py:486
  56.9 23.6 %collective-permute-start.1 = (bf16[8,128,128]{2,1,0:T(8,128)(2,1)S(1)}, bf16[8,128,128]{2,1,0:T(8,128)(2,1)S(1)}, u32[]{:S(2)}, u32[]{:S(2)}) collective-permute-start(bf16[8,128,128]{2,1,0:T(8,128)(2,1)S(1)} %get-tuple-element.44), channel_id=1, source_target_pairs={{0,1},{1,2},{2,3},{3,4},{4,5},{5,6},{6,7},{7,0},{8,9},{9,10},{10,1... | collective-permute-start | bytes 786440 | tf_op jit(solution)/shard_map/ppermute | solution.py:486
  56.9 8.1 %copy-start = (bf16[48,128,128]{2,1,0:T(8,128)(2,1)S(1)}, bf16[48,128,128]{2,1,0:T(8,128)(2,1)}, u32[]{:S(2)}) copy-start(bf16[48,128,128]{2,1,0:T(8,128)(2,1)} %refs_0_.9) | copy-start | bytes 4718596
  56.9 8.1 %copy-start.1 = (s32[48,2]{0,1:T(2,128)S(1)}, s32[48,2]{0,1:T(2,128)}, u32[]{:S(2)}) copy-start(s32[48,2]{0,1:T(2,128)} %param.19) | copy-start | bytes 1156
  56.9 23.5 %collective-permute-start.2 = (bf16[8,128,128]{2,1,0:T(8,128)(2,1)S(1)}, bf16[8,128,128]{2,1,0:T(8,128)(2,1)S(1)}, u32[]{:S(2)}, u32[]{:S(2)}) collective-permute-start(bf16[8,128,128]{2,1,0:T(8,128)(2,1)S(1)} %get-tuple-element.43), channel_id=1, source_target_pairs={{1,0},{2,1},{3,2},{4,3},{5,4},{6,5},{7,6},{0,7},{9,8},{10,9},{11,1... | collective-permute-start | bytes 786440 | tf_op jit(solution)/shard_map/ppermute | solution.py:486
  75.6 18.1 %collective-permute-start.7 = (bf16[8,128,128]{2,1,0:T(8,128)(2,1)S(1)}, bf16[8,128,128]{2,1,0:T(8,128)(2,1)S(1)}, u32[]{:S(2)}, u32[]{:S(2)}) collective-permute-start(bf16[8,128,128]{2,1,0:T(8,128)(2,1)S(1)} %get-tuple-element.38), channel_id=1, source_target_pairs={{0,1},{1,2},{2,3},{3,4},{4,5},{5,6},{6,7},{7,0},{8,9},{9,10},{10,1... | collective-permute-start | bytes 786440 | tf_op jit(solution)/shard_map/ppermute | solution.py:486
  75.7 20.5 %collective-permute-start.8 = (bf16[8,128,128]{2,1,0:T(8,128)(2,1)S(1)}, bf16[8,128,128]{2,1,0:T(8,128)(2,1)S(1)}, u32[]{:S(2)}, u32[]{:S(2)}) collective-permute-start(bf16[8,128,128]{2,1,0:T(8,128)(2,1)S(1)} %get-tuple-element.37), channel_id=1, source_target_pairs={{1,0},{2,1},{3,2},{4,3},{5,4},{6,5},{7,6},{0,7},{9,8},{10,9},{11,1... | collective-permute-start | bytes 786440 | tf_op jit(solution)/shard_map/ppermute | solution.py:486
  82.5 16.4 %collective-permute-start.3 = (bf16[8,128,128]{2,1,0:T(8,128)(2,1)S(1)}, bf16[8,128,128]{2,1,0:T(8,128)(2,1)S(1)}, u32[]{:S(2)}, u32[]{:S(2)}) collective-permute-start(bf16[8,128,128]{2,1,0:T(8,128)(2,1)S(1)} %get-tuple-element.42), channel_id=1, source_target_pairs={{0,1},{1,2},{2,3},{3,4},{4,5},{5,6},{6,7},{7,0},{8,9},{9,10},{10,1... | collective-permute-start | bytes 786440 | tf_op jit(solution)/shard_map/ppermute | solution.py:486
  82.6 18.2 %collective-permute-start.4 = (bf16[8,128,128]{2,1,0:T(8,128)(2,1)S(1)}, bf16[8,128,128]{2,1,0:T(8,128)(2,1)S(1)}, u32[]{:S(2)}, u32[]{:S(2)}) collective-permute-start(bf16[8,128,128]{2,1,0:T(8,128)(2,1)S(1)} %get-tuple-element.41), channel_id=1, source_target_pairs={{1,0},{2,1},{3,2},{4,3},{5,4},{6,5},{7,6},{0,7},{9,8},{10,9},{11,1... | collective-permute-start | bytes 786440 | tf_op jit(solution)/shard_map/ppermute | solution.py:486
